TPU v7x, 32 devices: a whole 2x2x4 slice. The times are simulated.
32 devices in a mesh: gx: 4 (over z), gy: 8 (over y, x, core).
Axes of the slice: x: 2, y: 2, z: 4, core: 2. Of those that a mesh axis runs over, the one named last changes fastest.
Arguments:
- permeability: float32 [3, 128, 16384], P(None, 'gx', 'gy'), may hold values from 0.03 to 1000, as said below
Outputs:
- fine_pressure: float32 [128, 16384], P('gx', 'gy')
- twin_pressure: float32 [64, 4096], P('gx', 'gy')
Inputs may be any that keep to these rules, and one draw needn't show every extreme that they name: `permeability`: positive conductivities; entry 0, 1, 2 of the first dimension is the conductivity along the grid's first, second, third dimension.
All inputs are finite; a program needn't handle non-finite values.
Results may differ from a plain program's by a relative error of at most 0.0003.
Values sent between devices are 32-bit elements; how exact they have to be, the bound alone decides.
No kernel may reach another device: no remote copies, remote signals or barrier semaphores. Data moves between devices by JAX's collectives and lax.ppermute only.
A program may use at most 192 MiB of HBM per device.

v0:
```python
import functools
import typing

import jax
import jax.numpy as jnp
from jax import lax
from jax.experimental import pallas as pl
from jax.experimental.pallas import tpu as pltpu
from jax.sharding import PartitionSpec as P

EL = 32
ELZ = 16
MX = 4
MZ = 2
EZ = 2
LANES = 128
SUBS = 8
COLUMNS = 2
F32 = jnp.float32
BF16 = jnp.bfloat16


class Level(typing.NamedTuple):
    edge: int
    edz: int
    mx: int
    mz: int
    spacing: float
    step: int

    @property
    def width(self):
        return self.edge + 2 * self.mx

    @property
    def inner(self):
        return self.edz + 2 * self.mz - 2

    @property
    def seg(self):
        return -(-self.width // SUBS)

    @property
    def tiles(self):
        return self.seg * self.seg

    @property
    def planes(self):
        return EZ * self.edz + 2

    @property
    def blocks(self):
        return -(-3 * self.seg // 2) * 2

    def base(self, e):
        return e * self.edz + 2 - self.mz


FINE = Level(EL, ELZ, MX, MZ, 1.0, 1)
TWIN = Level(EL // 2, ELZ // 2, MX // 2, MZ // 2, 2.0, 2)
LEVELS = (FINE, TWIN)


def lane_iota(shape=(SUBS, LANES)):
    return lax.broadcasted_iota(jnp.int32, shape, len(shape) - 1)


def sub_iota(shape=(SUBS, LANES)):
    return lax.broadcasted_iota(jnp.int32, shape, len(shape) - 2)


def turn(value, shift, axis=1):
    return pltpu.roll(value, shift % value.shape[axis], axis)


def lane_parts():
    lane = lane_iota()
    return lane // 16, lane // 2 % 8, lane % 2


class Consts:
    def __init__(self, lv):
        basis, xo, _ = lane_parts()
        yo = sub_iota()
        ax, ay, az = basis // 4, basis // 2 % 2, basis % 2
        self.lv = lv
        s = lv.seg
        self.az = az
        self.fx, self.fy, self.mask = [], [], {}
        self.inx, self.iny, self.facex, self.facey = [], [], [], []
        for i in range(s):
            x = xo * s + i
            y = yo * s + i
            px = (x.astype(F32) - lv.mx + 0.5) / lv.edge
            py = (y.astype(F32) - lv.mx + 0.5) / lv.edge
            self.fx.append(jnp.where(ax == 1, px, 1.0 - px))
            self.fy.append(jnp.where(ay == 1, py, 1.0 - py))
            xs = [s * o + i for o in range(SUBS)]

            def ranged(value, low, high):
                if all(low <= v <= high for v in xs):
                    return None
                return ((value >= low) & (value <= high)).astype(F32)

            self.inx.append((ranged(x, 1, lv.width - 2), ranged(x, lv.mx, lv.mx + lv.edge - 1)))
            self.iny.append((ranged(y, 1, lv.width - 2), ranged(y, lv.mx, lv.mx + lv.edge - 1)))
            cut = (lv.mx - 1, lv.mx + lv.edge - 1)
            self.facex.append(((x != cut[0]) & (x != cut[1])).astype(F32) if any(v in cut for v in xs) else None)
            self.facey.append(((y != cut[0]) & (y != cut[1])).astype(F32) if any(v in cut for v in xs) else None)
        self.sx = jnp.where(ax == 1, -1.0 / lv.edge, 1.0 / lv.edge).astype(F32)
        self.sy = jnp.where(ay == 1, -1.0 / lv.edge, 1.0 / lv.edge).astype(F32)
        self.sz = jnp.where(az == 1, -1.0 / lv.edz, 1.0 / lv.edz).astype(F32)

    def fz(self, plane):
        place = (jnp.asarray(plane, jnp.int32).astype(F32) - self.lv.mz + 0.5) / self.lv.edz
        return jnp.where(self.az == 1, place, 1.0 - place)

    def masked(self, value, i, j, kind):
        for table, index in ((self.inx, i), (self.iny, j)):
            factor = table[index][kind]
            if factor is not None:
                value = value * factor
        return value


def tree(values):
    values = list(values)
    while len(values) > 1:
        values = [a + b for a, b in zip(values[::2], values[1::2])] + (
            [values[-1]] if len(values) % 2 else []
        )
    return values[0]


def xor_lane(value, bit):
    return jnp.where(lane_iota(value.shape) // bit % 2 == 1, turn(value, bit), turn(value, -bit))


def problem_sum(value):
    for shift in (4, 2, 1):
        value = value + turn(value, shift, 0)
    for bit in (2, 4, 8):
        value = value + xor_lane(value, bit)
    return value


def spread_weights(lv, k_ref, ws_ref, hi_ref, lo_ref, w_ref):
    s = lv.seg
    wide = (SUBS, 2 * LANES)
    pos = lane_iota(wide) % LANES
    yo = sub_iota(wide)
    first = pos < 40
    second = (pos >= 40) & (pos < 80)
    edge_x = first & (pos >= (lv.width - 1) * lv.step)

    def plane(z, _):
        cells = [k_ref[z, i] for i in range(s)]
        for i in range(s):
            k = cells[i]
            nbx = turn(k, -lv.step)
            nby = cells[i + 1] if i < s - 1 else turn(cells[0], -1, 0)
            nbz = k_ref[z + 1, i]
            nb = jnp.where(first, nbx, jnp.where(second, nby, nbz))
            w = (2.0 * lv.spacing) * k * nb / (k + nb)
            bad = edge_x | (second & (yo * s + i >= lv.width - 1))
            ws_ref[z * s + i] = jnp.where(bad, 0.0, w)
        return 0

    lax.fori_loop(0, lv.planes, plane, 0)
    rows = lv.planes * s * SUBS
    full = ws_ref[...].reshape(rows, 2 * LANES)
    high = full.astype(BF16)
    hi_ref[...] = high
    lo_ref[...] = (full - high.astype(F32)).astype(BF16)
    shape = (2 * LANES, 2 * LANES)
    row = lax.broadcasted_iota(jnp.int32, shape, 0)
    lane = lax.broadcasted_iota(jnp.int32, shape, 1)
    xo = lane // 2 % 8
    upper = lane // LANES
    source = (lane % 2) * LANES + lv.step * s * xo

    def block(n, _):
        number = 2 * n + upper
        comp = number // s
        i = number - comp * s
        hit = (row == source + comp * 40 + lv.step * i) & (xo * s + i < lv.width)
        pick = hit.astype(F32).astype(BF16)
        out = jnp.dot(hi_ref[...], pick, preferred_element_type=F32)
        out = out + jnp.dot(lo_ref[...], pick, preferred_element_type=F32)
        w_ref[2 * n] = out[:, :LANES].reshape(lv.planes * s, SUBS, LANES)
        w_ref[2 * n + 1] = out[:, LANES:].reshape(lv.planes * s, SUBS, LANES)
        return 0

    lax.fori_loop(0, lv.blocks // 2, block, 0)


def load_weights(lv, w_ref, pz):
    s = lv.seg

    def get(m, i, j, plane=None):
        return w_ref[m * s + i, (pz if plane is None else plane) * s + j]

    return get


def start_residual(lv, cs, e, w_ref, d_ref):
    s = lv.seg

    def body(z, acc):
        pz = lv.base(e) + z
        below = jnp.maximum(pz - 1, 0)
        get = load_weights(lv, w_ref, pz)
        gz = cs.fz(z + 1)
        along_x = [cs.sx * gz * cs.fy[j] for j in range(s)]
        along_y = [cs.sy * gz * cs.fx[i] for i in range(s)]
        squares = []
        flux_y = {}
        for i in range(s):
            for j in range(s):
                flux_y[i, j] = get(1, i, j) * along_y[i]
        for j in range(s):
            flux_x = [get(0, i, j) * along_x[j] for i in range(s)]
            for i in range(s):
                prev_x = flux_x[i - 1] if i else turn(flux_x[s - 1], 2)
                prev_y = flux_y[i, j - 1] if j else turn(flux_y[i, s - 1], 1, 0)
                along_z = cs.sz * cs.fx[i] * cs.fy[j]
                value = (prev_x - flux_x[i]) + (prev_y - flux_y[i, j])
                value = value + along_z * (get(2, i, j, below) - get(2, i, j))
                value = cs.masked(value, i, j, 0)
                d_ref[z, i * s + j] = value
                squares.append(value * value)
        return acc + tree(squares)

    return lax.fori_loop(0, lv.inner, body, jnp.zeros((SUBS, LANES), F32))


def apply(lv, cs, e, w_ref, d_ref, q_ref, fz_ref, fresh):
    s = lv.seg
    keep = q_ref is not None

    def plane(z):
        return [fresh(z, k) for k in range(lv.tiles)]

    first = plane(0)
    below = max(lv.base(e) - 1, 0)
    get = load_weights(lv, w_ref, below)
    acc = jnp.zeros((SUBS, LANES), F32)
    for i in range(s):
        for j in range(s):
            flux = -get(2, i, j) * first[i * s + j]
            if keep:
                fz_ref[i * s + j] = flux
            else:
                acc = acc - flux * first[i * s + j]

    def body(z, acc):
        get = load_weights(lv, w_ref, lv.base(e) + z)
        terms = []
        u = [d_ref[z, k] for k in range(lv.tiles)]
        flux_y = {}
        for i in range(s):
            for j in range(s):
                after = u[i * s + j + 1] if j < s - 1 else turn(u[i * s], -1, 0)
                jump = u[i * s + j] - after
                flux_y[i, j] = get(1, i, j) * jump
                if not keep:
                    terms.append(flux_y[i, j] * jump)
        for j in range(s):
            flux_x = []
            for i in range(s):
                after = u[(i + 1) * s + j] if i < s - 1 else turn(u[j], -2)
                jump = u[i * s + j] - after
                flux_x.append(get(0, i, j) * jump)
                if not keep:
                    terms.append(flux_x[i] * jump)
            for i in range(s):
                k = i * s + j
                jump = u[k] - fresh(z + 1, k)
                flux = get(2, i, j) * jump
                if keep:
                    prev_x = flux_x[i - 1] if i else turn(flux_x[s - 1], 2)
                    prev_y = flux_y[i, j - 1] if j else turn(flux_y[i, s - 1], 1, 0)
                    value = (flux_x[i] - prev_x) + (flux_y[i, j] - prev_y) + (flux - fz_ref[k])
                    fz_ref[k] = flux
                    value = cs.masked(value, i, j, 0)
                    q_ref[z, k] = value
                    terms.append(u[k] * value)
                else:
                    terms.append(flux * jump)
        return acc + tree(terms)

    return lax.fori_loop(0, lv.inner, body, acc)


def reduce_residual(lv, source_ref, q_ref, r_ref, alpha):
    def body(z, acc):
        squares = []
        for k in range(lv.tiles):
            value = source_ref[z, k] - alpha * q_ref[z, k]
            r_ref[z, k] = value
            squares.append(value * value)
        return acc + tree(squares)

    return lax.fori_loop(0, lv.inner, body, jnp.zeros((SUBS, LANES), F32))


def finish(lv, cs, e, w_ref, d_refs, alphas, phi_ref, fz_ref):
    s = lv.seg
    even = (cs.az == 0).astype(F32)
    zero = jnp.zeros((SUBS, LANES), F32)

    def fresh(z, i, j):
        k = i * s + j
        inner = z + lv.mz - 1
        value = cs.fx[i] * cs.fy[j] * cs.fz(z + lv.mz)
        for alpha, d_ref in zip(alphas, d_refs):
            value = value + alpha * d_ref[inner, k]
        value = cs.masked(value, i, j, 1)
        phi_ref[e * lv.edz + z, k] = value
        return value

    for i in range(s):
        for j in range(s):
            fresh(0, i, j)
            fz_ref[i * s + j] = zero

    def body(z, accs):
        get = load_weights(lv, w_ref, lv.base(e) + lv.mz - 1 + z)
        after_z = jnp.minimum(z + 1, lv.edz - 1)
        u = [phi_ref[e * lv.edz + z, k] for k in range(lv.tiles)]
        sums = [[] for _ in accs]
        flux_y = {}
        for i in range(s):
            for j in range(s):
                after = u[i * s + j + 1] if j < s - 1 else turn(u[i * s], -1, 0)
                flux = get(1, i, j) * (u[i * s + j] - after)
                flux_y[i, j] = flux if cs.facey[j] is None else flux * cs.facey[j]
        for j in range(s):
            flux_x = []
            for i in range(s):
                after = u[(i + 1) * s + j] if i < s - 1 else turn(u[j], -2)
                flux = get(0, i, j) * (u[i * s + j] - after)
                flux_x.append(flux if cs.facex[i] is None else flux * cs.facex[i])
            for i in range(s):
                k = i * s + j
                flux = get(2, i, j) * (u[k] - fresh(after_z, i, j))
                prev_x = flux_x[i - 1] if i else turn(flux_x[s - 1], 2)
                prev_y = flux_y[i, j - 1] if j else turn(flux_y[i, s - 1], 1, 0)
                value = (flux_x[i] - prev_x) + (flux_y[i, j] - prev_y) + (flux - fz_ref[k])
                fz_ref[k] = flux
                sums[0].append(value * u[k])
                sums[1].append(value * turn(u[k], -32))
                sums[2].append(value * turn(u[k], 64))
                if e == 0:
                    low = u[k] * even
                    low = low + turn(low, 32)
                    low = low + turn(low, 64)
                    sums[3].append(value * turn(low, 16))
        return tuple(acc + tree(part) for acc, part in zip(accs, sums))

    count = 4 if e == 0 else 3
    return lax.fori_loop(0, lv.edz, body, (zero,) * count)


def solve_kernel(
    center, x_low, x_high, y_low, y_high,
    phi_fine, phi_twin, message,
    flat, rows, pairs, twin_rows,
    kf, kt, wsf, wst, hif, hit, lof, lot, wf, wt,
    fine_fields, twin_fields, fzf, fzt,
):
    lanes = center.shape[2]
    rim = y_low.shape[2]
    nx = center.shape[1]
    top = MX + nx
    for m in range(3):
        off = m * (nx + 2 * MX)
        flat[off : off + top + MX, :rim] = y_low[m]
        flat[off : off + MX, rim : rim + lanes] = x_low[m]
        flat[off + MX : off + top, rim : rim + lanes] = center[m]
        flat[off + top : off + top + MX, rim : rim + lanes] = x_high[m]
        flat[off : off + top + MX, rim + lanes :] = y_high[m]
    used = 3 * (nx + 2 * MX)
    flat[used:, :] = jnp.ones((LANES - used, flat.shape[1]), F32)
    for t in range(flat.shape[1] // LANES):
        rows[t * LANES : (t + 1) * LANES, :] = flat[:, t * LANES : (t + 1) * LANES].T

    nz = EZ * ELZ
    def coarse(y, _):
        start = pl.multiple_of(y * 2 * nz, 2 * nz)
        both = rows[pl.ds(start, nz), :] + rows[pl.ds(start + nz, nz), :]
        both = both + turn(both, -1)
        pairs[...] = both
        middle = 0.125 * (pairs[pl.ds(0, nz // 2, stride=2), :] + pairs[pl.ds(1, nz // 2, stride=2), :])
        to = pl.multiple_of(y * nz, nz)
        twin_rows[pl.ds(to, 8), :] = jnp.broadcast_to(0.25 * both[0:1], (8, LANES))
        twin_rows[pl.ds(to + 8, nz // 2), :] = middle
        twin_rows[pl.ds(to + 8 + nz // 2, 8), :] = jnp.broadcast_to(0.25 * both[nz - 1 : nz], (8, LANES))
        return 0

    twin_y = rows.shape[0] // nz // 2
    lax.fori_loop(0, twin_y, coarse, 0)
    twin_rows[twin_y * nz :, :] = jnp.ones((twin_rows.shape[0] - twin_y * nz, LANES), F32)

    def gather_fine(z, _):
        cell = jnp.clip(z - 1, 0, nz - 1)
        for i in range(FINE.seg):
            for c in range(COLUMNS):
                start = (EL * c + i) * nz + cell
                kf[z, i, :, c * LANES : (c + 1) * LANES] = rows[pl.ds(start, SUBS, stride=FINE.seg * nz), :]
        return 0

    lax.fori_loop(0, FINE.planes + 1, gather_fine, 0)

    def gather_twin(z, _):
        cell = jnp.minimum(z, TWIN.planes - 1) + 7
        for i in range(TWIN.seg):
            for c in range(COLUMNS):
                start = (TWIN.edge * c + i) * nz + cell
                kt[z, i, :, c * LANES : (c + 1) * LANES] = twin_rows[pl.ds(start, SUBS, stride=TWIN.seg * nz), :]
        return 0

    lax.fori_loop(0, TWIN.planes + 1, gather_twin, 0)

    spread_weights(FINE, kf, wsf, hif, lof, wf)
    spread_weights(TWIN, kt, wst, hit, lot, wt)

    consts = [Consts(lv) for lv in LEVELS]
    w_refs = (wf, wt)
    fields = (fine_fields, twin_fields)
    fz_refs = (fzf, fzt)
    phis = (phi_fine, phi_twin)
    cases = [(n, e) for n in range(2) for e in range(EZ)]

    def field(n, e, which):
        return fields[n].at[e * 5 + which]

    for n, e in cases:
        for which in range(5):
            for k in range(LEVELS[n].tiles):
                field(n, e, which)[LEVELS[n].inner, k] = jnp.zeros((SUBS, LANES), F32)

    rr = [problem_sum(v) for v in [start_residual(LEVELS[n], consts[n], e, w_refs[n], field(n, e, 0)) for n, e in cases]]
    alphas = [[] for _ in cases]
    betas = [None] * len(cases)
    for step in range(3):
        dots = []
        for p, (n, e) in enumerate(cases):
            d_ref = field(n, e, step)
            if step == 0:
                def fresh(z, k, d_ref=d_ref):
                    return d_ref[z, k]
            else:
                def fresh(z, k, d_ref=d_ref, old=field(n, e, step - 1), r=field(n, e, 4), beta=betas[p]):
                    value = r[z, k] + beta * old[z, k]
                    d_ref[z, k] = value
                    return value
            q_ref = field(n, e, 3) if step < 2 else None
            dots.append(apply(LEVELS[n], consts[n], e, w_refs[n], d_ref, q_ref, fz_refs[n], fresh))
        dots = [problem_sum(v) for v in dots]
        for p in range(len(cases)):
            alphas[p].append(rr[p] / dots[p])
        if step < 2:
            new = []
            for p, (n, e) in enumerate(cases):
                source = field(n, e, 0) if step == 0 else field(n, e, 4)
                new.append(reduce_residual(LEVELS[n], source, field(n, e, 3), field(n, e, 4), alphas[p][step]))
            new = [problem_sum(v) for v in new]
            betas = [a / b for a, b in zip(new, rr)]
            rr = new

    totals = []
    for p, (n, e) in enumerate(cases):
        d_refs = [field(n, e, which) for which in range(3)]
        totals.append(finish(LEVELS[n], consts[n], e, w_refs[n], d_refs, alphas[p], phis[n], fz_refs[n]))
    totals = [[problem_sum(v) for v in part] for part in totals]
    basis, xo, _ = lane_parts()
    packed = []
    for n in range(2):
        low, high = totals[2 * n], totals[2 * n + 1]
        parts = [turn(low[q], -16) + high[q] for q in range(3)] + [turn(low[3], -16)]
        slots = jnp.where(xo == 0, parts[0], jnp.where(xo == 1, parts[1], jnp.where(xo == 2, parts[2], parts[3])))
        packed.append(slots)
    row = jnp.where(basis % 2 == 0, packed[0], turn(packed[1], 16))
    for r in range(0, message.shape[0], SUBS):
        message[r : r + SUBS, :] = row


def coarse_nodes(gathered, gy_count, me):
    total_rows = gathered.shape[0]
    shape = gathered.shape
    lane = lane_iota(shape)
    row = sub_iota(shape)
    corner = lane // 32
    column = lane % 2
    last = row % gy_count == gy_count - 1
    start = row % gy_count == 0
    one = gathered
    two = turn(gathered, -2)
    four = turn(gathered, -4)
    rhs = turn(gathered, -6)
    two_back = turn(two, 32)

    def next_x(u):
        return turn(u, -gy_count, 0)

    def prev_x(u):
        return turn(u, gy_count, 0)

    def next_y(u):
        ahead = jnp.where(last, turn(u, gy_count - 1, 0), turn(u, -1, 0))
        return jnp.where(column == 0, turn(u, -1), turn(ahead, 1))

    def prev_y(u):
        behind = jnp.where(start, turn(u, 1 - gy_count, 0), turn(u, 1, 0))
        return jnp.where(column == 1, turn(u, 1), turn(behind, -1))

    def by_corner(a, b, c, d):
        return jnp.where(corner == 0, a, jnp.where(corner == 1, b, jnp.where(corner == 2, c, d)))

    def corners(u):
        ux = next_x(u)
        return by_corner(u, next_y(u), ux, next_y(ux))

    def assemble(v):
        vx = prev_x(v)
        w = by_corner(v, prev_y(v), vx, prev_y(vx))
        w = w + turn(w, 64)
        return w + turn(w, 32)

    def operate(u):
        c = corners(u)
        return assemble(one * c + two * turn(c, -32) + two_back * turn(c, 32) + four * turn(c, 64))

    def total(a, b):
        v = a * b
        v = tree([v[r : r + SUBS] for r in range(0, total_rows, SUBS)])
        for shift in (4, 2, 1):
            v = v + turn(v, shift, 0)
        v = v + xor_lane(v, 1)
        return v[0:1]

    residual = -assemble(rhs)
    direction = residual
    update = jnp.zeros_like(residual)
    now = total(residual, residual)
    for step in range(2):
        image = operate(direction)
        alpha = now / total(direction, image)
        update = update + alpha * direction
        if step == 0:
            residual = residual - alpha * image
            new = total(residual, residual)
            direction = residual + new / now * direction
            now = new
    mine = jnp.where(row == me, corners(update), 0.0)
    mine = jnp.sum(mine, axis=0, keepdims=True)
    mine = jnp.broadcast_to(mine, (SUBS, LANES))
    mine = jnp.where(lane_iota() // 2 % 8 == 0, mine, 0.0)
    for shift in (2, 4, 8):
        mine = mine + turn(mine, shift)
    return mine


def pressure(lv, phi_ref, scales, o_ref, t_ref, out_ref):
    s = lv.seg
    basis, _, _ = lane_parts()
    low4 = basis < 4
    low2 = basis // 2 % 2 == 0
    low1 = basis % 2 == 0
    nz = EZ * lv.edz

    def pair4(a, b):
        if b is None:
            return a + turn(a, 64)
        return jnp.where(low4, a, b) + turn(jnp.where(low4, b, a), 64)

    def fold(value, low, bit):
        return jnp.where(low, turn(value, -bit), turn(value, bit))

    def pair(a, b, low, bit):
        if b is None:
            return a + fold(a, low, bit)
        return jnp.where(low, a, b) + fold(jnp.where(low, b, a), low, bit)

    for e in range(EZ):
        def body(z, _, e=e):
            plane = e * lv.edz + z
            for j in range(s):
                v = [phi_ref[plane, i * s + j] * scales[e] for i in range(s)]
                v = v + [None] * (6 - s)
                t = [pair4(v[0], v[1]), pair4(v[2], v[3]), None if v[4] is None else pair4(v[4], v[5])]
                q = pair(t[0], t[1], low2, 32)
                q4 = None if t[2] is None else pair(t[2], None, low2, 32)
                o_ref[pl.ds(pl.multiple_of((plane * s + j) * SUBS, SUBS), SUBS), :] = pair(q, q4, low1, 16)
            return 0

        lax.fori_loop(0, lv.edz, body, 0)
    slots = (0, 4, 2, 6, 1)
    per = LANES // nz
    tiles = lv.edge // per
    for t in range(tiles):
        parts = []
        for n in range(per):
            y = lv.mx + t * per + n
            parts.append(o_ref[pl.ds(y % s * SUBS + y // s, nz, stride=s * SUBS), :])
        t_ref[t] = jnp.concatenate(parts, axis=0).T
        for c in range(COLUMNS):
            at = (c * tiles + t) * LANES
            for x in range(lv.edge):
                xo, i = divmod(x + lv.mx, s)
                out_ref[x : x + 1, at : at + LANES] = t_ref[t, pl.ds(slots[i] * 16 + xo * 2 + c, 1), :]


def pressure_kernel(gy_count, me_ref, gathered, phi_fine, phi_twin, fine_out, twin_out, of, ot, tf, tt):
    mine = coarse_nodes(gathered[...], gy_count, me_ref[0])
    even = lane_iota() // 16 % 2 == 0
    up = turn(mine, 16)
    down = turn(mine, -16)
    fine_scales = [jnp.where(even, 1.0, up), jnp.where(even, mine, 0.0)]
    twin_scales = [jnp.where(even, 1.0, mine), jnp.where(even, down, 0.0)]
    pressure(FINE, phi_fine, fine_scales, of, tf, fine_out)
    pressure(TWIN, phi_twin, twin_scales, ot, tt, twin_out)


def vmem(shape, dtype=F32):
    return pltpu.VMEM(shape, dtype)


def shards(permeability):
    nz = EZ * ELZ
    rows = permeability.shape[1]
    lanes = permeability.shape[2]
    assert rows == EL and lanes == COLUMNS * EL * nz
    rim = MX * nz
    gx, gy = lax.axis_size("gx"), lax.axis_size("gy")

    def sent(value, axis, shift):
        count = lax.axis_size(axis)
        return lax.ppermute(value, axis, [(i, (i + shift) % count) for i in range(count)])

    x_low = sent(permeability[:, rows - MX :], "gx", 1)
    x_high = sent(permeability[:, :MX], "gx", -1)

    def strip(part):
        return jnp.concatenate([x_low[:, :, part], permeability[:, :, part], x_high[:, :, part]], axis=1)

    y_low = sent(strip(slice(lanes - rim, lanes)), "gy", 1)
    y_high = sent(strip(slice(0, rim)), "gy", -1)
    halos = [x_low, x_high, y_low, y_high]
    flat_lanes = lanes + 2 * rim
    scratch = [
        vmem((LANES, flat_lanes)),
        vmem((flat_lanes, LANES)),
        vmem((nz, LANES)),
        vmem((SUBS * (TWIN.seg + 2) * nz, LANES)),
    ]
    for make in (
        lambda lv: vmem((lv.planes + 1, lv.seg, SUBS, 2 * LANES)),
        lambda lv: vmem((lv.planes * lv.seg, SUBS, 2 * LANES)),
        lambda lv: vmem((lv.planes * lv.seg * SUBS, 2 * LANES), BF16),
        lambda lv: vmem((lv.planes * lv.seg * SUBS, 2 * LANES), BF16),
        lambda lv: vmem((lv.blocks, lv.planes * lv.seg, SUBS, LANES)),
        lambda lv: vmem((EZ * 5, lv.inner + 1, lv.tiles, SUBS, LANES)),
        lambda lv: vmem((lv.tiles, SUBS, LANES)),
    ):
        scratch += [make(FINE), make(TWIN)]
    full = pl.BlockSpec(memory_space=pltpu.VMEM)
    phi_shapes = [
        jax.ShapeDtypeStruct((EZ * lv.edz, lv.tiles, SUBS, LANES), F32) for lv in LEVELS
    ]
    phi_fine, phi_twin, message = pl.pallas_call(
        solve_kernel,
        out_shape=phi_shapes + [jax.ShapeDtypeStruct((gx * gy, LANES), F32)],
        in_specs=[full] * 5,
        out_specs=[full] * 3,
        scratch_shapes=scratch,
        compiler_params=pltpu.CompilerParams(vmem_limit_bytes=56 * 1024 * 1024),
        name="solve",
    )(permeability, *halos)
    gathered = lax.all_to_all(message, ("gx", "gy"), 0, 0, tiled=True)
    me = (lax.axis_index("gx") * gy + lax.axis_index("gy")).astype(jnp.int32).reshape(1)
    outs = [
        jax.ShapeDtypeStruct((lv.edge, COLUMNS * lv.edge * EZ * lv.edz), F32) for lv in LEVELS
    ]
    scratch = [vmem((EZ * lv.edz * lv.seg * SUBS, LANES)) for lv in LEVELS]
    scratch += [vmem((lv.edge * EZ * lv.edz // LANES, LANES, LANES)) for lv in LEVELS]
    return tuple(
        pl.pallas_call(
            functools.partial(pressure_kernel, gy),
            out_shape=outs,
            in_specs=[pl.BlockSpec(memory_space=pltpu.SMEM)] + [full] * 3,
            out_specs=[full] * 2,
            scratch_shapes=scratch,
            compiler_params=pltpu.CompilerParams(vmem_limit_bytes=40 * 1024 * 1024),
            name="pressure",
        )(me, gathered, phi_fine, phi_twin)
    )


def solution(mesh):
    return jax.shard_map(
        shards,
        mesh=mesh,
        in_specs=(P(None, "gx", "gy"),),
        out_specs=(P("gx", "gy"), P("gx", "gy")),
        check_vma=False,
    )
```

profile of v0, /device:TPU:0, one launch (start us, length us, event | category | flops | bytes accessed | tf_op | source)
XLA Modules:
  0.0 103.1 jit_solution(9323462443489427784)
XLA Ops:
  0.6 1.1 %fusion.1 = (f32[3,4,2048]{2,1,0:T(4,128)S(1)}, f32[3,4,2048]{2,1,0:T(4,128)S(1)}) fusion(f32[3,32,2048]{2,1,0:T(8,128)} %center.1), kind=kLoop, calls=%fused_computation.3 | loop fusion | bytes 393216 | tf_op jit(solution)/shard_map/slice | solution.py:643
  1.7 3.1 %collective-permute-start = (f32[3,4,2048]{2,1,0:T(4,128)S(1)}, f32[3,4,2048]{2,1,0:T(4,128)S(1)}, u32[]{:S(2)}, u32[]{:S(2)}) collective-permute-start(f32[3,4,2048]{2,1,0:T(4,128)S(1)} %get-tuple-element.11), channel_id=1, source_target_pairs={{0,8},{8,16},{16,24},{24,0},{1,9},{9,17},{17,25},{25,1},{2,10},{10... | collective-permute-start | bytes 294920 | tf_op jit(solution)/shard_map/ppermute | solution.py:640
  4.8 2.1 %collective-permute-start.1 = (f32[3,4,2048]{2,1,0:T(4,128)S(1)}, f32[3,4,2048]{2,1,0:T(4,128)S(1)}, u32[]{:S(2)}, u32[]{:S(2)}) collective-permute-start(f32[3,4,2048]{2,1,0:T(4,128)S(1)} %get-tuple-element.10), channel_id=1, source_target_pairs={{0,24},{8,0},{16,8},{24,16},{1,25},{9,1},{17,9},{25,17},{2,26},{10... | collective-permute-start | bytes 294920 | tf_op jit(solution)/shard_map/ppermute | solution.py:640
  6.9 0.8 fusion
  7.7 2.6 %collective-permute-done.x_low = f32[3,4,2048]{2,1,0:T(4,128)S(1)} collective-permute-done((f32[3,4,2048]{2,1,0:T(4,128)S(1)}, f32[3,4,2048]{2,1,0:T(4,128)S(1)}, u32[]{:S(2)}, u32[]{:S(2)}) %collective-permute-start) | collective-permute-done | bytes 98336 | tf_op jit(solution)/shard_map/ppermute | solution.py:640
  10.3 0.0 copy-start.2
  10.3 0.8 collective-permute-done.1.x_high
  11.1 0.0 copy-start.3
  11.2 1.5 %collective-permute-start.3 = (f32[3,40,128]{2,1,0:T(8,128)S(1)}, f32[3,40,128]{2,1,0:T(8,128)S(1)}, u32[]{:S(2)}, u32[]{:S(2)}) collective-permute-start(f32[3,40,128]{2,1,0:T(8,128)S(1)} %pad_maximum_fusion.1), channel_id=1, source_target_pairs={{0,7},{1,0},{2,1},{3,2},{4,3},{5,4},{6,5},{7,6},{8,15},{9,8},{10,9... | collective-permute-start | bytes 184328 | tf_op jit(solution)/shard_map/ppermute | solution.py:640
  12.7 0.1 collective-permute-start.2
  12.7 1.9 %collective-permute-done.3.y_high = f32[3,40,128]{2,1,0:T(8,128)S(1)} collective-permute-done((f32[3,40,128]{2,1,0:T(8,128)S(1)}, f32[3,40,128]{2,1,0:T(8,128)S(1)}, u32[]{:S(2)}, u32[]{:S(2)}) %collective-permute-start.3) | collective-permute-done | bytes 61472 | tf_op jit(solution)/shard_map/ppermute | solution.py:640
  14.6 0.0 copy-start.4
  14.6 2.7 %collective-permute-done.2.y_low = f32[3,40,128]{2,1,0:T(8,128)S(1)} collective-permute-done((f32[3,40,128]{2,1,0:T(8,128)S(1)}, f32[3,40,128]{2,1,0:T(8,128)S(1)}, u32[]{:S(2)}, u32[]{:S(2)}) %collective-permute-start.2) | collective-permute-done | bytes 61472 | tf_op jit(solution)/shard_map/ppermute | solution.py:640
  17.3 0.0 copy-done.2
  17.3 0.0 copy-done.3
  17.3 0.0 copy-done.4
  17.3 0.0 copy-start.5
  17.3 0.6 copy-done.5
  17.9 58.8 %solve.1 = (f32[32,25,8,128]{3,2,1,0:T(8,128)}, f32[16,9,8,128]{3,2,1,0:T(8,128)}, f32[32,128]{1,0:T(8,128)}) custom-call(f32[3,32,2048]{2,1,0:T(8,128)} %center.1, f32[3,4,2048]{2,1,0:T(4,128)} %copy-done.2, f32[3,4,2048]{2,1,0:T(4,128)} %copy-done.3, f32[3,40,128]{2,1,0:T(8,128)} %copy-done.5, f32[3,40,128]{2,1,0:T(8,128)} %copy-done.4), custom_call_target="tpu_custom_call" | custom-call | tf_op jit(solution)/shard_map/solve/pallas_call | solution.py:672
  76.7 2.5 %all-to-all-start = ((f32[32,1,128]{2,1,0:T(1,128)}), f32[32,1,128]{2,1,0:T(1,128)S(1)}, u32[]{:S(2)}, u32[]{:S(2)}) async-start(f32[32,1,128]{2,1,0:T(1,128)} %bitcast.6), calls=%async_computation | async-start | bytes 32768 | tf_op jit(solution)/shard_map/all_to_all | solution.py:681
  79.2 7.1 %all-to-all-done = f32[32,1,128]{2,1,0:T(1,128)S(1)} async-done(((f32[32,1,128]{2,1,0:T(1,128)}), f32[32,1,128]{2,1,0:T(1,128)S(1)}, u32[]{:S(2)}, u32[]{:S(2)}) %all-to-all-start) | async-done | bytes 16416 | tf_op jit(solution)/shard_map/all_to_all | solution.py:681
  86.3 0.0 copy-start
  86.3 1.9 %copy-done = f32[32,25,8,128]{3,2,1,0:T(8,128)S(1)} copy-done((f32[32,25,8,128]{3,2,1,0:T(8,128)S(1)}, f32[32,25,8,128]{3,2,1,0:T(8,128)}, u32[]{:S(2)}) %copy-start) | copy-done | bytes 3276824
  88.2 0.0 copy-start.1
  88.2 1.1 %copy-done.1 = f32[16,9,8,128]{3,2,1,0:T(8,128)S(1)} copy-done((f32[16,9,8,128]{3,2,1,0:T(8,128)S(1)}, f32[16,9,8,128]{3,2,1,0:T(8,128)}, u32[]{:S(2)}) %copy-start.1) | copy-done | bytes 589848
  89.3 13.8 %pressure.1 = (f32[32,2048]{1,0:T(8,128)}, f32[16,512]{1,0:T(8,128)}) custom-call(s32[1]{0:T(128)} %bitcast.me_ref, f32[32,128]{1,0:T(8,128)S(1)} %bitcast.5, f32[32,25,8,128]{3,2,1,0:T(8,128)S(1)} %copy-done, f32[16,9,8,128]{3,2,1,0:T(8,128)S(1)} %copy-done.1), custom_call_target="tpu_custom_call" | custom-call | tf_op jit(solution)/shard_map/pressure/pallas_call | solution.py:689
  (4 shorter events, 0.0 us)
Async XLA Ops:
  1.7 8.6 %collective-permute-start = (f32[3,4,2048]{2,1,0:T(4,128)S(1)}, f32[3,4,2048]{2,1,0:T(4,128)S(1)}, u32[]{:S(2)}, u32[]{:S(2)}) collective-permute-start(f32[3,4,2048]{2,1,0:T(4,128)S(1)} %get-tuple-element.11), channel_id=1, source_target_pairs={{0,8},{8,16},{16,24},{24,0},{1,9},{9,17},{17,25},{25,1},{2,10},{10... | collective-permute-start | bytes 294920 | tf_op jit(solution)/shard_map/ppermute | solution.py:640
  4.8 6.4 %collective-permute-start.1 = (f32[3,4,2048]{2,1,0:T(4,128)S(1)}, f32[3,4,2048]{2,1,0:T(4,128)S(1)}, u32[]{:S(2)}, u32[]{:S(2)}) collective-permute-start(f32[3,4,2048]{2,1,0:T(4,128)S(1)} %get-tuple-element.10), channel_id=1, source_target_pairs={{0,24},{8,0},{16,8},{24,16},{1,25},{9,1},{17,9},{25,17},{2,26},{10... | collective-permute-start | bytes 294920 | tf_op jit(solution)/shard_map/ppermute | solution.py:640
  10.3 7.0 %copy-start.2 = (f32[3,4,2048]{2,1,0:T(4,128)}, f32[3,4,2048]{2,1,0:T(4,128)S(1)}, u32[]{:S(2)}) copy-start(f32[3,4,2048]{2,1,0:T(4,128)S(1)} %collective-permute-done.x_low) | copy-start | bytes 294916
  11.1 6.1 %copy-start.3 = (f32[3,4,2048]{2,1,0:T(4,128)}, f32[3,4,2048]{2,1,0:T(4,128)S(1)}, u32[]{:S(2)}) copy-start(f32[3,4,2048]{2,1,0:T(4,128)S(1)} %collective-permute-done.1.x_high) | copy-start | bytes 294916
  11.2 3.5 %collective-permute-start.3 = (f32[3,40,128]{2,1,0:T(8,128)S(1)}, f32[3,40,128]{2,1,0:T(8,128)S(1)}, u32[]{:S(2)}, u32[]{:S(2)}) collective-permute-start(f32[3,40,128]{2,1,0:T(8,128)S(1)} %pad_maximum_fusion.1), channel_id=1, source_target_pairs={{0,7},{1,0},{2,1},{3,2},{4,3},{5,4},{6,5},{7,6},{8,15},{9,8},{10,9... | collective-permute-start | bytes 184328 | tf_op jit(solution)/shard_map/ppermute | solution.py:640
  12.7 4.6 %collective-permute-start.2 = (f32[3,40,128]{2,1,0:T(8,128)S(1)}, f32[3,40,128]{2,1,0:T(8,128)S(1)}, u32[]{:S(2)}, u32[]{:S(2)}) collective-permute-start(f32[3,40,128]{2,1,0:T(8,128)S(1)} %pad_maximum_fusion), channel_id=1, source_target_pairs={{0,1},{1,2},{2,3},{3,4},{4,5},{5,6},{6,7},{7,0},{8,9},{9,10},{10,1... | collective-permute-start | bytes 184328 | tf_op jit(solution)/shard_map/ppermute | solution.py:640
  14.6 2.7 %copy-start.4 = (f32[3,40,128]{2,1,0:T(8,128)}, f32[3,40,128]{2,1,0:T(8,128)S(1)}, u32[]{:S(2)}) copy-start(f32[3,40,128]{2,1,0:T(8,128)S(1)} %collective-permute-done.3.y_high) | copy-start | bytes 184324
  17.3 0.6 copy-start.5
  76.7 9.6 %all-to-all-start = ((f32[32,1,128]{2,1,0:T(1,128)}), f32[32,1,128]{2,1,0:T(1,128)S(1)}, u32[]{:S(2)}, u32[]{:S(2)}) async-start(f32[32,1,128]{2,1,0:T(1,128)} %bitcast.6), calls=%async_computation | async-start | bytes 32768 | tf_op jit(solution)/shard_map/all_to_all | solution.py:681
  86.3 1.9 %copy-start = (f32[32,25,8,128]{3,2,1,0:T(8,128)S(1)}, f32[32,25,8,128]{3,2,1,0:T(8,128)}, u32[]{:S(2)}) copy-start(f32[32,25,8,128]{3,2,1,0:T(8,128)} %get-tuple-element.6.phi_fine) | copy-start | bytes 9830404
  88.2 1.1 %copy-start.1 = (f32[16,9,8,128]{3,2,1,0:T(8,128)S(1)}, f32[16,9,8,128]{3,2,1,0:T(8,128)}, u32[]{:S(2)}) copy-start(f32[16,9,8,128]{3,2,1,0:T(8,128)} %get-tuple-element.7.phi_twin) | copy-start | bytes 1769476
where the time goes:
time: 103 us
  Pallas kernels  72.6 us (70%)
  waiting for transfers between devices  15 us (15%)
  starting transfers between devices  9.27 us (9%)
  local copies, waits for them, and re-layouts  5.51 us (5%)
    pallas_call x1, Pallas kernels, shards(): pl.pallas_call(solve_kernel, out_shape=phi_shapes + [jax.ShapeDtypeStruct...  58.8 us
    pallas_call x1, Pallas kernels, shards(): pl.pallas_call(functools.partial(pressure_kernel, gy), out_shape=outs, in...  13.8 us
    ppermute x4, waiting for transfers between devices, sent(): lax.ppermute(value, axis, [(i, (i + shift) % count) for i in range(count)])  7.96 us
    all_to_all x1, waiting for transfers between devices, shards(): gathered = lax.all_to_all(message, ('gx', 'gy'), 0, 0, tiled=True)  7.07 us
    ppermute x4, starting transfers between devices, sent(): lax.ppermute(value, axis, [(i, (i + shift) % count) for i in range(count)])  6.73 us
    unnamed x12, local copies, waits for them, and re-layouts  3.61 us
    all_to_all x1, starting transfers between devices, shards(): gathered = lax.all_to_all(message, ('gx', 'gy'), 0, 0, tiled=True)  2.54 us
  transfers between devices with their start and end apart: 5, of which 5 were waited for; matrix products, arithmetic and copies ran while one was open for 1% of the time, Pallas kernels for 0%

commit v1 on v0

v1 whole, which is shorter than its diff:
```python
import functools
import typing

import jax
import jax.numpy as jnp
from jax import lax
from jax.experimental import pallas as pl
from jax.experimental.pallas import tpu as pltpu
from jax.sharding import PartitionSpec as P

EL = 32
ELZ = 16
MX = 4
MZ = 2
EZ = 2
LANES = 128
SUBS = 8
COLUMNS = 2
F32 = jnp.float32
BF16 = jnp.bfloat16


class Level(typing.NamedTuple):
    edge: int
    edz: int
    mx: int
    mz: int
    spacing: float
    step: int

    @property
    def width(self):
        return self.edge + 2 * self.mx

    @property
    def inner(self):
        return self.edz + 2 * self.mz - 2

    @property
    def seg(self):
        return -(-self.width // SUBS)

    @property
    def tiles(self):
        return self.seg * self.seg

    @property
    def planes(self):
        return EZ * self.edz + 2

    @property
    def blocks(self):
        return -(-3 * self.seg // 2) * 2

    def base(self, e):
        return e * self.edz + 2 - self.mz


FINE = Level(EL, ELZ, MX, MZ, 1.0, 1)
TWIN = Level(EL // 2, ELZ // 2, MX // 2, MZ // 2, 2.0, 2)
LEVELS = (FINE, TWIN)


def lane_iota(shape=(SUBS, LANES)):
    return lax.broadcasted_iota(jnp.int32, shape, len(shape) - 1)


def sub_iota(shape=(SUBS, LANES)):
    return lax.broadcasted_iota(jnp.int32, shape, len(shape) - 2)


def turn(value, shift, axis=1):
    return pltpu.roll(value, shift % value.shape[axis], axis)


def lane_parts():
    lane = lane_iota()
    return lane // 16, lane % 8, lane // 8 % 2


class Consts:
    def __init__(self, lv):
        basis, xo, _ = lane_parts()
        yo = sub_iota()
        ax, ay, az = basis // 4, basis // 2 % 2, basis % 2
        self.lv = lv
        s = lv.seg
        self.az = az
        self.fx, self.fy, self.mask = [], [], {}
        self.inx, self.iny, self.facex, self.facey = [], [], [], []
        for i in range(s):
            x = xo * s + i
            y = yo * s + i
            px = (x.astype(F32) - lv.mx + 0.5) / lv.edge
            py = (y.astype(F32) - lv.mx + 0.5) / lv.edge
            self.fx.append(jnp.where(ax == 1, px, 1.0 - px))
            self.fy.append(jnp.where(ay == 1, py, 1.0 - py))
            xs = [s * o + i for o in range(SUBS)]

            def ranged(value, low, high):
                if all(low <= v <= high for v in xs):
                    return None
                return ((value >= low) & (value <= high)).astype(F32)

            self.inx.append((ranged(x, 1, lv.width - 2), ranged(x, lv.mx, lv.mx + lv.edge - 1)))
            self.iny.append((ranged(y, 1, lv.width - 2), ranged(y, lv.mx, lv.mx + lv.edge - 1)))
            cut = (lv.mx - 1, lv.mx + lv.edge - 1)
            self.facex.append(((x != cut[0]) & (x != cut[1])).astype(F32) if any(v in cut for v in xs) else None)
            self.facey.append(((y != cut[0]) & (y != cut[1])).astype(F32) if any(v in cut for v in xs) else None)
        self.sx = jnp.where(ax == 1, -1.0 / lv.edge, 1.0 / lv.edge).astype(F32)
        self.sy = jnp.where(ay == 1, -1.0 / lv.edge, 1.0 / lv.edge).astype(F32)
        self.sz = jnp.where(az == 1, -1.0 / lv.edz, 1.0 / lv.edz).astype(F32)

    def fz(self, plane):
        place = (jnp.asarray(plane, jnp.int32).astype(F32) - self.lv.mz + 0.5) / self.lv.edz
        return jnp.where(self.az == 1, place, 1.0 - place)

    def masked(self, value, i, j, kind):
        for table, index in ((self.inx, i), (self.iny, j)):
            factor = table[index][kind]
            if factor is not None:
                value = value * factor
        return value


def tree(values):
    values = list(values)
    while len(values) > 1:
        values = [a + b for a, b in zip(values[::2], values[1::2])] + (
            [values[-1]] if len(values) % 2 else []
        )
    return values[0]


def xor_lane(value, bit):
    return jnp.where(lane_iota(value.shape) // bit % 2 == 1, turn(value, bit), turn(value, -bit))


def problem_sum(value):
    for shift in (4, 2, 1):
        value = value + turn(value, shift, 0)
    for bit in (1, 2, 4):
        value = value + xor_lane(value, bit)
    return value


def spread_weights(lv, k_ref, lhs_refs, w_refs):
    s = lv.seg
    wide = (SUBS, LANES)
    pos = lane_iota(wide)
    yo = sub_iota(wide)
    first = pos < 40
    third = pos >= 80
    second = (pos >= 40) & (pos < 80)
    edge_x = first & (pos >= (lv.width - 1) * lv.step)

    def one(z, i, c):
        part = slice(c * LANES, (c + 1) * LANES)
        k = k_ref[z, i, :, part]
        nbx = turn(k, -lv.step)
        nby = k_ref[z, i + 1, :, part] if i < s - 1 else turn(k_ref[z, 0, :, part], -1, 0)
        nbz = k_ref[z + 1, i, :, part]
        nb = jnp.where(first, nbx, jnp.where(second, nby, nbz))
        w = (2.0 * lv.spacing) * k * nb / (k + nb)
        bad = edge_x | (second & (yo * s + i >= lv.width - 1))
        w = jnp.where(bad, 0.0, w)
        high = w.astype(BF16).astype(F32)
        low = w - high
        near, wrap = turn(low, 40), turn(low, 48)
        return (
            jnp.where(first, high, near),
            jnp.where(third, near, high),
            jnp.where(third, high, wrap),
        )

    def planes(t, _):
        units = [(2 * t + n, i) for n in range(2) for i in range(s)]
        for p in range(s):
            for c in range(COLUMNS):
                up, down = one(*units[2 * p], c), one(*units[2 * p + 1], c)
                for m in range(3):
                    both = jnp.concatenate([up[m], down[m]], axis=0).astype(BF16)
                    lhs_refs[m][t * s + p, :, c * LANES : (c + 1) * LANES] = both
        return 0

    lax.fori_loop(0, lv.planes // 2, planes, 0)
    rows = lv.planes * s * SUBS
    shape = (2 * LANES, 2 * LANES)
    row = lax.broadcasted_iota(jnp.int32, shape, 0)
    lane = lax.broadcasted_iota(jnp.int32, (1, 2 * LANES), 1)
    xo = lane % 8
    upper = lane // LANES
    for q in range(-(-s // 2)):
        x = xo * s + 2 * q + upper
        for m in range(3):
            source = lane // 8 % 2 * LANES + lv.step * x
            valid = (x < lv.width) & (2 * q + upper < s)
            high = jnp.where(valid, source + m * 40, -1)
            low = jnp.where(valid, source + (m + 1) % 3 * 40, -1)
            pick = ((row == high) | (row == low)).astype(F32).astype(BF16)
            lhs = lhs_refs[m][...].reshape(rows, 2 * LANES)
            out = jnp.dot(lhs, pick, preferred_element_type=F32)
            for half in range(min(2, s - 2 * q)):
                part = out[:, half * LANES : (half + 1) * LANES]
                w_refs[m][2 * q + half] = part.reshape(lv.planes * s, SUBS, LANES)


class Case:
    def __init__(self, lv, cs, e, w_refs, fields, fz_ref):
        self.lv, self.cs, self.e, self.w_refs = lv, cs, e, w_refs
        self.d, self.q, self.r, self.fz = fields[:3], fields[3], fields[4], fz_ref

    def weights(self, plane):
        s = self.lv.seg
        return lambda m, i, j: self.w_refs[m][i, plane * s + j]


def looped(cases, count, group, begin, step):
    zero = jnp.zeros((SUBS, LANES), F32)
    counts = [begin(case) for case in cases]
    start = tuple(zero for n in counts for _ in range(n))

    def body(t, sums):
        sums = list(sums)
        at = 0
        for case, n in zip(cases, counts):
            got = step(case, t * group)
            for k in range(n):
                sums[at + k] = sums[at + k] + got[k]
            at += n
        return tuple(sums)

    if count == group:
        sums = body(0, start)
    else:
        sums = lax.fori_loop(0, count // group, body, start)
    out, at = [], 0
    for n in counts:
        out.append(sums[at : at + n])
        at += n
    return out


def start_residual(cases, group):
    lv, cs, s = cases[0].lv, cases[0].cs, cases[0].lv.seg

    def step(case, z0):
        total = []
        for z in [z0 + n for n in range(group)]:
            pz = lv.base(case.e) + z
            get = case.weights(pz)
            below = case.weights(jnp.maximum(pz - 1, 0))
            gz = cs.fz(z + 1)
            along_x = [cs.sx * gz * cs.fy[j] for j in range(s)]
            along_y = [cs.sy * gz * cs.fx[i] for i in range(s)]
            last = [get(1, i, s - 1) * along_y[i] for i in range(s)]
            before = [turn(v, 1, 0) for v in last]
            for j in range(s):
                flux_y = last if j == s - 1 else [get(1, i, j) * along_y[i] for i in range(s)]
                flux_x = [get(0, i, j) * along_x[j] for i in range(s)]
                squares = []
                for i in range(s):
                    prev_x = flux_x[i - 1] if i else turn(flux_x[s - 1], 1)
                    along_z = cs.sz * cs.fx[i] * cs.fy[j]
                    value = (prev_x - flux_x[i]) + (before[i] - flux_y[i])
                    value = value + along_z * (below(2, i, j) - get(2, i, j))
                    value = cs.masked(value, i, j, 0)
                    case.d[0][z, i * s + j] = value
                    squares.append(value * value)
                total.append(tree(squares))
                before = flux_y
        return [tree(total)]

    return [part[0] for part in looped(cases, lv.inner, group, lambda case: 1, step)]


def fluxes(case, get, u, j, last):
    s = case.lv.seg
    jump_y = []
    for i in range(s):
        after = u[i * s + j + 1] if j < s - 1 else turn(u[i * s], -1, 0)
        jump_y.append(u[i * s + j] - after)
    flux_y = last if last is not None else [get(1, i, j) * jump_y[i] for i in range(s)]
    jump_x = []
    for i in range(s):
        after = u[(i + 1) * s + j] if i < s - 1 else turn(u[j], -1)
        jump_x.append(u[i * s + j] - after)
    flux_x = [get(0, i, j) * jump_x[i] for i in range(s)]
    return flux_x, flux_y, jump_x, jump_y


def last_row(case, get, u):
    s = case.lv.seg
    return [get(1, i, s - 1) * (u[i * s + s - 1] - turn(u[i * s], -1, 0)) for i in range(s)]


def apply(cases, group, number, betas):
    lv, cs, s = cases[0].lv, cases[0].cs, cases[0].lv.seg
    keep = number < 2

    def fresh(case, z, k):
        if number == 0:
            return case.d[0][z, k]
        value = case.r[z, k] + betas[case.e] * case.d[number - 1][z, k]
        case.d[number][z, k] = value
        return value

    firsts = []
    for case in cases:
        get = case.weights(max(lv.base(case.e) - 1, 0))
        terms = []
        for k in range(lv.tiles):
            value = fresh(case, 0, k)
            flux = -get(2, k // s, k % s) * value
            if keep:
                case.fz[k] = flux
            else:
                terms.append(-flux * value)
        firsts.append(tree(terms) if terms else 0.0)

    def step(case, z0):
        total = []
        u = [case.d[number][z0, k] for k in range(lv.tiles)]
        flux_z = [case.fz[k] for k in range(lv.tiles)] if keep else None
        for z in [z0 + n for n in range(group)]:
            get = case.weights(lv.base(case.e) + z)
            after = [None] * lv.tiles
            if keep:
                last = last_row(case, get, u)
                before = [turn(v, 1, 0) for v in last]
            for j in range(s):
                flux_x, flux_y, jump_x, jump_y = fluxes(case, get, u, j, last if keep and j == s - 1 else None)
                terms = []
                for i in range(s):
                    k = i * s + j
                    after[k] = fresh(case, z + 1, k)
                    jump = u[k] - after[k]
                    flux = get(2, i, j) * jump
                    if keep:
                        prev_x = flux_x[i - 1] if i else turn(flux_x[s - 1], 1)
                        value = (flux_x[i] - prev_x) + (flux_y[i] - before[i]) + (flux - flux_z[k])
                        flux_z[k] = flux
                        value = cs.masked(value, i, j, 0)
                        case.q[z, k] = value
                        terms.append(u[k] * value)
                    else:
                        terms.append((flux * jump + flux_x[i] * jump_x[i]) + flux_y[i] * jump_y[i])
                before = flux_y
                total.append(tree(terms))
            u = after
        if keep:
            for k in range(lv.tiles):
                case.fz[k] = flux_z[k]
        return [tree(total)]

    sums = looped(cases, lv.inner, group, lambda case: 1, step)
    return [part[0] + first for part, first in zip(sums, firsts)]


def reduce_residual(cases, group, number, alphas):
    lv = cases[0].lv

    def step(case, z0):
        total = []
        source = case.d[0] if number == 0 else case.r
        for z in [z0 + n for n in range(group)]:
            squares = []
            for k in range(lv.tiles):
                value = source[z, k] - alphas[case.e] * case.q[z, k]
                case.r[z, k] = value
                squares.append(value * value)
            total.append(tree(squares))
        return [tree(total)]

    return [part[0] for part in looped(cases, lv.inner, group, lambda case: 1, step)]


def finish(cases, group, alphas, phi_ref):
    lv, cs, s = cases[0].lv, cases[0].cs, cases[0].lv.seg
    even = (cs.az == 0).astype(F32)
    zero = jnp.zeros((SUBS, LANES), F32)

    def place(case, z, k):
        return pl.ds(pl.multiple_of(((case.e * lv.edz + z) * lv.tiles + k) * SUBS, SUBS), SUBS)

    def fresh(case, z, i, j, gz):
        k = i * s + j
        inner = z + lv.mz - 1
        value = cs.fx[i] * cs.fy[j] * gz
        for alpha, d_ref in zip(alphas[case.e], case.d):
            value = value + alpha * d_ref[inner, k]
        value = cs.masked(value, i, j, 1)
        phi_ref[place(case, z, k), :] = value
        return value

    for case in cases:
        gz = cs.fz(lv.mz)
        for i in range(s):
            for j in range(s):
                fresh(case, 0, i, j, gz)
                case.fz[i * s + j] = zero

    def step(case, z0):
        sums = [[] for _ in range(4 if case.e == 0 else 3)]
        u = [phi_ref[place(case, z0, k), :] for k in range(lv.tiles)]
        flux_z = [case.fz[k] for k in range(lv.tiles)]
        for z in [z0 + n for n in range(group)]:
            get = case.weights(lv.base(case.e) + lv.mz - 1 + z)
            up = jnp.minimum(z + 1, lv.edz - 1)
            gz = cs.fz(up + lv.mz)
            after = [None] * lv.tiles

            def cut(values, table):
                return [v if f is None else v * f for v, f in zip(values, table)]

            last = cut(last_row(case, get, u), [cs.facey[s - 1]] * s)
            before = [turn(v, 1, 0) for v in last]
            for j in range(s):
                flux_x, flux_y, _, _ = fluxes(case, get, u, j, last if j == s - 1 else None)
                flux_x = cut(flux_x, cs.facex)
                if j < s - 1:
                    flux_y = cut(flux_y, [cs.facey[j]] * s)
                parts = [[] for _ in sums]
                for i in range(s):
                    k = i * s + j
                    after[k] = fresh(case, up, i, j, gz)
                    flux = get(2, i, j) * (u[k] - after[k])
                    prev_x = flux_x[i - 1] if i else turn(flux_x[s - 1], 1)
                    value = (flux_x[i] - prev_x) + (flux_y[i] - before[i]) + (flux - flux_z[k])
                    flux_z[k] = flux
                    parts[0].append(value * u[k])
                    parts[1].append(value * turn(u[k], -32))
                    parts[2].append(value * turn(u[k], 64))
                    if case.e == 0:
                        low = u[k] * even
                        low = low + turn(low, 32)
                        low = low + turn(low, 64)
                        parts[3].append(value * turn(low, 16))
                for total, part in zip(sums, parts):
                    total.append(tree(part))
                before = flux_y
            u = after
        for k in range(lv.tiles):
            case.fz[k] = flux_z[k]
        return [tree(total) for total in sums]

    return looped(cases, lv.edz, group, lambda case: 4 if case.e == 0 else 3, step)


GROUPS = {FINE: 2, TWIN: 8}


def solve_kernel(
    center, x_low, x_high, y_low, y_high,
    phi_fine, phi_twin, message,
    flat, rows, pairs, twin_rows, *refs,
):
    lanes = center.shape[2]
    rim = (flat.shape[1] - lanes) // 2
    nx = center.shape[1]
    top = MX + nx
    for m in range(3):
        off = m * (nx + 2 * MX)
        flat[off : off + top + MX, :rim] = y_low[m]
        flat[off : off + MX, rim : rim + lanes] = x_low[m]
        flat[off + MX : off + top, rim : rim + lanes] = center[m]
        flat[off + top : off + top + MX, rim : rim + lanes] = x_high[m]
        flat[off : off + top + MX, rim + lanes :] = y_high[m]
    used = 3 * (nx + 2 * MX)
    flat[used:, :] = jnp.ones((LANES - used, flat.shape[1]), F32)
    for t in range(flat.shape[1] // LANES):
        rows[t * LANES : (t + 1) * LANES, :] = flat[:, t * LANES : (t + 1) * LANES].T

    nz = EZ * ELZ
    twin_y = rows.shape[0] // nz // 2
    for y in range(twin_y):
        both = rows[2 * y * nz : (2 * y + 1) * nz, :] + rows[(2 * y + 1) * nz : (2 * y + 2) * nz, :]
        both = both + turn(both, -1)
        at = y * nz
        pairs[at : at + nz, :] = both
        twin_rows[at : at + 8, :] = jnp.broadcast_to(0.25 * both[0:1], (8, LANES))
        twin_rows[at + 8 + nz // 2 : at + nz, :] = jnp.broadcast_to(0.25 * both[nz - 1 : nz], (8, LANES))
    for y in range(twin_y):
        at = y * nz
        middle = pairs[pl.ds(at, nz // 2, stride=2), :] + pairs[pl.ds(at + 1, nz // 2, stride=2), :]
        twin_rows[at + 8 : at + 8 + nz // 2, :] = 0.125 * middle
    twin_rows[twin_y * nz :, :] = jnp.ones((twin_rows.shape[0] - twin_y * nz, LANES), F32)

    refs = list(refs)

    def take(count):
        got = refs[:count]
        del refs[:count]
        return got

    groups = []
    for lv, source in zip(LEVELS, (rows, twin_rows)):
        (k_ref,) = take(1)
        lhs_refs, w_refs = take(3), take(3)
        for z in range(lv.planes + 1):
            cell = min(max(z - 1, 0), nz - 1) if lv is FINE else min(z, lv.planes - 1) + 7
            for i in range(lv.seg):
                for c in range(COLUMNS):
                    start = (lv.edge * c + i) * nz + cell
                    k_ref[z, i, :, c * LANES : (c + 1) * LANES] = source[pl.ds(start, SUBS, stride=lv.seg * nz), :]
        spread_weights(lv, k_ref, lhs_refs, w_refs)
        cs = Consts(lv)
        cases = []
        for e in range(EZ):
            fields = take(5)
            (fz_ref,) = take(1)
            case = Case(lv, cs, e, w_refs, fields, fz_ref)
            for k in range(lv.tiles):
                case.d[0][lv.inner, k] = jnp.zeros((SUBS, LANES), F32)
                case.r[lv.inner, k] = jnp.zeros((SUBS, LANES), F32)
            cases.append(case)
        groups.append(cases)

    def both_levels(work):
        sums = [work(n, cases, GROUPS[cases[0].lv]) for n, cases in enumerate(groups)]
        return [[problem_sum(v) for v in part] for part in sums]

    rr = both_levels(lambda n, cases, group: start_residual(cases, group))
    alphas = [[[] for _ in range(EZ)] for _ in LEVELS]
    betas = [None] * len(LEVELS)
    for step in range(3):
        dots = both_levels(lambda n, cases, group: apply(cases, group, step, betas[n]))
        now = [[a / b for a, b in zip(rr[n], dots[n])] for n in range(len(LEVELS))]
        for n in range(len(LEVELS)):
            for e in range(EZ):
                alphas[n][e].append(now[n][e])
        if step < 2:
            new = both_levels(lambda n, cases, group: reduce_residual(cases, group, step, now[n]))
            betas = [[a / b for a, b in zip(new[n], rr[n])] for n in range(len(LEVELS))]
            rr = new

    phis = (phi_fine, phi_twin)
    totals = [finish(cases, GROUPS[cases[0].lv], alphas[n], phis[n]) for n, cases in enumerate(groups)]
    totals = [[[problem_sum(v) for v in part] for part in level] for level in totals]
    basis, xo, _ = lane_parts()
    packed = []
    for low, high in totals:
        parts = [turn(low[q], -16) + high[q] for q in range(3)] + [turn(low[3], -16)]
        packed.append(
            jnp.where(xo == 0, parts[0], jnp.where(xo == 1, parts[1], jnp.where(xo == 2, parts[2], parts[3])))
        )
    row = jnp.where(basis % 2 == 0, packed[0], turn(packed[1], 16))
    for r in range(0, message.shape[0], SUBS):
        message[r : r + SUBS, :] = row


def coarse_nodes(gathered, gy_count, me):
    total_rows = gathered.shape[0]
    shape = gathered.shape
    lane = lane_iota(shape)
    row = sub_iota(shape)
    corner = lane // 32
    column = lane // 8 % 2
    last = row % gy_count == gy_count - 1
    start = row % gy_count == 0
    one = gathered
    two = turn(gathered, -1)
    four = turn(gathered, -2)
    rhs = turn(gathered, -3)
    two_back = turn(two, 32)

    def next_x(u):
        return turn(u, -gy_count, 0)

    def prev_x(u):
        return turn(u, gy_count, 0)

    def next_y(u):
        ahead = jnp.where(last, turn(u, gy_count - 1, 0), turn(u, -1, 0))
        return jnp.where(column == 0, turn(u, -8), turn(ahead, 8))

    def prev_y(u):
        behind = jnp.where(start, turn(u, 1 - gy_count, 0), turn(u, 1, 0))
        return jnp.where(column == 1, turn(u, 8), turn(behind, -8))

    def by_corner(a, b, c, d):
        return jnp.where(corner == 0, a, jnp.where(corner == 1, b, jnp.where(corner == 2, c, d)))

    def corners(u):
        ux = next_x(u)
        return by_corner(u, next_y(u), ux, next_y(ux))

    def assemble(v):
        vx = prev_x(v)
        w = by_corner(v, prev_y(v), vx, prev_y(vx))
        w = w + turn(w, 64)
        return w + turn(w, 32)

    def operate(u):
        c = corners(u)
        return assemble(one * c + two * turn(c, -32) + two_back * turn(c, 32) + four * turn(c, 64))

    def total(a, b):
        v = a * b
        v = tree([v[r : r + SUBS] for r in range(0, total_rows, SUBS)])
        for shift in (4, 2, 1):
            v = v + turn(v, shift, 0)
        v = v + xor_lane(v, 8)
        return v[0:1]

    residual = -assemble(rhs)
    direction = residual
    update = jnp.zeros_like(residual)
    now = total(residual, residual)
    for step in range(2):
        image = operate(direction)
        alpha = now / total(direction, image)
        update = update + alpha * direction
        if step == 0:
            residual = residual - alpha * image
            new = total(residual, residual)
            direction = residual + new / now * direction
            now = new
    mine = jnp.where(row == me, corners(update), 0.0)
    mine = jnp.sum(mine, axis=0, keepdims=True)
    return jnp.broadcast_to(mine, (SUBS, LANES))


def turn_kernel(phi_fine, phi_twin, fine_out, twin_out):
    for lv, phi_ref, out_ref in ((FINE, phi_fine, fine_out), (TWIN, phi_twin, twin_out)):
        s = lv.seg
        nz = EZ * lv.edz
        per = LANES // nz
        tiles = lv.edge // per
        for i in range(s):
            for t in range(tiles):
                parts = []
                for n in range(per):
                    y = lv.mx + t * per + n
                    start = (i * s + y % s) * SUBS + y // s
                    parts.append(phi_ref[pl.ds(start, nz, stride=lv.tiles * SUBS), :])
                out_ref[i * tiles + t] = jnp.concatenate(parts, axis=0).T


def pressure_kernel(gy_count, me_ref, gathered, fine_turned, twin_turned, fine_out, twin_out, fine_all, twin_all):
    mine = coarse_nodes(gathered[...], gy_count, me_ref[0])
    for n, (lv, turned, out_ref, all_ref) in enumerate(
        ((FINE, fine_turned, fine_out, fine_all), (TWIN, twin_turned, twin_out, twin_all))
    ):
        s = lv.seg
        nz = EZ * lv.edz
        tiles = lv.edge * nz // LANES
        lower = lane_iota() % nz < lv.edz
        scales = {}
        for c in range(COLUMNS):
            for p in range(4):
                at = p * 32 + n * 16 + c * 8
                node = jnp.broadcast_to(mine[:, at : at + 1], (SUBS, LANES))
                scales[2 * p, c] = jnp.where(lower, 1.0, node)
                scales[2 * p + 1, c] = jnp.where(lower, node, 0.0)
        for c in range(COLUMNS):
            for t in range(tiles):
                at = (c * tiles + t) * LANES
                for i in range(s):
                    value = tree(
                        [turned[i * tiles + t, a * 16 + c * 8 : a * 16 + c * 8 + 8, :] * scales[a, c] for a in range(8)]
                    )
                    all_ref[c * tiles + t, pl.ds(i, SUBS, stride=s), :] = value
                out_ref[:, at : at + LANES] = all_ref[c * tiles + t, lv.mx : lv.mx + lv.edge, :]


def vmem(shape, dtype=F32):
    return pltpu.VMEM(shape, dtype)


def shards(permeability):
    nz = EZ * ELZ
    rows = permeability.shape[1]
    lanes = permeability.shape[2]
    assert rows == EL and lanes == COLUMNS * EL * nz
    rim = MX * nz
    gx, gy = lax.axis_size("gx"), lax.axis_size("gy")

    def sent(value, axis, shift):
        count = lax.axis_size(axis)
        return lax.ppermute(value, axis, [(i, (i + shift) % count) for i in range(count)])

    x_low = sent(permeability[:, rows - MX :], "gx", 1)
    x_high = sent(permeability[:, :MX], "gx", -1)

    def strip(part):
        return jnp.concatenate([x_low[:, :, part], permeability[:, :, part], x_high[:, :, part]], axis=1)

    y_low = sent(strip(slice(lanes - rim, lanes)), "gy", 1)
    y_high = sent(strip(slice(0, rim)), "gy", -1)
    halos = [x_low, x_high, y_low, y_high]
    flat_lanes = lanes + 2 * rim
    scratch = [
        vmem((LANES, flat_lanes)),
        vmem((flat_lanes, LANES)),
        vmem((flat_lanes // 2, LANES)),
        vmem((SUBS * (TWIN.seg + 2) * nz, LANES)),
    ]
    for lv in LEVELS:
        scratch.append(vmem((lv.planes + 1, lv.seg, SUBS, 2 * LANES)))
        scratch += [vmem((lv.planes * lv.seg // 2, 2 * SUBS, 2 * LANES), BF16)] * 3
        scratch += [vmem((lv.seg, lv.planes * lv.seg, SUBS, LANES))] * 3
        for e in range(EZ):
            scratch += [vmem((lv.inner + 1, lv.tiles, SUBS, LANES))] * 5
            scratch.append(vmem((lv.tiles, SUBS, LANES)))
    full = pl.BlockSpec(memory_space=pltpu.VMEM)
    phi_shapes = [
        jax.ShapeDtypeStruct((EZ * lv.edz * lv.tiles * SUBS, LANES), F32) for lv in LEVELS
    ]
    phi_fine, phi_twin, message = pl.pallas_call(
        solve_kernel,
        out_shape=phi_shapes + [jax.ShapeDtypeStruct((gx * gy, LANES), F32)],
        in_specs=[full] * 5,
        out_specs=[full] * 3,
        scratch_shapes=scratch,
        compiler_params=pltpu.CompilerParams(vmem_limit_bytes=52 * 1024 * 1024),
        name="solve",
    )(permeability, *halos)
    gathered = lax.all_to_all(message, ("gx", "gy"), 0, 0, tiled=True)
    turned = pl.pallas_call(
        turn_kernel,
        out_shape=[
            jax.ShapeDtypeStruct((lv.seg * lv.edge * EZ * lv.edz // LANES, LANES, LANES), F32) for lv in LEVELS
        ],
        in_specs=[full] * 2,
        out_specs=[full] * 2,
        compiler_params=pltpu.CompilerParams(vmem_limit_bytes=16 * 1024 * 1024),
        cost_estimate=pl.CostEstimate(flops=4000000, bytes_accessed=8000000, transcendentals=0),
        name="turned",
    )(phi_fine, phi_twin)
    me = (lax.axis_index("gx") * gy + lax.axis_index("gy")).astype(jnp.int32).reshape(1)
    return tuple(
        pl.pallas_call(
            functools.partial(pressure_kernel, gy),
            out_shape=[
                jax.ShapeDtypeStruct((lv.edge, COLUMNS * lv.edge * EZ * lv.edz), F32) for lv in LEVELS
            ],
            in_specs=[pl.BlockSpec(memory_space=pltpu.SMEM)] + [full] * 3,
            out_specs=[full] * 2,
            scratch_shapes=[vmem((COLUMNS * lv.edge * EZ * lv.edz // LANES, SUBS * lv.seg, LANES)) for lv in LEVELS],
            compiler_params=pltpu.CompilerParams(vmem_limit_bytes=16 * 1024 * 1024),
            name="pressure",
        )(me, gathered, *turned)
    )


def solution(mesh):
    return jax.shard_map(
        shards,
        mesh=mesh,
        in_specs=(P(None, "gx", "gy"),),
        out_specs=(P("gx", "gy"), P("gx", "gy")),
        check_vma=False,
    )
```

time: 103 us -> 85 us (0.83)
  Pallas kernels: 72.6 us -> 56.5 us
  waiting for transfers between devices: 15 us -> 11.5 us
  local copies, waits for them, and re-layouts: 5.51 us -> 6.69 us
    pallas_call x1 -> x2, Pallas kernels: 13.8 us -> 3.21 us  [the longest x1 2.38 us: shards(): pl.pallas_call(functools.partial(pressure_kernel, gy), out_shape=[jax.Sha...]
    pallas_call x1, Pallas kernels: 58.8 us -> 53.3 us  [shards(): pl.pallas_call(solve_kernel, out_shape=phi_shapes + [jax.ShapeDtypeStruct...]
    all_to_all x1, waiting for transfers between devices: 7.07 us -> 3.55 us  [shards(): gathered = lax.all_to_all(message, ('gx', 'gy'), 0, 0, tiled=True)]
    unnamed x12 -> x8, local copies, waits for them, and re-layouts: 3.61 us -> 4.79 us
  transfers between devices with their start and end apart: 5 -> 5, of which waited for: 5 -> 5; matrix products, arithmetic and copies ran while one was open for 1% -> 1% of each run, Pallas kernels for 0% -> 1%
where the time goes in v1:
time: 85 us; the launch traced here: 84.7 us
  Pallas kernels  56.5 us (66%)
  waiting for transfers between devices  11.5 us (14%)
  starting transfers between devices  9.27 us (11%)
  local copies, waits for them, and re-layouts  6.69 us (8%)
    pallas_call x1, Pallas kernels, shards(): pl.pallas_call(solve_kernel, out_shape=phi_shapes + [jax.ShapeDtypeStruct...  53.3 us
    ppermute x4, waiting for transfers between devices, sent(): lax.ppermute(value, axis, [(i, (i + shift) % count) for i in range(count)])  7.97 us
    ppermute x4, starting transfers between devices, sent(): lax.ppermute(value, axis, [(i, (i + shift) % count) for i in range(count)])  6.73 us
    unnamed x8, local copies, waits for them, and re-layouts  4.79 us
    all_to_all x1, waiting for transfers between devices, shards(): gathered = lax.all_to_all(message, ('gx', 'gy'), 0, 0, tiled=True)  3.55 us
    all_to_all x1, starting transfers between devices, shards(): gathered = lax.all_to_all(message, ('gx', 'gy'), 0, 0, tiled=True)  2.54 us
    pallas_call x1, Pallas kernels, shards(): pl.pallas_call(functools.partial(pressure_kernel, gy), out_shape=[jax.Sha...  2.38 us
  transfers between devices with their start and end apart: 5, of which 5 were waited for; matrix products, arithmetic and copies ran while one was open for 1% of the time, Pallas kernels for 1%

profile of v1, /device:TPU:0, one launch (start us, length us, event | category | flops | bytes accessed | tf_op | source)
XLA Modules:
  0.0 84.7 jit_solution(9599851218050427427)
XLA Ops:
  0.6 1.1 %fusion.1 = (f32[3,4,2048]{2,1,0:T(4,128)S(1)}, f32[3,4,2048]{2,1,0:T(4,128)S(1)}) fusion(f32[3,32,2048]{2,1,0:T(8,128)} %center.1), kind=kLoop, calls=%fused_computation.3 | loop fusion | bytes 393216 | tf_op jit(solution)/shard_map/slice | solution.py:684
  1.7 3.1 %collective-permute-start = (f32[3,4,2048]{2,1,0:T(4,128)S(1)}, f32[3,4,2048]{2,1,0:T(4,128)S(1)}, u32[]{:S(2)}, u32[]{:S(2)}) collective-permute-start(f32[3,4,2048]{2,1,0:T(4,128)S(1)} %get-tuple-element.15), channel_id=1, source_target_pairs={{0,8},{8,16},{16,24},{24,0},{1,9},{9,17},{17,25},{25,1},{2,10},{10... | collective-permute-start | bytes 294920 | tf_op jit(solution)/shard_map/ppermute | solution.py:681
  4.8 2.1 %collective-permute-start.1 = (f32[3,4,2048]{2,1,0:T(4,128)S(1)}, f32[3,4,2048]{2,1,0:T(4,128)S(1)}, u32[]{:S(2)}, u32[]{:S(2)}) collective-permute-start(f32[3,4,2048]{2,1,0:T(4,128)S(1)} %get-tuple-element.14), channel_id=1, source_target_pairs={{0,24},{8,0},{16,8},{24,16},{1,25},{9,1},{17,9},{25,17},{2,26},{10... | collective-permute-start | bytes 294920 | tf_op jit(solution)/shard_map/ppermute | solution.py:681
  6.9 0.8 fusion
  7.7 2.6 %collective-permute-done.x_low = f32[3,4,2048]{2,1,0:T(4,128)S(1)} collective-permute-done((f32[3,4,2048]{2,1,0:T(4,128)S(1)}, f32[3,4,2048]{2,1,0:T(4,128)S(1)}, u32[]{:S(2)}, u32[]{:S(2)}) %collective-permute-start) | collective-permute-done | bytes 98336 | tf_op jit(solution)/shard_map/ppermute | solution.py:681
  10.3 0.8 collective-permute-done.1.x_high
  11.1 1.5 %collective-permute-start.3 = (f32[3,40,128]{2,1,0:T(8,128)S(1)}, f32[3,40,128]{2,1,0:T(8,128)S(1)}, u32[]{:S(2)}, u32[]{:S(2)}) collective-permute-start(f32[3,40,128]{2,1,0:T(8,128)S(1)} %pad_maximum_fusion.1), channel_id=1, source_target_pairs={{0,7},{1,0},{2,1},{3,2},{4,3},{5,4},{6,5},{7,6},{8,15},{9,8},{10,9... | collective-permute-start | bytes 184328 | tf_op jit(solution)/shard_map/ppermute | solution.py:681
  12.7 0.1 collective-permute-start.2
  12.7 1.9 %collective-permute-done.3.y_high = f32[3,40,128]{2,1,0:T(8,128)S(1)} collective-permute-done((f32[3,40,128]{2,1,0:T(8,128)S(1)}, f32[3,40,128]{2,1,0:T(8,128)S(1)}, u32[]{:S(2)}, u32[]{:S(2)}) %collective-permute-start.3) | collective-permute-done | bytes 61472 | tf_op jit(solution)/shard_map/ppermute | solution.py:681
  14.6 2.7 %collective-permute-done.2.y_low = f32[3,40,128]{2,1,0:T(8,128)S(1)} collective-permute-done((f32[3,40,128]{2,1,0:T(8,128)S(1)}, f32[3,40,128]{2,1,0:T(8,128)S(1)}, u32[]{:S(2)}, u32[]{:S(2)}) %collective-permute-start.2) | collective-permute-done | bytes 61472 | tf_op jit(solution)/shard_map/ppermute | solution.py:681
  17.3 0.0 copy-start.1
  17.3 1.1 %copy-done.1 = f32[3,32,2048]{2,1,0:T(8,128)S(1)} copy-done((f32[3,32,2048]{2,1,0:T(8,128)S(1)}, f32[3,32,2048]{2,1,0:T(8,128)}, u32[]{:S(2)}) %copy-start.1) | copy-done | bytes 786456
  18.4 53.3 %solve.1 = (f32[6400,128]{1,0:T(8,128)}, f32[1152,128]{1,0:T(8,128)S(1)}, f32[32,128]{1,0:T(8,128)}) custom-call(f32[3,32,2048]{2,1,0:T(8,128)S(1)} %copy-done.1, f32[3,4,2048]{2,1,0:T(4,128)S(1)} %collective-permute-done.x_low, f32[3,4,2048]{2,1,0:T(4,128)S(1)} %collective-permute-done.1.x_high, f32[3,40,128]{2,1,0:T(8,128)S(1)} %collective-permute-done.2.y_low, ...), custom_call_target="tpu_custom_call" | custom-call | tf_op jit(solution)/shard_map/solve/pallas_call | solution.py:710
  71.7 2.5 %all-to-all-start = ((f32[32,1,128]{2,1,0:T(1,128)}), f32[32,1,128]{2,1,0:T(1,128)S(1)}, u32[]{:S(2)}, u32[]{:S(2)}) async-start(f32[32,1,128]{2,1,0:T(1,128)} %bitcast.2), calls=%async_computation | async-start | bytes 32768 | tf_op jit(solution)/shard_map/all_to_all | solution.py:719
  74.2 0.0 copy-start
  74.2 1.9 %copy-done = f32[6400,128]{1,0:T(8,128)S(1)} copy-done((f32[6400,128]{1,0:T(8,128)S(1)}, f32[6400,128]{1,0:T(8,128)}, u32[]{:S(2)}) %copy-start) | copy-done | bytes 3276824
  76.1 0.8 turned.1
  77.0 0.0 copy-start.2
  77.0 0.7 copy-done.2
  77.7 3.5 %all-to-all-done = f32[32,1,128]{2,1,0:T(1,128)S(1)} async-done(((f32[32,1,128]{2,1,0:T(1,128)}), f32[32,1,128]{2,1,0:T(1,128)S(1)}, u32[]{:S(2)}, u32[]{:S(2)}) %all-to-all-start) | async-done | bytes 16416 | tf_op jit(solution)/shard_map/all_to_all | solution.py:719
  81.3 0.0 copy-start.3
  81.3 1.0 %copy-done.3 = f32[6,128,128]{2,1,0:T(8,128)S(1)} copy-done((f32[6,128,128]{2,1,0:T(8,128)S(1)}, f32[6,128,128]{2,1,0:T(8,128)}, u32[]{:S(2)}) %copy-start.3) | copy-done | bytes 393240
  82.3 2.4 %pressure.1 = (f32[32,2048]{1,0:T(8,128)}, f32[16,512]{1,0:T(8,128)}) custom-call(s32[1]{0:T(128)} %bitcast.me_ref, f32[32,128]{1,0:T(8,128)S(1)} %bitcast.5, f32[40,128,128]{2,1,0:T(8,128)S(1)} %get-tuple-element.10.fine_turned, f32[6,128,128]{2,1,0:T(8,128)S(1)} %copy-done.3), custom_call_target="tpu_custom_call" | custom-call | tf_op jit(solution)/shard_map/pressure/pallas_call | solution.py:733
  (4 shorter events, 0.0 us)
Async XLA Ops:
  1.7 8.6 %collective-permute-start = (f32[3,4,2048]{2,1,0:T(4,128)S(1)}, f32[3,4,2048]{2,1,0:T(4,128)S(1)}, u32[]{:S(2)}, u32[]{:S(2)}) collective-permute-start(f32[3,4,2048]{2,1,0:T(4,128)S(1)} %get-tuple-element.15), channel_id=1, source_target_pairs={{0,8},{8,16},{16,24},{24,0},{1,9},{9,17},{17,25},{25,1},{2,10},{10... | collective-permute-start | bytes 294920 | tf_op jit(solution)/shard_map/ppermute | solution.py:681
  4.8 6.4 %collective-permute-start.1 = (f32[3,4,2048]{2,1,0:T(4,128)S(1)}, f32[3,4,2048]{2,1,0:T(4,128)S(1)}, u32[]{:S(2)}, u32[]{:S(2)}) collective-permute-start(f32[3,4,2048]{2,1,0:T(4,128)S(1)} %get-tuple-element.14), channel_id=1, source_target_pairs={{0,24},{8,0},{16,8},{24,16},{1,25},{9,1},{17,9},{25,17},{2,26},{10... | collective-permute-start | bytes 294920 | tf_op jit(solution)/shard_map/ppermute | solution.py:681
  11.1 3.5 %collective-permute-start.3 = (f32[3,40,128]{2,1,0:T(8,128)S(1)}, f32[3,40,128]{2,1,0:T(8,128)S(1)}, u32[]{:S(2)}, u32[]{:S(2)}) collective-permute-start(f32[3,40,128]{2,1,0:T(8,128)S(1)} %pad_maximum_fusion.1), channel_id=1, source_target_pairs={{0,7},{1,0},{2,1},{3,2},{4,3},{5,4},{6,5},{7,6},{8,15},{9,8},{10,9... | collective-permute-start | bytes 184328 | tf_op jit(solution)/shard_map/ppermute | solution.py:681
  12.7 4.6 %collective-permute-start.2 = (f32[3,40,128]{2,1,0:T(8,128)S(1)}, f32[3,40,128]{2,1,0:T(8,128)S(1)}, u32[]{:S(2)}, u32[]{:S(2)}) collective-permute-start(f32[3,40,128]{2,1,0:T(8,128)S(1)} %pad_maximum_fusion), channel_id=1, source_target_pairs={{0,1},{1,2},{2,3},{3,4},{4,5},{5,6},{6,7},{7,0},{8,9},{9,10},{10,1... | collective-permute-start | bytes 184328 | tf_op jit(solution)/shard_map/ppermute | solution.py:681
  17.3 1.1 %copy-start.1 = (f32[3,32,2048]{2,1,0:T(8,128)S(1)}, f32[3,32,2048]{2,1,0:T(8,128)}, u32[]{:S(2)}) copy-start(f32[3,32,2048]{2,1,0:T(8,128)} %center.1) | copy-start | bytes 2359300
  71.7 9.6 %all-to-all-start = ((f32[32,1,128]{2,1,0:T(1,128)}), f32[32,1,128]{2,1,0:T(1,128)S(1)}, u32[]{:S(2)}, u32[]{:S(2)}) async-start(f32[32,1,128]{2,1,0:T(1,128)} %bitcast.2), calls=%async_computation | async-start | bytes 32768 | tf_op jit(solution)/shard_map/all_to_all | solution.py:719
  74.2 1.9 %copy-start = (f32[6400,128]{1,0:T(8,128)S(1)}, f32[6400,128]{1,0:T(8,128)}, u32[]{:S(2)}) copy-start(f32[6400,128]{1,0:T(8,128)} %get-tuple-element.8.phi_fine) | copy-start | bytes 9830404
  77.0 0.8 copy-start.2
  81.3 1.0 %copy-start.3 = (f32[6,128,128]{2,1,0:T(8,128)S(1)}, f32[6,128,128]{2,1,0:T(8,128)}, u32[]{:S(2)}) copy-start(f32[6,128,128]{2,1,0:T(8,128)} %copy-done.2) | copy-start | bytes 1179652

commit v2 on v1

v2 whole, which is shorter than its diff:
```python
import functools
import typing

import jax
import jax.numpy as jnp
from jax import lax
from jax.experimental import pallas as pl
from jax.experimental.pallas import tpu as pltpu
from jax.sharding import PartitionSpec as P

EL = 32
ELZ = 16
MX = 4
MZ = 2
EZ = 2
LANES = 128
SUBS = 8
COLUMNS = 2
F32 = jnp.float32
BF16 = jnp.bfloat16


class Level(typing.NamedTuple):
    edge: int
    edz: int
    mx: int
    mz: int
    spacing: float
    step: int

    @property
    def width(self):
        return self.edge + 2 * self.mx

    @property
    def inner(self):
        return self.edz + 2 * self.mz - 2

    @property
    def seg(self):
        return -(-self.width // SUBS)

    @property
    def tiles(self):
        return self.seg * self.seg

    @property
    def levels(self):
        return EZ * self.edz + 2

    @property
    def planes(self):
        return -(-(self.inner + 1) // 2) * 2


FINE = Level(EL, ELZ, MX, MZ, 1.0, 1)
TWIN = Level(EL // 2, ELZ // 2, MX // 2, MZ // 2, 2.0, 2)
LEVELS = (FINE, TWIN)


def lane_iota(shape=(SUBS, LANES)):
    return lax.broadcasted_iota(jnp.int32, shape, len(shape) - 1)


def sub_iota(shape=(SUBS, LANES)):
    return lax.broadcasted_iota(jnp.int32, shape, len(shape) - 2)


def turn(value, shift, axis=1):
    return pltpu.roll(value, shift % value.shape[axis], axis)


def lane_parts():
    lane = lane_iota()
    return lane // 32, lane // 16 % 2, lane // 8 % 2, lane % 8


class Consts:
    def __init__(self, lv):
        corner, _, _, xo = lane_parts()
        yo = sub_iota()
        ax, ay = corner // 2, corner % 2
        self.lv = lv
        s = lv.seg
        self.fx, self.fy = [], []
        self.inx, self.iny, self.facex, self.facey = [], [], [], []
        for i in range(s):
            x = xo * s + i
            y = yo * s + i
            px = (x.astype(F32) - lv.mx + 0.5) / lv.edge
            py = (y.astype(F32) - lv.mx + 0.5) / lv.edge
            self.fx.append(jnp.where(ax == 1, px, 1.0 - px))
            self.fy.append(jnp.where(ay == 1, py, 1.0 - py))
            xs = [s * o + i for o in range(SUBS)]

            def ranged(value, low, high):
                if all(low <= v <= high for v in xs):
                    return None
                return ((value >= low) & (value <= high)).astype(F32)

            self.inx.append((ranged(x, 1, lv.width - 2), ranged(x, lv.mx, lv.mx + lv.edge - 1)))
            self.iny.append((ranged(y, 1, lv.width - 2), ranged(y, lv.mx, lv.mx + lv.edge - 1)))
            cut = (lv.mx - 1, lv.mx + lv.edge - 1)
            self.facex.append(((x != cut[0]) & (x != cut[1])).astype(F32) if any(v in cut for v in xs) else None)
            self.facey.append(((y != cut[0]) & (y != cut[1])).astype(F32) if any(v in cut for v in xs) else None)
        sx = jnp.where(ax == 1, -1.0 / lv.edge, 1.0 / lv.edge).astype(F32)
        sy = jnp.where(ay == 1, -1.0 / lv.edge, 1.0 / lv.edge).astype(F32)
        self.along_x = [sx * f for f in self.fy]
        self.along_y = [sy * f for f in self.fx]

    def fz(self, plane):
        place = (jnp.asarray(plane, jnp.int32).astype(F32) - self.lv.mz + 0.5) / self.lv.edz
        return 1.0 - place, place

    def masked(self, value, i, j, kind):
        for table, index in ((self.inx, i), (self.iny, j)):
            factor = table[index][kind]
            if factor is not None:
                value = value * factor
        return value


def tree(values):
    values = list(values)
    while len(values) > 1:
        values = [a + b for a, b in zip(values[::2], values[1::2])] + (
            [values[-1]] if len(values) % 2 else []
        )
    return values[0]


def xor_lane(value, bit):
    return jnp.where(lane_iota(value.shape) // bit % 2 == 1, turn(value, bit), turn(value, -bit))


def problem_sum(value):
    for shift in (4, 2, 1):
        value = value + turn(value, shift, 0)
    for bit in (1, 2, 4):
        value = value + xor_lane(value, bit)
    return value


def spread_weights(lv, k_ref, high_refs, low_refs, w_refs):
    s = lv.seg
    wide = (SUBS, LANES)
    pos = lane_iota(wide)
    yo = sub_iota(wide)
    first = pos < 40
    third = pos >= 80
    second = (pos >= 40) & (pos < 80)
    edge_x = first & (pos >= (lv.width - 1) * lv.step)

    def one(z, i, c):
        part = slice(c * LANES, (c + 1) * LANES)
        k = k_ref[z, i, :, part]
        nbx = turn(k, -lv.step)
        nby = k_ref[z, i + 1, :, part] if i < s - 1 else turn(k_ref[z, 0, :, part], -1, 0)
        nbz = k_ref[z + 1, i, :, part]
        nb = jnp.where(first, nbx, jnp.where(second, nby, nbz))
        w = (2.0 * lv.spacing) * k * nb / (k + nb)
        bad = edge_x | (second & (yo * s + i >= lv.width - 1))
        return jnp.where(bad, 0.0, w)

    def planes(t, _):
        units = [(2 * t + n, i) for n in range(2) for i in range(s)]
        for e in range(EZ):
            made = []
            for plane, i in units:
                z = jnp.clip(e * lv.edz + plane + 1 - lv.mz, 0, lv.levels - 1)
                w0, w1 = one(z, i, 0), one(z, i, 1)
                near, wrap = turn(w1, 40), turn(w1, 48)
                made.append((jnp.where(first, w0, near), jnp.where(third, near, w0), jnp.where(third, w0, wrap)))
            for p in range(s):
                for m in range(3):
                    both = jnp.concatenate([made[2 * p][m], made[2 * p + 1][m]], axis=0)
                    high = both.astype(BF16)
                    part = slice(e * LANES, (e + 1) * LANES)
                    high_refs[m][t * s + p, :, part] = high
                    low_refs[m][t * s + p, :, part] = (both - high.astype(F32)).astype(BF16)
        return 0

    lax.fori_loop(0, lv.planes // 2, planes, 0)
    rows = lv.planes * s * SUBS
    row = lax.broadcasted_iota(jnp.int32, (2 * LANES, 2 * LANES), 0)
    lane = lax.broadcasted_iota(jnp.int32, (1, 2 * LANES), 1)
    upper = lane // LANES
    for q in range(-(-s // 2)):
        x = lane % 8 * s + 2 * q + upper
        valid = (x < lv.width) & (2 * q + upper < s)
        for m in range(3):
            segment = jnp.where(lane // 8 % 2 == 0, m, (m + 1) % 3)
            source = jnp.where(valid, lane // 16 % 2 * LANES + segment * 40 + lv.step * x, -1)
            pick = (row == source).astype(F32).astype(BF16)
            out = jnp.dot(high_refs[m][...].reshape(rows, 2 * LANES), pick, preferred_element_type=F32)
            out = out + jnp.dot(low_refs[m][...].reshape(rows, 2 * LANES), pick, preferred_element_type=F32)
            for half in range(min(2, s - 2 * q)):
                part = out[:, half * LANES : (half + 1) * LANES]
                w_refs[m][2 * q + half] = part.reshape(lv.planes * s, SUBS, LANES)


class Case:
    def __init__(self, lv, w_refs, fields, planes):
        self.lv, self.cs, self.w_refs = lv, Consts(lv), w_refs
        self.d, self.q, self.r = fields[:3], fields[3], fields[4]
        self.fz, self.chosen, self.total = planes

    def weights(self, plane):
        s = self.lv.seg
        return lambda m, i, j: self.w_refs[m][i, plane * s + j]


HALVES = (0, 1)


def looped(count, group, sums, step):
    def body(t, sums):
        return tuple(a + b for a, b in zip(sums, step(t * group)))

    start = tuple(jnp.zeros((SUBS, LANES), F32) for _ in range(sums))
    return list(lax.fori_loop(0, count // group, body, start))


def start_residual(case, group):
    lv, cs, s = case.lv, case.cs, case.lv.seg

    def step(z0):
        total = [[], []]
        for z in [z0 + n for n in range(group)]:
            get, below = case.weights(z + 1), case.weights(z)
            gz = cs.fz(z + 1)
            last = [get(1, i, s - 1) * cs.along_y[i] for i in range(s)]
            before = [turn(v, 1, 0) for v in last]
            for j in range(s):
                flux_y = last if j == s - 1 else [get(1, i, j) * cs.along_y[i] for i in range(s)]
                flux_x = [get(0, i, j) * cs.along_x[j] for i in range(s)]
                squares = [[], []]
                for i in range(s):
                    k = i * s + j
                    prev_x = flux_x[i - 1] if i else turn(flux_x[s - 1], 1)
                    flat = (prev_x - flux_x[i]) + (before[i] - flux_y[i])
                    flat = cs.masked(flat, i, j, 0)
                    tall = (cs.fx[i] * cs.fy[j]) * (1.0 / lv.edz) * (below(2, i, j) - get(2, i, j))
                    tall = cs.masked(tall, i, j, 0)
                    for h, value in enumerate((flat * gz[0] + tall, flat * gz[1] - tall)):
                        case.d[0][z, h * lv.tiles + k] = value
                        squares[h].append(value * value)
                for h in HALVES:
                    total[h].append(tree(squares[h]))
                before = flux_y
        return [tree(t) for t in total]

    return looped(lv.inner, group, 2, step)


def row_jumps(u, s, j):
    jump_x = [u[i * s + j] - (u[(i + 1) * s + j] if i < s - 1 else turn(u[j], -1)) for i in range(s)]
    jump_y = [u[i * s + j] - (u[i * s + j + 1] if j < s - 1 else turn(u[i * s], -1, 0)) for i in range(s)]
    return jump_x, jump_y


def apply(case, group, number, betas):
    lv, cs, s = case.lv, case.cs, case.lv.seg
    keep = number < 2
    n = lv.tiles

    def fresh(z, h, k):
        at = h * n + k
        if number == 0:
            return case.d[0][z, at]
        value = case.r[z, at] + betas[h] * case.d[number - 1][z, at]
        case.d[number][z, at] = value
        return value

    firsts = []
    get = case.weights(0)
    for h in HALVES:
        terms = []
        for k in range(n):
            value = fresh(0, h, k)
            flux = -get(2, k // s, k % s) * value
            if keep:
                case.fz[h * n + k] = flux
            else:
                terms.append(-flux * value)
        firsts.append(tree(terms) if terms else 0.0)

    def step(z0):
        total = [[], []]
        u = [[case.d[number][z0, h * n + k] for k in range(n)] for h in HALVES]
        flux_z = [[case.fz[h * n + k] for k in range(n)] for h in HALVES] if keep else None
        for z in [z0 + t for t in range(group)]:
            get = case.weights(z + 1)
            after = [[None] * n for _ in HALVES]
            if keep:
                wy = [get(1, i, s - 1) for i in range(s)]
                last = [[wy[i] * (u[h][i * s + s - 1] - turn(u[h][i * s], -1, 0)) for i in range(s)] for h in HALVES]
                before = [[turn(v, 1, 0) for v in last[h]] for h in HALVES]
            for j in range(s):
                wx = [get(0, i, j) for i in range(s)]
                wy = [get(1, i, j) for i in range(s)]
                wz = [get(2, i, j) for i in range(s)]
                for h in HALVES:
                    jump_x, jump_y = row_jumps(u[h], s, j)
                    flux_x = [w * v for w, v in zip(wx, jump_x)]
                    flux_y = last[h] if keep and j == s - 1 else [w * v for w, v in zip(wy, jump_y)]
                    terms = []
                    for i in range(s):
                        k = i * s + j
                        after[h][k] = fresh(z + 1, h, k)
                        jump = u[h][k] - after[h][k]
                        flux = wz[i] * jump
                        if keep:
                            prev_x = flux_x[i - 1] if i else turn(flux_x[s - 1], 1)
                            value = (flux_x[i] - prev_x) + (flux_y[i] - before[h][i]) + (flux - flux_z[h][k])
                            flux_z[h][k] = flux
                            value = cs.masked(value, i, j, 0)
                            case.q[z, h * n + k] = value
                            terms.append(u[h][k] * value)
                        else:
                            terms.append((flux * jump + flux_x[i] * jump_x[i]) + flux_y[i] * jump_y[i])
                    total[h].append(tree(terms))
                    if keep:
                        before[h] = flux_y
            u = after
        if keep:
            for h in HALVES:
                for k in range(n):
                    case.fz[h * n + k] = flux_z[h][k]
        return [tree(t) for t in total]

    return [a + b for a, b in zip(looped(lv.inner, group, 2, step), firsts)]


def reduce_residual(case, group, number, alphas):
    lv = case.lv

    def step(z0):
        total = [[], []]
        source = case.d[0] if number == 0 else case.r
        for z in [z0 + n for n in range(group)]:
            for h in HALVES:
                squares = []
                for k in range(lv.tiles):
                    at = h * lv.tiles + k
                    value = source[z, at] - alphas[h] * case.q[z, at]
                    case.r[z, at] = value
                    squares.append(value * value)
                total[h].append(tree(squares))
        return [tree(t) for t in total]

    return looped(lv.inner, group, 2, step)


def finish(case, group, alphas, phi_ref):
    lv, cs, s = case.lv, case.cs, case.lv.seg
    n = lv.tiles
    lower = lane_parts()[1] == 0

    def fresh(z, i, j, gz):
        k = i * s + j
        inner = z + lv.mz - 1
        both = cs.fx[i] * cs.fy[j]
        values = []
        for h in HALVES:
            value = both * gz[h]
            for alpha, d_ref in zip(alphas[h], case.d):
                value = value + alpha * d_ref[inner, h * n + k]
            value = cs.masked(value, i, j, 1)
            at = pl.multiple_of(((z * 2 + h) * n + k) * SUBS, SUBS)
            phi_ref[pl.ds(at, SUBS), :] = value
            values.append(value)
        total = values[0] + turn(values[0], 32)
        return jnp.where(lower, values[1], values[0]), total + turn(total, 64)

    gz = cs.fz(lv.mz)
    for i in range(s):
        for j in range(s):
            k = i * s + j
            case.chosen[k], case.total[k] = fresh(0, i, j, gz)
            case.fz[k] = jnp.zeros((SUBS, LANES), F32)

    def cut(values, table):
        return [v if f is None else v * f for v, f in zip(values, table)]

    def step(z0):
        sums = [[] for _ in range(4)]
        u = [case.chosen[k] for k in range(n)]
        low = [case.total[k] for k in range(n)]
        flux_z = [case.fz[k] for k in range(n)]
        for z in [z0 + t for t in range(group)]:
            get = case.weights(z + lv.mz)
            up = jnp.minimum(z + 1, lv.edz - 1)
            gz = cs.fz(up + lv.mz)
            after, after_low = [None] * n, [None] * n
            last = [get(1, i, s - 1) * (u[i * s + s - 1] - turn(u[i * s], -1, 0)) for i in range(s)]
            last = cut(last, [cs.facey[s - 1]] * s)
            before = [turn(v, 1, 0) for v in last]
            for j in range(s):
                jump_x, jump_y = row_jumps(u, s, j)
                flux_x = cut([get(0, i, j) * jump_x[i] for i in range(s)], cs.facex)
                flux_y = last
                if j < s - 1:
                    flux_y = cut([get(1, i, j) * jump_y[i] for i in range(s)], [cs.facey[j]] * s)
                parts = [[] for _ in sums]
                for i in range(s):
                    k = i * s + j
                    after[k], after_low[k] = fresh(up, i, j, gz)
                    flux = get(2, i, j) * (u[k] - after[k])
                    prev_x = flux_x[i - 1] if i else turn(flux_x[s - 1], 1)
                    value = (flux_x[i] - prev_x) + (flux_y[i] - before[i]) + (flux - flux_z[k])
                    flux_z[k] = flux
                    parts[0].append(value * u[k])
                    parts[1].append(value * turn(u[k], -32))
                    parts[2].append(value * turn(u[k], 64))
                    parts[3].append(value * low[k])
                for total, part in zip(sums, parts):
                    total.append(tree(part))
                before = flux_y
            u, low = after, after_low
        for k in range(n):
            case.fz[k], case.chosen[k], case.total[k] = flux_z[k], u[k], low[k]
        return [tree(total) for total in sums]

    return looped(lv.edz, group, 4, step)


GROUPS = {FINE: 1, TWIN: 4}


def solve_kernel(
    center, x_low, x_high, y_low, y_high,
    phi_fine, phi_twin, message,
    flat, rows, pairs, twin_rows, *refs,
):
    lanes = center.shape[2]
    rim = (flat.shape[1] - lanes) // 2
    nx = center.shape[1]
    top = MX + nx
    for m in range(3):
        off = m * (nx + 2 * MX)
        flat[off : off + top + MX, :rim] = y_low[m]
        flat[off : off + MX, rim : rim + lanes] = x_low[m]
        flat[off + MX : off + top, rim : rim + lanes] = center[m]
        flat[off + top : off + top + MX, rim : rim + lanes] = x_high[m]
        flat[off : off + top + MX, rim + lanes :] = y_high[m]
    used = 3 * (nx + 2 * MX)
    flat[used:, :] = jnp.ones((LANES - used, flat.shape[1]), F32)
    for t in range(flat.shape[1] // LANES):
        rows[t * LANES : (t + 1) * LANES, :] = flat[:, t * LANES : (t + 1) * LANES].T

    nz = EZ * ELZ
    twin_y = rows.shape[0] // nz // 2
    for y in range(twin_y):
        both = rows[2 * y * nz : (2 * y + 1) * nz, :] + rows[(2 * y + 1) * nz : (2 * y + 2) * nz, :]
        both = both + turn(both, -1)
        at = y * nz
        pairs[at : at + nz, :] = both
        twin_rows[at : at + 8, :] = jnp.broadcast_to(0.25 * both[0:1], (8, LANES))
        twin_rows[at + 8 + nz // 2 : at + nz, :] = jnp.broadcast_to(0.25 * both[nz - 1 : nz], (8, LANES))
    for y in range(twin_y):
        at = y * nz
        middle = pairs[pl.ds(at, nz // 2, stride=2), :] + pairs[pl.ds(at + 1, nz // 2, stride=2), :]
        twin_rows[at + 8 : at + 8 + nz // 2, :] = 0.125 * middle
    twin_rows[twin_y * nz :, :] = jnp.ones((twin_rows.shape[0] - twin_y * nz, LANES), F32)

    refs = list(refs)

    def take(count):
        got = refs[:count]
        del refs[:count]
        return got

    cases = []
    for lv, source in zip(LEVELS, (rows, twin_rows)):
        (k_ref,) = take(1)
        high_refs, low_refs, w_refs = take(3), take(3), take(3)
        for z in range(lv.levels + 1):
            cell = min(max(z - 1, 0), nz - 1) if lv is FINE else min(z, lv.levels - 1) + 7
            for i in range(lv.seg):
                for c in range(COLUMNS):
                    start = (lv.edge * c + i) * nz + cell
                    k_ref[z, i, :, c * LANES : (c + 1) * LANES] = source[pl.ds(start, SUBS, stride=lv.seg * nz), :]
        spread_weights(lv, k_ref, high_refs, low_refs, w_refs)
        case = Case(lv, w_refs, take(5), take(3))
        for k in range(2 * lv.tiles):
            case.d[0][lv.inner, k] = jnp.zeros((SUBS, LANES), F32)
            case.r[lv.inner, k] = jnp.zeros((SUBS, LANES), F32)
        cases.append(case)

    def both_levels(work):
        sums = [work(n, case, GROUPS[case.lv]) for n, case in enumerate(cases)]
        return [[problem_sum(v) for v in part] for part in sums]

    rr = both_levels(lambda n, case, group: start_residual(case, group))
    alphas = [[[], []] for _ in LEVELS]
    betas = [None] * len(LEVELS)
    for step in range(3):
        dots = both_levels(lambda n, case, group: apply(case, group, step, betas[n]))
        now = [[a / b for a, b in zip(rr[n], dots[n])] for n in range(len(LEVELS))]
        for n in range(len(LEVELS)):
            for h in HALVES:
                alphas[n][h].append(now[n][h])
        if step < 2:
            new = both_levels(lambda n, case, group: reduce_residual(case, group, step, now[n]))
            betas = [[a / b for a, b in zip(new[n], rr[n])] for n in range(len(LEVELS))]
            rr = new

    phis = (phi_fine, phi_twin)
    totals = both_levels(lambda n, case, group: finish(case, group, alphas[n], phis[n]))
    _, element, _, slot = lane_parts()
    packed = []
    for level in totals:
        parts = [v + xor_lane(v, 16) for v in level[:3]]
        parts.append(jnp.where(element == 0, level[3], turn(level[3], 16)))
        packed.append(
            jnp.where(slot == 0, parts[0], jnp.where(slot == 1, parts[1], jnp.where(slot == 2, parts[2], parts[3])))
        )
    row = jnp.where(element == 0, packed[0], packed[1])
    for r in range(0, message.shape[0], SUBS):
        message[r : r + SUBS, :] = row


def coarse_nodes(gathered, gy_count, me):
    total_rows = gathered.shape[0]
    shape = gathered.shape
    lane = lane_iota(shape)
    row = sub_iota(shape)
    corner = lane // 32
    column = lane // 8 % 2
    last = row % gy_count == gy_count - 1
    start = row % gy_count == 0
    one = gathered
    two = turn(gathered, -1)
    four = turn(gathered, -2)
    rhs = turn(gathered, -3)
    two_back = turn(two, 32)

    def next_x(u):
        return turn(u, -gy_count, 0)

    def prev_x(u):
        return turn(u, gy_count, 0)

    def next_y(u):
        ahead = jnp.where(last, turn(u, gy_count - 1, 0), turn(u, -1, 0))
        return jnp.where(column == 0, turn(u, -8), turn(ahead, 8))

    def prev_y(u):
        behind = jnp.where(start, turn(u, 1 - gy_count, 0), turn(u, 1, 0))
        return jnp.where(column == 1, turn(u, 8), turn(behind, -8))

    def by_corner(a, b, c, d):
        return jnp.where(corner == 0, a, jnp.where(corner == 1, b, jnp.where(corner == 2, c, d)))

    def corners(u):
        ux = next_x(u)
        return by_corner(u, next_y(u), ux, next_y(ux))

    def assemble(v):
        vx = prev_x(v)
        w = by_corner(v, prev_y(v), vx, prev_y(vx))
        w = w + turn(w, 64)
        return w + turn(w, 32)

    def operate(u):
        c = corners(u)
        return assemble(one * c + two * turn(c, -32) + two_back * turn(c, 32) + four * turn(c, 64))

    def total(a, b):
        v = a * b
        v = tree([v[r : r + SUBS] for r in range(0, total_rows, SUBS)])
        for shift in (4, 2, 1):
            v = v + turn(v, shift, 0)
        v = v + xor_lane(v, 8)
        return v[0:1]

    residual = -assemble(rhs)
    direction = residual
    update = jnp.zeros_like(residual)
    now = total(residual, residual)
    for step in range(2):
        image = operate(direction)
        alpha = now / total(direction, image)
        update = update + alpha * direction
        if step == 0:
            residual = residual - alpha * image
            new = total(residual, residual)
            direction = residual + new / now * direction
            now = new
    mine = jnp.where(row == me, corners(update), 0.0)
    mine = jnp.sum(mine, axis=0, keepdims=True)
    return jnp.broadcast_to(mine, (SUBS, LANES))


def turn_kernel(phi_fine, phi_twin, fine_out, twin_out):
    for lv, phi_ref, out_ref in ((FINE, phi_fine, fine_out), (TWIN, phi_twin, twin_out)):
        s = lv.seg
        nz = EZ * lv.edz
        per = LANES // nz
        tiles = lv.edge // per
        for i in range(s):
            for t in range(tiles):
                parts = []
                for n in range(per):
                    y = lv.mx + t * per + n
                    start = (i * s + y % s) * SUBS + y // s
                    halves = [
                        phi_ref[pl.ds(h * lv.tiles * SUBS + start, lv.edz, stride=2 * lv.tiles * SUBS), :]
                        for h in range(2)
                    ]
                    lower = lane_iota(halves[0].shape) // 16 % 2 == 0
                    parts.append(jnp.where(lower, halves[0], turn(halves[1], 16)))
                    parts.append(jnp.where(lower, turn(halves[0], -16), halves[1]))
                out_ref[i * tiles + t] = jnp.concatenate(parts, axis=0).T


def pressure_kernel(gy_count, me_ref, gathered, fine_turned, twin_turned, fine_out, twin_out, fine_all, twin_all):
    mine = coarse_nodes(gathered[...], gy_count, me_ref[0])
    for n, (lv, turned, out_ref, all_ref) in enumerate(
        ((FINE, fine_turned, fine_out, fine_all), (TWIN, twin_turned, twin_out, twin_all))
    ):
        s = lv.seg
        nz = EZ * lv.edz
        tiles = lv.edge * nz // LANES
        lower = lane_iota() % nz < lv.edz
        scales = {}
        for c in range(COLUMNS):
            for p in range(4):
                at = p * 32 + n * 16 + c * 8
                node = jnp.broadcast_to(mine[:, at : at + 1], (SUBS, LANES))
                scales[2 * p, c] = jnp.where(lower, 1.0, node)
                scales[2 * p + 1, c] = jnp.where(lower, node, 0.0)
        for c in range(COLUMNS):
            for t in range(tiles):
                at = (c * tiles + t) * LANES
                for i in range(s):
                    value = tree(
                        [turned[i * tiles + t, a * 16 + c * 8 : a * 16 + c * 8 + 8, :] * scales[a, c] for a in range(8)]
                    )
                    all_ref[c * tiles + t, pl.ds(i, SUBS, stride=s), :] = value
                out_ref[:, at : at + LANES] = all_ref[c * tiles + t, lv.mx : lv.mx + lv.edge, :]


def vmem(shape, dtype=F32):
    return pltpu.VMEM(shape, dtype)


def shards(permeability):
    nz = EZ * ELZ
    rows = permeability.shape[1]
    lanes = permeability.shape[2]
    assert rows == EL and lanes == COLUMNS * EL * nz
    rim = MX * nz
    gx, gy = lax.axis_size("gx"), lax.axis_size("gy")

    def sent(value, axis, shift):
        count = lax.axis_size(axis)
        return lax.ppermute(value, axis, [(i, (i + shift) % count) for i in range(count)])

    x_low = sent(permeability[:, rows - MX :], "gx", 1)
    x_high = sent(permeability[:, :MX], "gx", -1)

    def strip(part):
        return jnp.concatenate([x_low[:, :, part], permeability[:, :, part], x_high[:, :, part]], axis=1)

    y_low = sent(strip(slice(lanes - rim, lanes)), "gy", 1)
    y_high = sent(strip(slice(0, rim)), "gy", -1)
    halos = [x_low, x_high, y_low, y_high]
    flat_lanes = lanes + 2 * rim
    scratch = [
        vmem((LANES, flat_lanes)),
        vmem((flat_lanes, LANES)),
        vmem((flat_lanes // 2, LANES)),
        vmem((SUBS * (TWIN.seg + 2) * nz, LANES)),
    ]
    for lv in LEVELS:
        scratch.append(vmem((lv.levels + 1, lv.seg, SUBS, 2 * LANES)))
        scratch += [vmem((lv.planes * lv.seg // 2, 2 * SUBS, 2 * LANES), BF16)] * 6
        scratch += [vmem((lv.seg, lv.planes * lv.seg, SUBS, LANES))] * 3
        scratch += [vmem((lv.inner + 1, 2 * lv.tiles, SUBS, LANES))] * 5
        scratch.append(vmem((2 * lv.tiles, SUBS, LANES)))
        scratch += [vmem((lv.tiles, SUBS, LANES))] * 2
    full = pl.BlockSpec(memory_space=pltpu.VMEM)
    phi_shapes = [
        jax.ShapeDtypeStruct((EZ * lv.edz * lv.tiles * SUBS, LANES), F32) for lv in LEVELS
    ]
    phi_fine, phi_twin, message = pl.pallas_call(
        solve_kernel,
        out_shape=phi_shapes + [jax.ShapeDtypeStruct((gx * gy, LANES), F32)],
        in_specs=[full] * 5,
        out_specs=[full] * 3,
        scratch_shapes=scratch,
        compiler_params=pltpu.CompilerParams(vmem_limit_bytes=44 * 1024 * 1024),
        name="solve",
    )(permeability, *halos)
    gathered = lax.all_to_all(message, ("gx", "gy"), 0, 0, tiled=True)
    turned = pl.pallas_call(
        turn_kernel,
        out_shape=[
            jax.ShapeDtypeStruct((lv.seg * lv.edge * EZ * lv.edz // LANES, LANES, LANES), F32) for lv in LEVELS
        ],
        in_specs=[full] * 2,
        out_specs=[full] * 2,
        compiler_params=pltpu.CompilerParams(vmem_limit_bytes=16 * 1024 * 1024),
        cost_estimate=pl.CostEstimate(flops=4000000, bytes_accessed=8000000, transcendentals=0),
        name="turned",
    )(phi_fine, phi_twin)
    me = (lax.axis_index("gx") * gy + lax.axis_index("gy")).astype(jnp.int32).reshape(1)
    return tuple(
        pl.pallas_call(
            functools.partial(pressure_kernel, gy),
            out_shape=[
                jax.ShapeDtypeStruct((lv.edge, COLUMNS * lv.edge * EZ * lv.edz), F32) for lv in LEVELS
            ],
            in_specs=[pl.BlockSpec(memory_space=pltpu.SMEM)] + [full] * 3,
            out_specs=[full] * 2,
            scratch_shapes=[vmem((COLUMNS * lv.edge * EZ * lv.edz // LANES, SUBS * lv.seg, LANES)) for lv in LEVELS],
            compiler_params=pltpu.CompilerParams(vmem_limit_bytes=16 * 1024 * 1024),
            name="pressure",
        )(me, gathered, *turned)
    )


def solution(mesh):
    return jax.shard_map(
        shards,
        mesh=mesh,
        in_specs=(P(None, "gx", "gy"),),
        out_specs=(P("gx", "gy"), P("gx", "gy")),
        check_vma=False,
    )
```

time: 85 us -> 62.9 us (0.74)
  Pallas kernels: 56.5 us -> 32.6 us
  local copies, waits for them, and re-layouts: 6.69 us -> 9.9 us
  waiting for transfers between devices: 11.5 us -> 10 us
    pallas_call x1, Pallas kernels: 53.3 us -> 28.6 us  [shards(): pl.pallas_call(solve_kernel, out_shape=phi_shapes + [jax.ShapeDtypeStruct...]
    unnamed x8 -> x14, local copies, waits for them, and re-layouts: 4.79 us -> 8.01 us
    all_to_all x1, waiting for transfers between devices: 3.55 us -> 2.06 us  [shards(): gathered = lax.all_to_all(message, ('gx', 'gy'), 0, 0, tiled=True)]
  transfers between devices with their start and end apart: 5 -> 5, of which waited for: 5 -> 5; matrix products, arithmetic and copies ran while one was open for 1% -> 1% of each run, Pallas kernels for 1% -> 3%
where the time goes in v2:
time: 62.9 us; the launch traced here: 62.6 us
  Pallas kernels  32.6 us (52%)
  waiting for transfers between devices  10 us (16%)
  local copies, waits for them, and re-layouts  9.9 us (16%)
  starting transfers between devices  9.27 us (15%)
  between operations  0.69 us (1%)
    pallas_call x1, Pallas kernels, shards(): pl.pallas_call(solve_kernel, out_shape=phi_shapes + [jax.ShapeDtypeStruct...  28.6 us
    unnamed x14, local copies, waits for them, and re-layouts  8.01 us
    ppermute x4, waiting for transfers between devices, sent(): lax.ppermute(value, axis, [(i, (i + shift) % count) for i in range(count)])  7.97 us
    ppermute x4, starting transfers between devices, sent(): lax.ppermute(value, axis, [(i, (i + shift) % count) for i in range(count)])  6.73 us
    all_to_all x1, starting transfers between devices, shards(): gathered = lax.all_to_all(message, ('gx', 'gy'), 0, 0, tiled=True)  2.54 us
    pallas_call x1, Pallas kernels, shards(): pl.pallas_call(functools.partial(pressure_kernel, gy), out_shape=[jax.Sha...  2.38 us
    all_to_all x1, waiting for transfers between devices, shards(): gathered = lax.all_to_all(message, ('gx', 'gy'), 0, 0, tiled=True)  2.06 us
    pallas_call x1, Pallas kernels, shards(): pl.pallas_call(turn_kernel, out_shape=[jax.ShapeDtypeStruct((lv.seg * lv....  1.67 us
  transfers between devices with their start and end apart: 5, of which 5 were waited for; matrix products, arithmetic and copies ran while one was open for 1% of the time, Pallas kernels for 3%

profile of v2, /device:TPU:0, one launch (start us, length us, event | category | flops | bytes accessed | tf_op | source)
XLA Modules:
  0.0 62.6 jit_solution(18435522121397303096)
XLA Ops:
  0.6 1.1 %fusion.1 = (f32[3,4,2048]{2,1,0:T(4,128)S(1)}, f32[3,4,2048]{2,1,0:T(4,128)S(1)}) fusion(f32[3,32,2048]{2,1,0:T(8,128)} %center.1), kind=kLoop, calls=%fused_computation.3 | loop fusion | bytes 393216 | tf_op jit(solution)/shard_map/slice | solution.py:662
  1.7 3.1 %collective-permute-start = (f32[3,4,2048]{2,1,0:T(4,128)S(1)}, f32[3,4,2048]{2,1,0:T(4,128)S(1)}, u32[]{:S(2)}, u32[]{:S(2)}) collective-permute-start(f32[3,4,2048]{2,1,0:T(4,128)S(1)} %get-tuple-element.15), channel_id=1, source_target_pairs={{0,8},{8,16},{16,24},{24,0},{1,9},{9,17},{17,25},{25,1},{2,10},{10... | collective-permute-start | bytes 294920 | tf_op jit(solution)/shard_map/ppermute | solution.py:659
  4.8 2.1 %collective-permute-start.1 = (f32[3,4,2048]{2,1,0:T(4,128)S(1)}, f32[3,4,2048]{2,1,0:T(4,128)S(1)}, u32[]{:S(2)}, u32[]{:S(2)}) collective-permute-start(f32[3,4,2048]{2,1,0:T(4,128)S(1)} %get-tuple-element.14), channel_id=1, source_target_pairs={{0,24},{8,0},{16,8},{24,16},{1,25},{9,1},{17,9},{25,17},{2,26},{10... | collective-permute-start | bytes 294920 | tf_op jit(solution)/shard_map/ppermute | solution.py:659
  6.9 0.8 %fusion = (f32[3,32,128]{2,1,0:T(8,128)S(1)}, f32[3,32,128]{2,1,0:T(8,128)S(1)}) fusion(f32[3,32,2048]{2,1,0:T(8,128)} %center.1), kind=kLoop, calls=%fused_computation.2 | loop fusion | bytes 196608 | tf_op jit(solution)/shard_map/slice | solution.py:665
  7.7 2.6 %collective-permute-done.x_low = f32[3,4,2048]{2,1,0:T(4,128)S(1)} collective-permute-done((f32[3,4,2048]{2,1,0:T(4,128)S(1)}, f32[3,4,2048]{2,1,0:T(4,128)S(1)}, u32[]{:S(2)}, u32[]{:S(2)}) %collective-permute-start) | collective-permute-done | bytes 98336 | tf_op jit(solution)/shard_map/ppermute | solution.py:659
  10.3 0.8 %collective-permute-done.1.x_high = f32[3,4,2048]{2,1,0:T(4,128)S(1)} collective-permute-done((f32[3,4,2048]{2,1,0:T(4,128)S(1)}, f32[3,4,2048]{2,1,0:T(4,128)S(1)}, u32[]{:S(2)}, u32[]{:S(2)}) %collective-permute-start.1) | collective-permute-done | bytes 98336 | tf_op jit(solution)/shard_map/ppermute | solution.py:659
  11.1 1.5 %collective-permute-start.3 = (f32[3,40,128]{2,1,0:T(8,128)S(1)}, f32[3,40,128]{2,1,0:T(8,128)S(1)}, u32[]{:S(2)}, u32[]{:S(2)}) collective-permute-start(f32[3,40,128]{2,1,0:T(8,128)S(1)} %pad_maximum_fusion.1), channel_id=1, source_target_pairs={{0,7},{1,0},{2,1},{3,2},{4,3},{5,4},{6,5},{7,6},{8,15},{9,8},{10,9... | collective-permute-start | bytes 184328 | tf_op jit(solution)/shard_map/ppermute | solution.py:659
  12.7 0.1 collective-permute-start.2
  12.7 1.9 %collective-permute-done.3.y_high = f32[3,40,128]{2,1,0:T(8,128)S(1)} collective-permute-done((f32[3,40,128]{2,1,0:T(8,128)S(1)}, f32[3,40,128]{2,1,0:T(8,128)S(1)}, u32[]{:S(2)}, u32[]{:S(2)}) %collective-permute-start.3) | collective-permute-done | bytes 61472 | tf_op jit(solution)/shard_map/ppermute | solution.py:659
  14.6 2.7 %collective-permute-done.2.y_low = f32[3,40,128]{2,1,0:T(8,128)S(1)} collective-permute-done((f32[3,40,128]{2,1,0:T(8,128)S(1)}, f32[3,40,128]{2,1,0:T(8,128)S(1)}, u32[]{:S(2)}, u32[]{:S(2)}) %collective-permute-start.2) | collective-permute-done | bytes 61472 | tf_op jit(solution)/shard_map/ppermute | solution.py:659
  17.3 0.0 copy-start.2
  17.3 1.1 %copy-done.2 = f32[3,32,2048]{2,1,0:T(8,128)S(1)} copy-done((f32[3,32,2048]{2,1,0:T(8,128)S(1)}, f32[3,32,2048]{2,1,0:T(8,128)}, u32[]{:S(2)}) %copy-start.2) | copy-done | bytes 786456
  18.4 28.6 %solve.1 = (f32[6400,128]{1,0:T(8,128)S(1)}, f32[1152,128]{1,0:T(8,128)S(1)}, f32[32,128]{1,0:T(8,128)}) custom-call(f32[3,32,2048]{2,1,0:T(8,128)S(1)} %copy-done.2, f32[3,4,2048]{2,1,0:T(4,128)S(1)} %collective-permute-done.x_low, f32[3,4,2048]{2,1,0:T(4,128)S(1)} %collective-permute-done.1.x_high, f32[3,40,128]{2,1,0:T(8,128)S(1)} %collective-permute-done.2.y_low, ...), custom_call_target="tpu_custom_call" | custom-call | tf_op jit(solution)/shard_map/solve/pallas_call | solution.py:688
  47.0 0.0 copy-start.3
  47.0 0.8 %copy-done.3 = f32[1152,128]{1,0:T(8,128)} copy-done((f32[1152,128]{1,0:T(8,128)}, f32[1152,128]{1,0:T(8,128)S(1)}, u32[]{:S(2)}) %copy-start.3) | copy-done | bytes 589848
  47.8 2.5 %all-to-all-start = ((f32[32,1,128]{2,1,0:T(1,128)}), f32[32,1,128]{2,1,0:T(1,128)S(1)}, u32[]{:S(2)}, u32[]{:S(2)}) async-start(f32[32,1,128]{2,1,0:T(1,128)} %bitcast.2), calls=%async_computation | async-start | bytes 32768 | tf_op jit(solution)/shard_map/all_to_all | solution.py:697
  50.4 0.0 copy-start.4
  50.4 1.1 %copy-done.4 = f32[1152,128]{1,0:T(8,128)S(1)} copy-done((f32[1152,128]{1,0:T(8,128)S(1)}, f32[1152,128]{1,0:T(8,128)}, u32[]{:S(2)}) %copy-start.4) | copy-done | bytes 589848
  51.4 1.7 %turned.1 = (f32[40,128,128]{2,1,0:T(8,128)S(1)}, f32[6,128,128]{2,1,0:T(8,128)S(1)}) custom-call(f32[6400,128]{1,0:T(8,128)S(1)} %get-tuple-element.8.phi_fine, f32[1152,128]{1,0:T(8,128)S(1)} %copy-done.4), custom_call_target="tpu_custom_call" | custom-call | flops 4000000 | bytes 8000000 | tf_op jit(solution)/shard_map/turned/pallas_call | solution.py:698
  53.1 0.0 copy-start
  53.1 1.5 %copy-done = f32[40,128,128]{2,1,0:T(8,128)} copy-done((f32[40,128,128]{2,1,0:T(8,128)}, f32[40,128,128]{2,1,0:T(8,128)S(1)}, u32[]{:S(2)}) %copy-start) | copy-done | bytes 2621464
  54.6 0.0 copy-start.5
  54.6 0.8 %copy-done.5 = f32[6,128,128]{2,1,0:T(8,128)} copy-done((f32[6,128,128]{2,1,0:T(8,128)}, f32[6,128,128]{2,1,0:T(8,128)S(1)}, u32[]{:S(2)}) %copy-start.5) | copy-done | bytes 393240
  55.4 2.1 %all-to-all-done = f32[32,1,128]{2,1,0:T(1,128)S(1)} async-done(((f32[32,1,128]{2,1,0:T(1,128)}), f32[32,1,128]{2,1,0:T(1,128)S(1)}, u32[]{:S(2)}, u32[]{:S(2)}) %all-to-all-start) | async-done | bytes 16416 | tf_op jit(solution)/shard_map/all_to_all | solution.py:697
  57.4 0.0 copy-start.1
  57.4 1.7 %copy-done.1 = f32[40,128,128]{2,1,0:T(8,128)S(1)} copy-done((f32[40,128,128]{2,1,0:T(8,128)S(1)}, f32[40,128,128]{2,1,0:T(8,128)}, u32[]{:S(2)}) %copy-start.1) | copy-done | bytes 2621464
  59.2 0.0 copy-start.6
  59.2 1.0 %copy-done.6 = f32[6,128,128]{2,1,0:T(8,128)S(1)} copy-done((f32[6,128,128]{2,1,0:T(8,128)S(1)}, f32[6,128,128]{2,1,0:T(8,128)}, u32[]{:S(2)}) %copy-start.6) | copy-done | bytes 393240
  60.2 2.4 %pressure.1 = (f32[32,2048]{1,0:T(8,128)}, f32[16,512]{1,0:T(8,128)}) custom-call(s32[1]{0:T(128)} %bitcast.me_ref, f32[32,128]{1,0:T(8,128)S(1)} %bitcast.5, f32[40,128,128]{2,1,0:T(8,128)S(1)} %copy-done.1, f32[6,128,128]{2,1,0:T(8,128)S(1)} %copy-done.6), custom_call_target="tpu_custom_call" | custom-call | tf_op jit(solution)/shard_map/pressure/pallas_call | solution.py:711
  (4 shorter events, 0.0 us)
Async XLA Ops:
  1.7 8.6 %collective-permute-start = (f32[3,4,2048]{2,1,0:T(4,128)S(1)}, f32[3,4,2048]{2,1,0:T(4,128)S(1)}, u32[]{:S(2)}, u32[]{:S(2)}) collective-permute-start(f32[3,4,2048]{2,1,0:T(4,128)S(1)} %get-tuple-element.15), channel_id=1, source_target_pairs={{0,8},{8,16},{16,24},{24,0},{1,9},{9,17},{17,25},{25,1},{2,10},{10... | collective-permute-start | bytes 294920 | tf_op jit(solution)/shard_map/ppermute | solution.py:659
  4.8 6.4 %collective-permute-start.1 = (f32[3,4,2048]{2,1,0:T(4,128)S(1)}, f32[3,4,2048]{2,1,0:T(4,128)S(1)}, u32[]{:S(2)}, u32[]{:S(2)}) collective-permute-start(f32[3,4,2048]{2,1,0:T(4,128)S(1)} %get-tuple-element.14), channel_id=1, source_target_pairs={{0,24},{8,0},{16,8},{24,16},{1,25},{9,1},{17,9},{25,17},{2,26},{10... | collective-permute-start | bytes 294920 | tf_op jit(solution)/shard_map/ppermute | solution.py:659
  11.1 3.5 %collective-permute-start.3 = (f32[3,40,128]{2,1,0:T(8,128)S(1)}, f32[3,40,128]{2,1,0:T(8,128)S(1)}, u32[]{:S(2)}, u32[]{:S(2)}) collective-permute-start(f32[3,40,128]{2,1,0:T(8,128)S(1)} %pad_maximum_fusion.1), channel_id=1, source_target_pairs={{0,7},{1,0},{2,1},{3,2},{4,3},{5,4},{6,5},{7,6},{8,15},{9,8},{10,9... | collective-permute-start | bytes 184328 | tf_op jit(solution)/shard_map/ppermute | solution.py:659
  12.7 4.6 %collective-permute-start.2 = (f32[3,40,128]{2,1,0:T(8,128)S(1)}, f32[3,40,128]{2,1,0:T(8,128)S(1)}, u32[]{:S(2)}, u32[]{:S(2)}) collective-permute-start(f32[3,40,128]{2,1,0:T(8,128)S(1)} %pad_maximum_fusion), channel_id=1, source_target_pairs={{0,1},{1,2},{2,3},{3,4},{4,5},{5,6},{6,7},{7,0},{8,9},{9,10},{10,1... | collective-permute-start | bytes 184328 | tf_op jit(solution)/shard_map/ppermute | solution.py:659
  17.3 1.1 %copy-start.2 = (f32[3,32,2048]{2,1,0:T(8,128)S(1)}, f32[3,32,2048]{2,1,0:T(8,128)}, u32[]{:S(2)}) copy-start(f32[3,32,2048]{2,1,0:T(8,128)} %center.1) | copy-start | bytes 2359300
  47.0 0.8 %copy-start.3 = (f32[1152,128]{1,0:T(8,128)}, f32[1152,128]{1,0:T(8,128)S(1)}, u32[]{:S(2)}) copy-start(f32[1152,128]{1,0:T(8,128)S(1)} %get-tuple-element.9.phi_twin) | copy-start | bytes 1769476
  47.8 9.6 %all-to-all-start = ((f32[32,1,128]{2,1,0:T(1,128)}), f32[32,1,128]{2,1,0:T(1,128)S(1)}, u32[]{:S(2)}, u32[]{:S(2)}) async-start(f32[32,1,128]{2,1,0:T(1,128)} %bitcast.2), calls=%async_computation | async-start | bytes 32768 | tf_op jit(solution)/shard_map/all_to_all | solution.py:697
  50.4 1.1 %copy-start.4 = (f32[1152,128]{1,0:T(8,128)S(1)}, f32[1152,128]{1,0:T(8,128)}, u32[]{:S(2)}) copy-start(f32[1152,128]{1,0:T(8,128)} %copy-done.3) | copy-start | bytes 1769476
  53.1 1.5 %copy-start = (f32[40,128,128]{2,1,0:T(8,128)}, f32[40,128,128]{2,1,0:T(8,128)S(1)}, u32[]{:S(2)}) copy-start(f32[40,128,128]{2,1,0:T(8,128)S(1)} %get-tuple-element.10.fine_turned) | copy-start | bytes 7864324
  54.6 0.8 %copy-start.5 = (f32[6,128,128]{2,1,0:T(8,128)}, f32[6,128,128]{2,1,0:T(8,128)S(1)}, u32[]{:S(2)}) copy-start(f32[6,128,128]{2,1,0:T(8,128)S(1)} %get-tuple-element.11.twin_turned) | copy-start | bytes 1179652
  57.4 1.7 %copy-start.1 = (f32[40,128,128]{2,1,0:T(8,128)S(1)}, f32[40,128,128]{2,1,0:T(8,128)}, u32[]{:S(2)}) copy-start(f32[40,128,128]{2,1,0:T(8,128)} %copy-done) | copy-start | bytes 7864324
  59.2 1.0 %copy-start.6 = (f32[6,128,128]{2,1,0:T(8,128)S(1)}, f32[6,128,128]{2,1,0:T(8,128)}, u32[]{:S(2)}) copy-start(f32[6,128,128]{2,1,0:T(8,128)} %copy-done.5) | copy-start | bytes 1179652

commit v3 on v2

--- a/solution.py
+++ b/solution.py
@@ -211,6 +211,14 @@
 
 
 HALVES = (0, 1)
+
+
+def phi_rows(lv):
+    return EZ * lv.edz * lv.tiles * SUBS
+
+
+def turned_tiles(lv):
+    return lv.edge * EZ * lv.edz // LANES
 
 
 def looped(count, group, sums, step):
@@ -425,12 +433,12 @@
     return looped(lv.edz, group, 4, step)
 
 
-GROUPS = {FINE: 1, TWIN: 4}
+GROUPS = {FINE: 2, TWIN: 8}
 
 
 def solve_kernel(
     center, x_low, x_high, y_low, y_high,
-    phi_fine, phi_twin, message,
+    phi, message,
     flat, rows, pairs, twin_rows, *refs,
 ):
     lanes = center.shape[2]
@@ -506,7 +514,8 @@
             betas = [[a / b for a, b in zip(new[n], rr[n])] for n in range(len(LEVELS))]
             rr = new
 
-    phis = (phi_fine, phi_twin)
+    split = phi.shape[0] - phi_rows(TWIN)
+    phis = (phi.at[pl.ds(0, split)], phi.at[pl.ds(split, phi_rows(TWIN))])
     totals = both_levels(lambda n, case, group: finish(case, group, alphas[n], phis[n]))
     _, element, _, slot = lane_parts()
     packed = []
@@ -593,36 +602,50 @@
     return jnp.broadcast_to(mine, (SUBS, LANES))
 
 
-def turn_kernel(phi_fine, phi_twin, fine_out, twin_out):
-    for lv, phi_ref, out_ref in ((FINE, phi_fine, fine_out), (TWIN, phi_twin, twin_out)):
+def turn_kernel(phi, out_ref, work, sem):
+    start_row, number = 0, 0
+    copies = []
+    for lv in LEVELS:
         s = lv.seg
         nz = EZ * lv.edz
         per = LANES // nz
-        tiles = lv.edge // per
         for i in range(s):
-            for t in range(tiles):
+            for t in range(turned_tiles(lv)):
                 parts = []
                 for n in range(per):
                     y = lv.mx + t * per + n
-                    start = (i * s + y % s) * SUBS + y // s
+                    start = start_row + (i * s + y % s) * SUBS + y // s
                     halves = [
-                        phi_ref[pl.ds(h * lv.tiles * SUBS + start, lv.edz, stride=2 * lv.tiles * SUBS), :]
+                        phi[pl.ds(h * lv.tiles * SUBS + start, lv.edz, stride=2 * lv.tiles * SUBS), :]
                         for h in range(2)
                     ]
                     lower = lane_iota(halves[0].shape) // 16 % 2 == 0
                     parts.append(jnp.where(lower, halves[0], turn(halves[1], 16)))
                     parts.append(jnp.where(lower, turn(halves[0], -16), halves[1]))
-                out_ref[i * tiles + t] = jnp.concatenate(parts, axis=0).T
-
-
-def pressure_kernel(gy_count, me_ref, gathered, fine_turned, twin_turned, fine_out, twin_out, fine_all, twin_all):
+                work[number] = jnp.concatenate(parts, axis=0).T
+                number += 1
+            done = number - turned_tiles(lv)
+            copies.append(
+                pltpu.make_async_copy(
+                    work.at[pl.ds(done, turned_tiles(lv))], out_ref.at[pl.ds(done, turned_tiles(lv))], sem.at[len(copies)]
+                )
+            )
+            copies[-1].start()
+        start_row += phi_rows(lv)
+    for copy in copies:
+        copy.wait()
+
+
+def pressure_kernel(gy_count, me_ref, gathered, source, fine_out, twin_out, turned, fine_all, twin_all, sem):
+    fetch = pltpu.make_async_copy(source, turned, sem)
+    fetch.start()
     mine = coarse_nodes(gathered[...], gy_count, me_ref[0])
-    for n, (lv, turned, out_ref, all_ref) in enumerate(
-        ((FINE, fine_turned, fine_out, fine_all), (TWIN, twin_turned, twin_out, twin_all))
-    ):
+    fetch.wait()
+    first = 0
+    for n, (lv, out_ref, all_ref) in enumerate(((FINE, fine_out, fine_all), (TWIN, twin_out, twin_all))):
         s = lv.seg
         nz = EZ * lv.edz
-        tiles = lv.edge * nz // LANES
+        tiles = turned_tiles(lv)
         lower = lane_iota() % nz < lv.edz
         scales = {}
         for c in range(COLUMNS):
@@ -636,10 +659,11 @@
                 at = (c * tiles + t) * LANES
                 for i in range(s):
                     value = tree(
-                        [turned[i * tiles + t, a * 16 + c * 8 : a * 16 + c * 8 + 8, :] * scales[a, c] for a in range(8)]
+                        [turned[first + i * tiles + t, a * 16 + c * 8 : a * 16 + c * 8 + 8, :] * scales[a, c] for a in range(8)]
                     )
                     all_ref[c * tiles + t, pl.ds(i, SUBS, stride=s), :] = value
                 out_ref[:, at : at + LANES] = all_ref[c * tiles + t, lv.mx : lv.mx + lv.edge, :]
+        first += s * tiles
 
 
 def vmem(shape, dtype=F32):
@@ -682,30 +706,33 @@
         scratch.append(vmem((2 * lv.tiles, SUBS, LANES)))
         scratch += [vmem((lv.tiles, SUBS, LANES))] * 2
     full = pl.BlockSpec(memory_space=pltpu.VMEM)
-    phi_shapes = [
-        jax.ShapeDtypeStruct((EZ * lv.edz * lv.tiles * SUBS, LANES), F32) for lv in LEVELS
-    ]
-    phi_fine, phi_twin, message = pl.pallas_call(
+    phi, message = pl.pallas_call(
         solve_kernel,
-        out_shape=phi_shapes + [jax.ShapeDtypeStruct((gx * gy, LANES), F32)],
+        out_shape=[
+            jax.ShapeDtypeStruct((sum(phi_rows(lv) for lv in LEVELS), LANES), F32),
+            jax.ShapeDtypeStruct((gx * gy, LANES), F32),
+        ],
         in_specs=[full] * 5,
-        out_specs=[full] * 3,
+        out_specs=[full] * 2,
         scratch_shapes=scratch,
         compiler_params=pltpu.CompilerParams(vmem_limit_bytes=44 * 1024 * 1024),
         name="solve",
     )(permeability, *halos)
     gathered = lax.all_to_all(message, ("gx", "gy"), 0, 0, tiled=True)
+    tiles = sum(lv.seg * turned_tiles(lv) for lv in LEVELS)
     turned = pl.pallas_call(
         turn_kernel,
-        out_shape=[
-            jax.ShapeDtypeStruct((lv.seg * lv.edge * EZ * lv.edz // LANES, LANES, LANES), F32) for lv in LEVELS
+        out_shape=jax.ShapeDtypeStruct((tiles, LANES, LANES), F32),
+        in_specs=[full],
+        out_specs=pl.BlockSpec(memory_space=pltpu.HBM),
+        scratch_shapes=[
+            vmem((tiles, LANES, LANES)),
+            pltpu.SemaphoreType.DMA((sum(lv.seg for lv in LEVELS),)),
         ],
-        in_specs=[full] * 2,
-        out_specs=[full] * 2,
         compiler_params=pltpu.CompilerParams(vmem_limit_bytes=16 * 1024 * 1024),
         cost_estimate=pl.CostEstimate(flops=4000000, bytes_accessed=8000000, transcendentals=0),
         name="turned",
-    )(phi_fine, phi_twin)
+    )(phi)
     me = (lax.axis_index("gx") * gy + lax.axis_index("gy")).astype(jnp.int32).reshape(1)
     return tuple(
         pl.pallas_call(
@@ -713,12 +740,14 @@
             out_shape=[
                 jax.ShapeDtypeStruct((lv.edge, COLUMNS * lv.edge * EZ * lv.edz), F32) for lv in LEVELS
             ],
-            in_specs=[pl.BlockSpec(memory_space=pltpu.SMEM)] + [full] * 3,
+            in_specs=[pl.BlockSpec(memory_space=pltpu.SMEM), full, pl.BlockSpec(memory_space=pltpu.HBM)],
             out_specs=[full] * 2,
-            scratch_shapes=[vmem((COLUMNS * lv.edge * EZ * lv.edz // LANES, SUBS * lv.seg, LANES)) for lv in LEVELS],
+            scratch_shapes=[vmem((tiles, LANES, LANES))]
+            + [vmem((COLUMNS * turned_tiles(lv), SUBS * lv.seg, LANES)) for lv in LEVELS]
+            + [pltpu.SemaphoreType.DMA],
             compiler_params=pltpu.CompilerParams(vmem_limit_bytes=16 * 1024 * 1024),
             name="pressure",
-        )(me, gathered, *turned)
+        )(me, gathered, turned)
     )
 
 

time: 62.9 us -> 63.3 us (level)
  Pallas kernels: 32.6 us -> 36.1 us
  local copies, waits for them, and re-layouts: 9.9 us -> 6.95 us
    pallas_call x2, Pallas kernels: 30.3 us -> 33.4 us  [the longest x1 30.2 us: shards(): pl.pallas_call(solve_kernel, out_shape=[jax.ShapeDtypeStruct((sum((phi_ro...]
    unnamed x14 -> x6, local copies, waits for them, and re-layouts: 8.01 us -> 5.06 us
  transfers between devices with their start and end apart: 5 -> 5, of which waited for: 5 -> 5; matrix products, arithmetic and copies ran while one was open for 1% -> 1% of each run, Pallas kernels for 3% -> 5%
where the time goes in v3:
time: 63.3 us; the launch traced here: 63 us
  Pallas kernels  36.1 us (57%)
  waiting for transfers between devices  9.56 us (15%)
  starting transfers between devices  9.45 us (15%)
  local copies, waits for them, and re-layouts  6.95 us (11%)
  between operations  0.84 us (1%)
    pallas_call x1, Pallas kernels, shards(): pl.pallas_call(solve_kernel, out_shape=[jax.ShapeDtypeStruct((sum((phi_ro...  30.2 us
    ppermute x4, waiting for transfers between devices, sent(): lax.ppermute(value, axis, [(i, (i + shift) % count) for i in range(count)])  7.97 us
    ppermute x4, starting transfers between devices, sent(): lax.ppermute(value, axis, [(i, (i + shift) % count) for i in range(count)])  6.73 us
    unnamed x6, local copies, waits for them, and re-layouts  5.06 us
    pallas_call x1, Pallas kernels, shards(): pl.pallas_call(turn_kernel, out_shape=jax.ShapeDtypeStruct((tiles, LANES,...  3.19 us
    pallas_call x1, Pallas kernels, shards(): pl.pallas_call(functools.partial(pressure_kernel, gy), out_shape=[jax.Sha...  2.77 us
    all_to_all x1, starting transfers between devices, shards(): gathered = lax.all_to_all(message, ('gx', 'gy'), 0, 0, tiled=True)  2.72 us
    all_to_all x1, waiting for transfers between devices, shards(): gathered = lax.all_to_all(message, ('gx', 'gy'), 0, 0, tiled=True)  1.6 us
  transfers between devices with their start and end apart: 5, of which 5 were waited for; matrix products, arithmetic and copies ran while one was open for 1% of the time, Pallas kernels for 5%

profile of v3, /device:TPU:0, one launch (start us, length us, event | category | flops | bytes accessed | tf_op | source)
XLA Modules:
  0.0 63.0 jit_solution(10203561192796961103)
XLA Ops:
  0.6 1.1 %fusion.1 = (f32[3,4,2048]{2,1,0:T(4,128)S(1)}, f32[3,4,2048]{2,1,0:T(4,128)S(1)}) fusion(f32[3,32,2048]{2,1,0:T(8,128)} %center.1), kind=kLoop, calls=%fused_computation.3 | loop fusion | bytes 393216 | tf_op jit(solution)/shard_map/slice | solution.py:686
  1.7 3.1 %collective-permute-start = (f32[3,4,2048]{2,1,0:T(4,128)S(1)}, f32[3,4,2048]{2,1,0:T(4,128)S(1)}, u32[]{:S(2)}, u32[]{:S(2)}) collective-permute-start(f32[3,4,2048]{2,1,0:T(4,128)S(1)} %get-tuple-element.9), channel_id=1, source_target_pairs={{0,8},{8,16},{16,24},{24,0},{1,9},{9,17},{17,25},{25,1},{2,10},{10... | collective-permute-start | bytes 294920 | tf_op jit(solution)/shard_map/ppermute | solution.py:683
  4.8 2.1 %collective-permute-start.1 = (f32[3,4,2048]{2,1,0:T(4,128)S(1)}, f32[3,4,2048]{2,1,0:T(4,128)S(1)}, u32[]{:S(2)}, u32[]{:S(2)}) collective-permute-start(f32[3,4,2048]{2,1,0:T(4,128)S(1)} %get-tuple-element.8), channel_id=1, source_target_pairs={{0,24},{8,0},{16,8},{24,16},{1,25},{9,1},{17,9},{25,17},{2,26},{10... | collective-permute-start | bytes 294920 | tf_op jit(solution)/shard_map/ppermute | solution.py:683
  6.9 0.8 %fusion = (f32[3,32,128]{2,1,0:T(8,128)S(1)}, f32[3,32,128]{2,1,0:T(8,128)S(1)}) fusion(f32[3,32,2048]{2,1,0:T(8,128)} %center.1), kind=kLoop, calls=%fused_computation.2 | loop fusion | bytes 196608 | tf_op jit(solution)/shard_map/slice | solution.py:689
  7.7 2.6 %collective-permute-done.x_low = f32[3,4,2048]{2,1,0:T(4,128)S(1)} collective-permute-done((f32[3,4,2048]{2,1,0:T(4,128)S(1)}, f32[3,4,2048]{2,1,0:T(4,128)S(1)}, u32[]{:S(2)}, u32[]{:S(2)}) %collective-permute-start) | collective-permute-done | bytes 98336 | tf_op jit(solution)/shard_map/ppermute | solution.py:683
  10.3 0.8 %collective-permute-done.1.x_high = f32[3,4,2048]{2,1,0:T(4,128)S(1)} collective-permute-done((f32[3,4,2048]{2,1,0:T(4,128)S(1)}, f32[3,4,2048]{2,1,0:T(4,128)S(1)}, u32[]{:S(2)}, u32[]{:S(2)}) %collective-permute-start.1) | collective-permute-done | bytes 98336 | tf_op jit(solution)/shard_map/ppermute | solution.py:683
  11.1 1.5 %collective-permute-start.3 = (f32[3,40,128]{2,1,0:T(8,128)S(1)}, f32[3,40,128]{2,1,0:T(8,128)S(1)}, u32[]{:S(2)}, u32[]{:S(2)}) collective-permute-start(f32[3,40,128]{2,1,0:T(8,128)S(1)} %pad_maximum_fusion.1), channel_id=1, source_target_pairs={{0,7},{1,0},{2,1},{3,2},{4,3},{5,4},{6,5},{7,6},{8,15},{9,8},{10,9... | collective-permute-start | bytes 184328 | tf_op jit(solution)/shard_map/ppermute | solution.py:683
  12.7 0.1 collective-permute-start.2
  12.7 1.9 %collective-permute-done.3.y_high = f32[3,40,128]{2,1,0:T(8,128)S(1)} collective-permute-done((f32[3,40,128]{2,1,0:T(8,128)S(1)}, f32[3,40,128]{2,1,0:T(8,128)S(1)}, u32[]{:S(2)}, u32[]{:S(2)}) %collective-permute-start.3) | collective-permute-done | bytes 61472 | tf_op jit(solution)/shard_map/ppermute | solution.py:683
  14.6 2.7 %collective-permute-done.2.y_low = f32[3,40,128]{2,1,0:T(8,128)S(1)} collective-permute-done((f32[3,40,128]{2,1,0:T(8,128)S(1)}, f32[3,40,128]{2,1,0:T(8,128)S(1)}, u32[]{:S(2)}, u32[]{:S(2)}) %collective-permute-start.2) | collective-permute-done | bytes 61472 | tf_op jit(solution)/shard_map/ppermute | solution.py:683
  17.3 0.0 copy-start.2
  17.3 1.1 %copy-done.2 = f32[3,32,2048]{2,1,0:T(8,128)S(1)} copy-done((f32[3,32,2048]{2,1,0:T(8,128)S(1)}, f32[3,32,2048]{2,1,0:T(8,128)}, u32[]{:S(2)}) %copy-start.2) | copy-done | bytes 786456
  18.4 30.2 %solve.1 = (f32[7552,128]{1,0:T(8,128)S(1)}, f32[32,128]{1,0:T(8,128)}) custom-call(f32[3,32,2048]{2,1,0:T(8,128)S(1)} %copy-done.2, f32[3,4,2048]{2,1,0:T(4,128)S(1)} %collective-permute-done.x_low, f32[3,4,2048]{2,1,0:T(4,128)S(1)} %collective-permute-done.1.x_high, f32[3,40,128]{2,1,0:T(8,128)S(1)} %collective-permute-done.2.y_low, ...), custom_call_target="tpu_custom_call" | custom-call | tf_op jit(solution)/shard_map/solve/pallas_call | solution.py:709
  48.6 0.0 copy-start
  48.6 1.8 %copy-done = f32[7552,128]{1,0:T(8,128)} copy-done((f32[7552,128]{1,0:T(8,128)}, f32[7552,128]{1,0:T(8,128)S(1)}, u32[]{:S(2)}) %copy-start) | copy-done | bytes 3866648
  50.4 2.7 %all-to-all-start = ((f32[32,1,128]{2,1,0:T(1,128)}), f32[32,1,128]{2,1,0:T(1,128)S(1)}, u32[]{:S(2)}, u32[]{:S(2)}) async-start(f32[32,1,128]{2,1,0:T(1,128)} %bitcast.2), calls=%async_computation | async-start | bytes 32768 | tf_op jit(solution)/shard_map/all_to_all | solution.py:721
  53.1 0.0 copy-start.1
  53.1 2.1 %copy-done.1 = f32[7552,128]{1,0:T(8,128)S(1)} copy-done((f32[7552,128]{1,0:T(8,128)S(1)}, f32[7552,128]{1,0:T(8,128)}, u32[]{:S(2)}) %copy-start.1) | copy-done | bytes 3866648
  55.2 3.2 %turned.1.source = f32[46,128,128]{2,1,0:T(8,128)S(1)} custom-call(f32[7552,128]{1,0:T(8,128)S(1)} %copy-done.1), custom_call_target="tpu_custom_call" | custom-call | flops 4000000 | bytes 8000000 | tf_op jit(solution)/shard_map/turned/pallas_call | solution.py:723
  58.4 1.6 %all-to-all-done = f32[32,1,128]{2,1,0:T(1,128)S(1)} async-done(((f32[32,1,128]{2,1,0:T(1,128)}), f32[32,1,128]{2,1,0:T(1,128)S(1)}, u32[]{:S(2)}, u32[]{:S(2)}) %all-to-all-start) | async-done | bytes 16416 | tf_op jit(solution)/shard_map/all_to_all | solution.py:721
  60.0 2.8 %pressure.1 = (f32[32,2048]{1,0:T(8,128)}, f32[16,512]{1,0:T(8,128)}) custom-call(s32[1]{0:T(128)} %bitcast.me_ref, f32[32,128]{1,0:T(8,128)S(1)} %bitcast.5, f32[46,128,128]{2,1,0:T(8,128)S(1)} %turned.1.source), custom_call_target="tpu_custom_call" | custom-call | tf_op jit(solution)/shard_map/pressure/pallas_call | solution.py:738
  (4 shorter events, 0.0 us)
Async XLA Ops:
  1.7 8.6 %collective-permute-start = (f32[3,4,2048]{2,1,0:T(4,128)S(1)}, f32[3,4,2048]{2,1,0:T(4,128)S(1)}, u32[]{:S(2)}, u32[]{:S(2)}) collective-permute-start(f32[3,4,2048]{2,1,0:T(4,128)S(1)} %get-tuple-element.9), channel_id=1, source_target_pairs={{0,8},{8,16},{16,24},{24,0},{1,9},{9,17},{17,25},{25,1},{2,10},{10... | collective-permute-start | bytes 294920 | tf_op jit(solution)/shard_map/ppermute | solution.py:683
  4.8 6.4 %collective-permute-start.1 = (f32[3,4,2048]{2,1,0:T(4,128)S(1)}, f32[3,4,2048]{2,1,0:T(4,128)S(1)}, u32[]{:S(2)}, u32[]{:S(2)}) collective-permute-start(f32[3,4,2048]{2,1,0:T(4,128)S(1)} %get-tuple-element.8), channel_id=1, source_target_pairs={{0,24},{8,0},{16,8},{24,16},{1,25},{9,1},{17,9},{25,17},{2,26},{10... | collective-permute-start | bytes 294920 | tf_op jit(solution)/shard_map/ppermute | solution.py:683
  11.1 3.5 %collective-permute-start.3 = (f32[3,40,128]{2,1,0:T(8,128)S(1)}, f32[3,40,128]{2,1,0:T(8,128)S(1)}, u32[]{:S(2)}, u32[]{:S(2)}) collective-permute-start(f32[3,40,128]{2,1,0:T(8,128)S(1)} %pad_maximum_fusion.1), channel_id=1, source_target_pairs={{0,7},{1,0},{2,1},{3,2},{4,3},{5,4},{6,5},{7,6},{8,15},{9,8},{10,9... | collective-permute-start | bytes 184328 | tf_op jit(solution)/shard_map/ppermute | solution.py:683
  12.7 4.6 %collective-permute-start.2 = (f32[3,40,128]{2,1,0:T(8,128)S(1)}, f32[3,40,128]{2,1,0:T(8,128)S(1)}, u32[]{:S(2)}, u32[]{:S(2)}) collective-permute-start(f32[3,40,128]{2,1,0:T(8,128)S(1)} %pad_maximum_fusion), channel_id=1, source_target_pairs={{0,1},{1,2},{2,3},{3,4},{4,5},{5,6},{6,7},{7,0},{8,9},{9,10},{10,1... | collective-permute-start | bytes 184328 | tf_op jit(solution)/shard_map/ppermute | solution.py:683
  17.3 1.1 %copy-start.2 = (f32[3,32,2048]{2,1,0:T(8,128)S(1)}, f32[3,32,2048]{2,1,0:T(8,128)}, u32[]{:S(2)}) copy-start(f32[3,32,2048]{2,1,0:T(8,128)} %center.1) | copy-start | bytes 2359300
  48.6 1.8 %copy-start = (f32[7552,128]{1,0:T(8,128)}, f32[7552,128]{1,0:T(8,128)S(1)}, u32[]{:S(2)}) copy-start(f32[7552,128]{1,0:T(8,128)S(1)} %get-tuple-element.5.phi) | copy-start | bytes 11599876
  50.4 9.6 %all-to-all-start = ((f32[32,1,128]{2,1,0:T(1,128)}), f32[32,1,128]{2,1,0:T(1,128)S(1)}, u32[]{:S(2)}, u32[]{:S(2)}) async-start(f32[32,1,128]{2,1,0:T(1,128)} %bitcast.2), calls=%async_computation | async-start | bytes 32768 | tf_op jit(solution)/shard_map/all_to_all | solution.py:721
  53.1 2.1 %copy-start.1 = (f32[7552,128]{1,0:T(8,128)S(1)}, f32[7552,128]{1,0:T(8,128)}, u32[]{:S(2)}) copy-start(f32[7552,128]{1,0:T(8,128)} %copy-done) | copy-start | bytes 11599876

commit v4 on v3

--- a/solution.py
+++ b/solution.py
@@ -433,7 +433,7 @@
     return looped(lv.edz, group, 4, step)
 
 
-GROUPS = {FINE: 2, TWIN: 8}
+GROUPS = {FINE: 1, TWIN: 2}
 
 
 def solve_kernel(
@@ -602,9 +602,8 @@
     return jnp.broadcast_to(mine, (SUBS, LANES))
 
 
-def turn_kernel(phi, out_ref, work, sem):
+def turn_kernel(phi, out_ref):
     start_row, number = 0, 0
-    copies = []
     for lv in LEVELS:
         s = lv.seg
         nz = EZ * lv.edz
@@ -622,25 +621,13 @@
                     lower = lane_iota(halves[0].shape) // 16 % 2 == 0
                     parts.append(jnp.where(lower, halves[0], turn(halves[1], 16)))
                     parts.append(jnp.where(lower, turn(halves[0], -16), halves[1]))
-                work[number] = jnp.concatenate(parts, axis=0).T
+                out_ref[number] = jnp.concatenate(parts, axis=0).T
                 number += 1
-            done = number - turned_tiles(lv)
-            copies.append(
-                pltpu.make_async_copy(
-                    work.at[pl.ds(done, turned_tiles(lv))], out_ref.at[pl.ds(done, turned_tiles(lv))], sem.at[len(copies)]
-                )
-            )
-            copies[-1].start()
         start_row += phi_rows(lv)
-    for copy in copies:
-        copy.wait()
-
-
-def pressure_kernel(gy_count, me_ref, gathered, source, fine_out, twin_out, turned, fine_all, twin_all, sem):
-    fetch = pltpu.make_async_copy(source, turned, sem)
-    fetch.start()
+
+
+def pressure_kernel(gy_count, me_ref, gathered, turned, fine_out, twin_out, fine_all, twin_all):
     mine = coarse_nodes(gathered[...], gy_count, me_ref[0])
-    fetch.wait()
     first = 0
     for n, (lv, out_ref, all_ref) in enumerate(((FINE, fine_out, fine_all), (TWIN, twin_out, twin_all))):
         s = lv.seg
@@ -709,7 +696,7 @@
     phi, message = pl.pallas_call(
         solve_kernel,
         out_shape=[
-            jax.ShapeDtypeStruct((sum(phi_rows(lv) for lv in LEVELS), LANES), F32),
+            vmem((sum(phi_rows(lv) for lv in LEVELS), LANES)),
             jax.ShapeDtypeStruct((gx * gy, LANES), F32),
         ],
         in_specs=[full] * 5,
@@ -722,13 +709,9 @@
     tiles = sum(lv.seg * turned_tiles(lv) for lv in LEVELS)
     turned = pl.pallas_call(
         turn_kernel,
-        out_shape=jax.ShapeDtypeStruct((tiles, LANES, LANES), F32),
+        out_shape=vmem((tiles, LANES, LANES)),
         in_specs=[full],
-        out_specs=pl.BlockSpec(memory_space=pltpu.HBM),
-        scratch_shapes=[
-            vmem((tiles, LANES, LANES)),
-            pltpu.SemaphoreType.DMA((sum(lv.seg for lv in LEVELS),)),
-        ],
+        out_specs=full,
         compiler_params=pltpu.CompilerParams(vmem_limit_bytes=16 * 1024 * 1024),
         cost_estimate=pl.CostEstimate(flops=4000000, bytes_accessed=8000000, transcendentals=0),
         name="turned",
@@ -740,11 +723,9 @@
             out_shape=[
                 jax.ShapeDtypeStruct((lv.edge, COLUMNS * lv.edge * EZ * lv.edz), F32) for lv in LEVELS
             ],
-            in_specs=[pl.BlockSpec(memory_space=pltpu.SMEM), full, pl.BlockSpec(memory_space=pltpu.HBM)],
+            in_specs=[pl.BlockSpec(memory_space=pltpu.SMEM), full, full],
             out_specs=[full] * 2,
-            scratch_shapes=[vmem((tiles, LANES, LANES))]
-            + [vmem((COLUMNS * turned_tiles(lv), SUBS * lv.seg, LANES)) for lv in LEVELS]
-            + [pltpu.SemaphoreType.DMA],
+            scratch_shapes=[vmem((COLUMNS * turned_tiles(lv), SUBS * lv.seg, LANES)) for lv in LEVELS],
             compiler_params=pltpu.CompilerParams(vmem_limit_bytes=16 * 1024 * 1024),
             name="pressure",
         )(me, gathered, turned)

time: 63.3 us -> 61.6 us (0.973)
  Pallas kernels: 36.1 us -> 33.1 us
  waiting for transfers between devices: 9.56 us -> 11.3 us
    pallas_call x2, Pallas kernels: 33.4 us -> 30.8 us  [the longest x1 29.1 us: shards(): pl.pallas_call(solve_kernel, out_shape=[vmem((sum((phi_rows(lv) for lv in...]
    all_to_all x1, waiting for transfers between devices: 1.6 us -> 3.3 us  [shards(): gathered = lax.all_to_all(message, ('gx', 'gy'), 0, 0, tiled=True)]
  transfers between devices with their start and end apart: 5 -> 5, of which waited for: 5 -> 5; matrix products, arithmetic and copies ran while one was open for 1% -> 1% of each run, Pallas kernels for 5% -> 3%
where the time goes in v4:
time: 61.6 us; the launch traced here: 61.3 us
  Pallas kernels  33.1 us (54%)
  waiting for transfers between devices  11.3 us (18%)
  starting transfers between devices  9.27 us (15%)
  local copies, waits for them, and re-layouts  6.95 us (11%)
  between operations  0.68 us (1%)
    pallas_call x1, Pallas kernels, shards(): pl.pallas_call(solve_kernel, out_shape=[vmem((sum((phi_rows(lv) for lv in...  29.1 us
    ppermute x4, waiting for transfers between devices, sent(): lax.ppermute(value, axis, [(i, (i + shift) % count) for i in range(count)])  7.97 us
    ppermute x4, starting transfers between devices, sent(): lax.ppermute(value, axis, [(i, (i + shift) % count) for i in range(count)])  6.73 us
    unnamed x6, local copies, waits for them, and re-layouts  5.06 us
    all_to_all x1, waiting for transfers between devices, shards(): gathered = lax.all_to_all(message, ('gx', 'gy'), 0, 0, tiled=True)  3.3 us
    all_to_all x1, starting transfers between devices, shards(): gathered = lax.all_to_all(message, ('gx', 'gy'), 0, 0, tiled=True)  2.54 us
    pallas_call x1, Pallas kernels, shards(): pl.pallas_call(functools.partial(pressure_kernel, gy), out_shape=[jax.Sha...  2.38 us
    pallas_call x1, Pallas kernels, shards(): pl.pallas_call(turn_kernel, out_shape=vmem((tiles, LANES, LANES)), in_spe...  1.67 us
  transfers between devices with their start and end apart: 5, of which 5 were waited for; matrix products, arithmetic and copies ran while one was open for 1% of the time, Pallas kernels for 3%

profile of v4, /device:TPU:0, one launch (start us, length us, event | category | flops | bytes accessed | tf_op | source)
XLA Modules:
  0.0 61.3 jit_solution(7586917786616887943)
XLA Ops:
  0.6 1.1 %fusion.1 = (f32[3,4,2048]{2,1,0:T(4,128)S(1)}, f32[3,4,2048]{2,1,0:T(4,128)S(1)}) fusion(f32[3,32,2048]{2,1,0:T(8,128)} %center.1), kind=kLoop, calls=%fused_computation.3 | loop fusion | bytes 393216 | tf_op jit(solution)/shard_map/slice | solution.py:673
  1.7 3.1 %collective-permute-start = (f32[3,4,2048]{2,1,0:T(4,128)S(1)}, f32[3,4,2048]{2,1,0:T(4,128)S(1)}, u32[]{:S(2)}, u32[]{:S(2)}) collective-permute-start(f32[3,4,2048]{2,1,0:T(4,128)S(1)} %get-tuple-element.9), channel_id=1, source_target_pairs={{0,8},{8,16},{16,24},{24,0},{1,9},{9,17},{17,25},{25,1},{2,10},{10... | collective-permute-start | bytes 294920 | tf_op jit(solution)/shard_map/ppermute | solution.py:670
  4.8 2.1 %collective-permute-start.1 = (f32[3,4,2048]{2,1,0:T(4,128)S(1)}, f32[3,4,2048]{2,1,0:T(4,128)S(1)}, u32[]{:S(2)}, u32[]{:S(2)}) collective-permute-start(f32[3,4,2048]{2,1,0:T(4,128)S(1)} %get-tuple-element.8), channel_id=1, source_target_pairs={{0,24},{8,0},{16,8},{24,16},{1,25},{9,1},{17,9},{25,17},{2,26},{10... | collective-permute-start | bytes 294920 | tf_op jit(solution)/shard_map/ppermute | solution.py:670
  6.9 0.8 %fusion = (f32[3,32,128]{2,1,0:T(8,128)S(1)}, f32[3,32,128]{2,1,0:T(8,128)S(1)}) fusion(f32[3,32,2048]{2,1,0:T(8,128)} %center.1), kind=kLoop, calls=%fused_computation.2 | loop fusion | bytes 196608 | tf_op jit(solution)/shard_map/slice | solution.py:676
  7.7 2.6 %collective-permute-done.x_low = f32[3,4,2048]{2,1,0:T(4,128)S(1)} collective-permute-done((f32[3,4,2048]{2,1,0:T(4,128)S(1)}, f32[3,4,2048]{2,1,0:T(4,128)S(1)}, u32[]{:S(2)}, u32[]{:S(2)}) %collective-permute-start) | collective-permute-done | bytes 98336 | tf_op jit(solution)/shard_map/ppermute | solution.py:670
  10.3 0.8 %collective-permute-done.1.x_high = f32[3,4,2048]{2,1,0:T(4,128)S(1)} collective-permute-done((f32[3,4,2048]{2,1,0:T(4,128)S(1)}, f32[3,4,2048]{2,1,0:T(4,128)S(1)}, u32[]{:S(2)}, u32[]{:S(2)}) %collective-permute-start.1) | collective-permute-done | bytes 98336 | tf_op jit(solution)/shard_map/ppermute | solution.py:670
  11.1 1.5 %collective-permute-start.3 = (f32[3,40,128]{2,1,0:T(8,128)S(1)}, f32[3,40,128]{2,1,0:T(8,128)S(1)}, u32[]{:S(2)}, u32[]{:S(2)}) collective-permute-start(f32[3,40,128]{2,1,0:T(8,128)S(1)} %pad_maximum_fusion.1), channel_id=1, source_target_pairs={{0,7},{1,0},{2,1},{3,2},{4,3},{5,4},{6,5},{7,6},{8,15},{9,8},{10,9... | collective-permute-start | bytes 184328 | tf_op jit(solution)/shard_map/ppermute | solution.py:670
  12.7 0.1 collective-permute-start.2
  12.7 1.9 %collective-permute-done.3.y_high = f32[3,40,128]{2,1,0:T(8,128)S(1)} collective-permute-done((f32[3,40,128]{2,1,0:T(8,128)S(1)}, f32[3,40,128]{2,1,0:T(8,128)S(1)}, u32[]{:S(2)}, u32[]{:S(2)}) %collective-permute-start.3) | collective-permute-done | bytes 61472 | tf_op jit(solution)/shard_map/ppermute | solution.py:670
  14.6 2.7 %collective-permute-done.2.y_low = f32[3,40,128]{2,1,0:T(8,128)S(1)} collective-permute-done((f32[3,40,128]{2,1,0:T(8,128)S(1)}, f32[3,40,128]{2,1,0:T(8,128)S(1)}, u32[]{:S(2)}, u32[]{:S(2)}) %collective-permute-start.2) | collective-permute-done | bytes 61472 | tf_op jit(solution)/shard_map/ppermute | solution.py:670
  17.3 0.0 copy-start.2
  17.3 1.1 %copy-done.2 = f32[3,32,2048]{2,1,0:T(8,128)S(1)} copy-done((f32[3,32,2048]{2,1,0:T(8,128)S(1)}, f32[3,32,2048]{2,1,0:T(8,128)}, u32[]{:S(2)}) %copy-start.2) | copy-done | bytes 786456
  18.4 29.1 %solve.1 = (f32[7552,128]{1,0:T(8,128)S(1)}, f32[32,128]{1,0:T(8,128)}) custom-call(f32[3,32,2048]{2,1,0:T(8,128)S(1)} %copy-done.2, f32[3,4,2048]{2,1,0:T(4,128)S(1)} %collective-permute-done.x_low, f32[3,4,2048]{2,1,0:T(4,128)S(1)} %collective-permute-done.1.x_high, f32[3,40,128]{2,1,0:T(8,128)S(1)} %collective-permute-done.2.y_low, ...), custom_call_target="tpu_custom_call" | custom-call | tf_op jit(solution)/shard_map/solve/pallas_call | solution.py:696
  47.5 0.0 copy-start
  47.5 1.8 %copy-done = f32[7552,128]{1,0:T(8,128)} copy-done((f32[7552,128]{1,0:T(8,128)}, f32[7552,128]{1,0:T(8,128)S(1)}, u32[]{:S(2)}) %copy-start) | copy-done | bytes 3866648
  49.3 2.5 %all-to-all-start = ((f32[32,1,128]{2,1,0:T(1,128)}), f32[32,1,128]{2,1,0:T(1,128)S(1)}, u32[]{:S(2)}, u32[]{:S(2)}) async-start(f32[32,1,128]{2,1,0:T(1,128)} %bitcast.2), calls=%async_computation | async-start | bytes 32768 | tf_op jit(solution)/shard_map/all_to_all | solution.py:708
  51.9 0.0 copy-start.1
  51.9 2.1 %copy-done.1 = f32[7552,128]{1,0:T(8,128)S(1)} copy-done((f32[7552,128]{1,0:T(8,128)S(1)}, f32[7552,128]{1,0:T(8,128)}, u32[]{:S(2)}) %copy-start.1) | copy-done | bytes 3866648
  54.0 1.7 %turned.1 = f32[46,128,128]{2,1,0:T(8,128)S(1)} custom-call(f32[7552,128]{1,0:T(8,128)S(1)} %copy-done.1), custom_call_target="tpu_custom_call" | custom-call | flops 4000000 | bytes 8000000 | tf_op jit(solution)/shard_map/turned/pallas_call | solution.py:710
  55.7 3.3 %all-to-all-done = f32[32,1,128]{2,1,0:T(1,128)S(1)} async-done(((f32[32,1,128]{2,1,0:T(1,128)}), f32[32,1,128]{2,1,0:T(1,128)S(1)}, u32[]{:S(2)}, u32[]{:S(2)}) %all-to-all-start) | async-done | bytes 16416 | tf_op jit(solution)/shard_map/all_to_all | solution.py:708
  59.0 2.4 %pressure.1 = (f32[32,2048]{1,0:T(8,128)}, f32[16,512]{1,0:T(8,128)}) custom-call(s32[1]{0:T(128)} %bitcast.me_ref, f32[32,128]{1,0:T(8,128)S(1)} %bitcast.5, f32[46,128,128]{2,1,0:T(8,128)S(1)} %turned.1), custom_call_target="tpu_custom_call" | custom-call | tf_op jit(solution)/shard_map/pressure/pallas_call | solution.py:721
  (4 shorter events, 0.0 us)
Async XLA Ops:
  1.7 8.6 %collective-permute-start = (f32[3,4,2048]{2,1,0:T(4,128)S(1)}, f32[3,4,2048]{2,1,0:T(4,128)S(1)}, u32[]{:S(2)}, u32[]{:S(2)}) collective-permute-start(f32[3,4,2048]{2,1,0:T(4,128)S(1)} %get-tuple-element.9), channel_id=1, source_target_pairs={{0,8},{8,16},{16,24},{24,0},{1,9},{9,17},{17,25},{25,1},{2,10},{10... | collective-permute-start | bytes 294920 | tf_op jit(solution)/shard_map/ppermute | solution.py:670
  4.8 6.4 %collective-permute-start.1 = (f32[3,4,2048]{2,1,0:T(4,128)S(1)}, f32[3,4,2048]{2,1,0:T(4,128)S(1)}, u32[]{:S(2)}, u32[]{:S(2)}) collective-permute-start(f32[3,4,2048]{2,1,0:T(4,128)S(1)} %get-tuple-element.8), channel_id=1, source_target_pairs={{0,24},{8,0},{16,8},{24,16},{1,25},{9,1},{17,9},{25,17},{2,26},{10... | collective-permute-start | bytes 294920 | tf_op jit(solution)/shard_map/ppermute | solution.py:670
  11.1 3.5 %collective-permute-start.3 = (f32[3,40,128]{2,1,0:T(8,128)S(1)}, f32[3,40,128]{2,1,0:T(8,128)S(1)}, u32[]{:S(2)}, u32[]{:S(2)}) collective-permute-start(f32[3,40,128]{2,1,0:T(8,128)S(1)} %pad_maximum_fusion.1), channel_id=1, source_target_pairs={{0,7},{1,0},{2,1},{3,2},{4,3},{5,4},{6,5},{7,6},{8,15},{9,8},{10,9... | collective-permute-start | bytes 184328 | tf_op jit(solution)/shard_map/ppermute | solution.py:670
  12.7 4.6 %collective-permute-start.2 = (f32[3,40,128]{2,1,0:T(8,128)S(1)}, f32[3,40,128]{2,1,0:T(8,128)S(1)}, u32[]{:S(2)}, u32[]{:S(2)}) collective-permute-start(f32[3,40,128]{2,1,0:T(8,128)S(1)} %pad_maximum_fusion), channel_id=1, source_target_pairs={{0,1},{1,2},{2,3},{3,4},{4,5},{5,6},{6,7},{7,0},{8,9},{9,10},{10,1... | collective-permute-start | bytes 184328 | tf_op jit(solution)/shard_map/ppermute | solution.py:670
  17.3 1.1 %copy-start.2 = (f32[3,32,2048]{2,1,0:T(8,128)S(1)}, f32[3,32,2048]{2,1,0:T(8,128)}, u32[]{:S(2)}) copy-start(f32[3,32,2048]{2,1,0:T(8,128)} %center.1) | copy-start | bytes 2359300
  47.5 1.8 %copy-start = (f32[7552,128]{1,0:T(8,128)}, f32[7552,128]{1,0:T(8,128)S(1)}, u32[]{:S(2)}) copy-start(f32[7552,128]{1,0:T(8,128)S(1)} %get-tuple-element.5.phi) | copy-start | bytes 11599876
  49.3 9.6 %all-to-all-start = ((f32[32,1,128]{2,1,0:T(1,128)}), f32[32,1,128]{2,1,0:T(1,128)S(1)}, u32[]{:S(2)}, u32[]{:S(2)}) async-start(f32[32,1,128]{2,1,0:T(1,128)} %bitcast.2), calls=%async_computation | async-start | bytes 32768 | tf_op jit(solution)/shard_map/all_to_all | solution.py:708
  51.9 2.1 %copy-start.1 = (f32[7552,128]{1,0:T(8,128)S(1)}, f32[7552,128]{1,0:T(8,128)}, u32[]{:S(2)}) copy-start(f32[7552,128]{1,0:T(8,128)} %copy-done) | copy-start | bytes 11599876

commit v5 on v4

--- a/solution.py
+++ b/solution.py
@@ -214,7 +214,7 @@
 
 
 def phi_rows(lv):
-    return EZ * lv.edz * lv.tiles * SUBS
+    return lv.edz * (lv.tiles + lv.seg) * SUBS
 
 
 def turned_tiles(lv):
@@ -363,7 +363,8 @@
 def finish(case, group, alphas, phi_ref):
     lv, cs, s = case.lv, case.cs, case.lv.seg
     n = lv.tiles
-    lower = lane_parts()[1] == 0
+    corner, element, _, _ = lane_parts()
+    lower = element == 0
 
     def fresh(z, i, j, gz):
         k = i * s + j
@@ -375,11 +376,21 @@
             for alpha, d_ref in zip(alphas[h], case.d):
                 value = value + alpha * d_ref[inner, h * n + k]
             value = cs.masked(value, i, j, 1)
-            at = pl.multiple_of(((z * 2 + h) * n + k) * SUBS, SUBS)
-            phi_ref[pl.ds(at, SUBS), :] = value
             values.append(value)
         total = values[0] + turn(values[0], 32)
-        return jnp.where(lower, values[1], values[0]), total + turn(total, 64)
+        chosen = jnp.where(lower, values[1], values[0])
+        at = pl.multiple_of((z * n + k) * SUBS, SUBS)
+        phi_ref[pl.ds(at, SUBS), :] = chosen
+        return chosen, total + turn(total, 64)
+
+    def pack(z, j, totals):
+        packed = totals[0]
+        for i in range(1, min(s, 4)):
+            packed = jnp.where(corner == i, totals[i], packed)
+        if s > 4:
+            packed = jnp.where(lower, packed, turn(totals[4], 16))
+        at = pl.multiple_of((lv.edz * n + z * s + j) * SUBS, SUBS)
+        phi_ref[pl.ds(at, SUBS), :] = packed
 
     gz = cs.fz(lv.mz)
     for i in range(s):
@@ -387,6 +398,8 @@
             k = i * s + j
             case.chosen[k], case.total[k] = fresh(0, i, j, gz)
             case.fz[k] = jnp.zeros((SUBS, LANES), F32)
+    for j in range(s):
+        pack(0, j, [case.total[i * s + j] for i in range(s)])
 
     def cut(values, table):
         return [v if f is None else v * f for v, f in zip(values, table)]
@@ -422,6 +435,7 @@
                     parts[1].append(value * turn(u[k], -32))
                     parts[2].append(value * turn(u[k], 64))
                     parts[3].append(value * low[k])
+                pack(up, j, [after_low[i * s + j] for i in range(s)])
                 for total, part in zip(sums, parts):
                     total.append(tree(part))
                 before = flux_y
@@ -433,29 +447,42 @@
     return looped(lv.edz, group, 4, step)
 
 
-GROUPS = {FINE: 1, TWIN: 2}
+GROUPS = {FINE: 1, TWIN: 8}
+
+
+def place_kernel(center, out_ref):
+    nx = center.shape[1]
+    out_ref[...] = jnp.ones(out_ref.shape, F32)
+    for m in range(3):
+        off = m * (nx + 2 * MX) + MX
+        out_ref[off : off + nx, :] = center[m]
 
 
 def solve_kernel(
-    center, x_low, x_high, y_low, y_high,
+    inside, x_low, x_high, y_low, y_high,
     phi, message,
-    flat, rows, pairs, twin_rows, *refs,
+    flat, sides, rows, pairs, twin_rows, *refs,
 ):
-    lanes = center.shape[2]
-    rim = (flat.shape[1] - lanes) // 2
-    nx = center.shape[1]
-    top = MX + nx
+    lanes = inside.shape[1]
+    rim = y_low.shape[2]
+    wide = y_low.shape[1]
     for m in range(3):
-        off = m * (nx + 2 * MX)
-        flat[off : off + top + MX, :rim] = y_low[m]
-        flat[off : off + MX, rim : rim + lanes] = x_low[m]
-        flat[off + MX : off + top, rim : rim + lanes] = center[m]
-        flat[off + top : off + top + MX, rim : rim + lanes] = x_high[m]
-        flat[off : off + top + MX, rim + lanes :] = y_high[m]
-    used = 3 * (nx + 2 * MX)
-    flat[used:, :] = jnp.ones((LANES - used, flat.shape[1]), F32)
-    for t in range(flat.shape[1] // LANES):
-        rows[t * LANES : (t + 1) * LANES, :] = flat[:, t * LANES : (t + 1) * LANES].T
+        off = m * wide
+        flat[off : off + MX, :] = x_low[m]
+        flat[off + wide - MX : off + wide, :] = x_high[m]
+        sides[off : off + wide, :rim] = y_low[m]
+        sides[off : off + wide, rim:] = y_high[m]
+    sides[3 * wide :, :] = jnp.ones((LANES - 3 * wide, sides.shape[1]), F32)
+    row = sub_iota((LANES, LANES))
+    place = row % wide
+    outer = (row < 3 * wide) & ((place < MX) | (place >= wide - MX))
+    for t in range(rim // LANES):
+        low, high = slice(t * LANES, (t + 1) * LANES), slice(rim + t * LANES, rim + (t + 1) * LANES)
+        rows[low, :] = sides[:, low].T
+        rows[lanes + rim + t * LANES : lanes + rim + (t + 1) * LANES, :] = sides[:, high].T
+    for t in range(lanes // LANES):
+        part = slice(t * LANES, (t + 1) * LANES)
+        rows[rim + t * LANES : rim + (t + 1) * LANES, :] = jnp.where(outer, flat[:, part], inside[:, part]).T
 
     nz = EZ * ELZ
     twin_y = rows.shape[0] // nz // 2
@@ -608,19 +635,17 @@
         s = lv.seg
         nz = EZ * lv.edz
         per = LANES // nz
+        sums_row = start_row + lv.edz * lv.tiles * SUBS
         for i in range(s):
             for t in range(turned_tiles(lv)):
                 parts = []
                 for n in range(per):
-                    y = lv.mx + t * per + n
-                    start = start_row + (i * s + y % s) * SUBS + y // s
-                    halves = [
-                        phi[pl.ds(h * lv.tiles * SUBS + start, lv.edz, stride=2 * lv.tiles * SUBS), :]
-                        for h in range(2)
-                    ]
-                    lower = lane_iota(halves[0].shape) // 16 % 2 == 0
-                    parts.append(jnp.where(lower, halves[0], turn(halves[1], 16)))
-                    parts.append(jnp.where(lower, turn(halves[0], -16), halves[1]))
+                    yo, j = divmod(lv.mx + t * per + n, s)
+                    chosen = phi[pl.ds(start_row + (i * s + j) * SUBS + yo, lv.edz, stride=lv.tiles * SUBS), :]
+                    total = phi[pl.ds(sums_row + j * SUBS + yo, lv.edz, stride=s * SUBS), :]
+                    lower = lane_iota(chosen.shape) // 16 % 2 == 0
+                    parts.append(jnp.where(lower, chosen, turn(total, 16) if i < 4 else total))
+                    parts.append(jnp.where(lower, turn(chosen, -16), 0.0))
                 out_ref[number] = jnp.concatenate(parts, axis=0).T
                 number += 1
         start_row += phi_rows(lv)
@@ -631,23 +656,20 @@
     first = 0
     for n, (lv, out_ref, all_ref) in enumerate(((FINE, fine_out, fine_all), (TWIN, twin_out, twin_all))):
         s = lv.seg
-        nz = EZ * lv.edz
         tiles = turned_tiles(lv)
-        lower = lane_iota() % nz < lv.edz
-        scales = {}
+        nodes = {}
         for c in range(COLUMNS):
             for p in range(4):
                 at = p * 32 + n * 16 + c * 8
-                node = jnp.broadcast_to(mine[:, at : at + 1], (SUBS, LANES))
-                scales[2 * p, c] = jnp.where(lower, 1.0, node)
-                scales[2 * p + 1, c] = jnp.where(lower, node, 0.0)
+                nodes[p, c] = jnp.broadcast_to(mine[:, at : at + 1], (SUBS, LANES))
         for c in range(COLUMNS):
             for t in range(tiles):
                 at = (c * tiles + t) * LANES
                 for i in range(s):
-                    value = tree(
-                        [turned[first + i * tiles + t, a * 16 + c * 8 : a * 16 + c * 8 + 8, :] * scales[a, c] for a in range(8)]
-                    )
+                    def part(group):
+                        return turned[first + i * tiles + t, group * 16 + c * 8 : group * 16 + c * 8 + 8, :]
+
+                    value = tree([part(2 * p) * nodes[p, c] for p in range(4)]) + part(2 * (i % 4) + 1)
                     all_ref[c * tiles + t, pl.ds(i, SUBS, stride=s), :] = value
                 out_ref[:, at : at + LANES] = all_ref[c * tiles + t, lv.mx : lv.mx + lv.edge, :]
         first += s * tiles
@@ -680,7 +702,8 @@
     halos = [x_low, x_high, y_low, y_high]
     flat_lanes = lanes + 2 * rim
     scratch = [
-        vmem((LANES, flat_lanes)),
+        vmem((LANES, lanes)),
+        vmem((LANES, 2 * rim)),
         vmem((flat_lanes, LANES)),
         vmem((flat_lanes // 2, LANES)),
         vmem((SUBS * (TWIN.seg + 2) * nz, LANES)),
@@ -693,6 +716,15 @@
         scratch.append(vmem((2 * lv.tiles, SUBS, LANES)))
         scratch += [vmem((lv.tiles, SUBS, LANES))] * 2
     full = pl.BlockSpec(memory_space=pltpu.VMEM)
+    inside = pl.pallas_call(
+        place_kernel,
+        out_shape=vmem((LANES, lanes)),
+        in_specs=[full],
+        out_specs=full,
+        compiler_params=pltpu.CompilerParams(vmem_limit_bytes=8 * 1024 * 1024),
+        cost_estimate=pl.CostEstimate(flops=1000000, bytes_accessed=4000000, transcendentals=0),
+        name="place",
+    )(permeability)
     phi, message = pl.pallas_call(
         solve_kernel,
         out_shape=[
@@ -704,7 +736,7 @@
         scratch_shapes=scratch,
         compiler_params=pltpu.CompilerParams(vmem_limit_bytes=44 * 1024 * 1024),
         name="solve",
-    )(permeability, *halos)
+    )(inside, *halos)
     gathered = lax.all_to_all(message, ("gx", "gy"), 0, 0, tiled=True)
     tiles = sum(lv.seg * turned_tiles(lv) for lv in LEVELS)
     turned = pl.pallas_call(

time: 61.6 us -> 61.1 us (level)
  starting transfers between devices: 9.27 us -> 12.8 us
  waiting for transfers between devices: 11.3 us -> 7.9 us
  local copies, waits for them, and re-layouts: 6.95 us -> 6.1 us
    ppermute x4, waiting for transfers between devices: 7.97 us -> 4.07 us  [sent(): lax.ppermute(value, axis, [(i, (i + shift) % count) for i in range(count)])]
    all_to_all x1, starting transfers between devices: 2.54 us -> 4.94 us  [shards(): gathered = lax.all_to_all(message, ('gx', 'gy'), 0, 0, tiled=True)]
    ppermute x4, starting transfers between devices: 6.73 us -> 7.9 us  [sent(): lax.ppermute(value, axis, [(i, (i + shift) % count) for i in range(count)])]
    unnamed x6, local copies, waits for them, and re-layouts: 5.06 us -> 4.21 us
  transfers between devices with their start and end apart: 5 -> 5, of which waited for: 5 -> 4; matrix products, arithmetic and copies ran while one was open for 1% -> 1% of each run, Pallas kernels for 3% -> 3%
where the time goes in v5:
time: 61.1 us; the launch traced here: 60.8 us
  Pallas kernels  33.2 us (54%)
  starting transfers between devices  12.8 us (21%)
  waiting for transfers between devices  7.9 us (13%)
  local copies, waits for them, and re-layouts  6.1 us (10%)
  between operations  0.69 us (1%)
    pallas_call x1, Pallas kernels, shards(): pl.pallas_call(solve_kernel, out_shape=[vmem((sum((phi_rows(lv) for lv in...  29.2 us
    ppermute x4, starting transfers between devices, sent(): lax.ppermute(value, axis, [(i, (i + shift) % count) for i in range(count)])  7.9 us
    all_to_all x1, starting transfers between devices, shards(): gathered = lax.all_to_all(message, ('gx', 'gy'), 0, 0, tiled=True)  4.94 us
    unnamed x6, local copies, waits for them, and re-layouts  4.21 us
    ppermute x4, waiting for transfers between devices, sent(): lax.ppermute(value, axis, [(i, (i + shift) % count) for i in range(count)])  4.07 us
    all_to_all x1, waiting for transfers between devices, shards(): gathered = lax.all_to_all(message, ('gx', 'gy'), 0, 0, tiled=True)  3.83 us
    pallas_call x1, Pallas kernels, shards(): pl.pallas_call(functools.partial(pressure_kernel, gy), out_shape=[jax.Sha...  2.36 us
    pallas_call x1, Pallas kernels, shards(): pl.pallas_call(turn_kernel, out_shape=vmem((tiles, LANES, LANES)), in_spe...  1.56 us
  transfers between devices with their start and end apart: 5, of which 4 were waited for; matrix products, arithmetic and copies ran while one was open for 1% of the time, Pallas kernels for 3%

profile of v5, /device:TPU:0, one launch (start us, length us, event | category | flops | bytes accessed | tf_op | source)
XLA Modules:
  0.0 60.8 jit_solution(1488878895084742779)
XLA Ops:
  0.6 1.1 %fusion.1 = (f32[3,4,2048]{2,1,0:T(4,128)S(1)}, f32[3,4,2048]{2,1,0:T(4,128)S(1)}) fusion(f32[3,32,2048]{2,1,0:T(8,128)} %center.1), kind=kLoop, calls=%fused_computation.3 | loop fusion | bytes 393216 | tf_op jit(solution)/shard_map/slice | solution.py:695
  1.7 3.1 %collective-permute-start = (f32[3,4,2048]{2,1,0:T(4,128)S(1)}, f32[3,4,2048]{2,1,0:T(4,128)S(1)}, u32[]{:S(2)}, u32[]{:S(2)}) collective-permute-start(f32[3,4,2048]{2,1,0:T(4,128)S(1)} %get-tuple-element.9), channel_id=1, source_target_pairs={{0,8},{8,16},{16,24},{24,0},{1,9},{9,17},{17,25},{25,1},{2,10},{10... | collective-permute-start | bytes 294920 | tf_op jit(solution)/shard_map/ppermute | solution.py:692
  4.8 2.1 %collective-permute-start.1 = (f32[3,4,2048]{2,1,0:T(4,128)S(1)}, f32[3,4,2048]{2,1,0:T(4,128)S(1)}, u32[]{:S(2)}, u32[]{:S(2)}) collective-permute-start(f32[3,4,2048]{2,1,0:T(4,128)S(1)} %get-tuple-element.8), channel_id=1, source_target_pairs={{0,24},{8,0},{16,8},{24,16},{1,25},{9,1},{17,9},{25,17},{2,26},{10... | collective-permute-start | bytes 294920 | tf_op jit(solution)/shard_map/ppermute | solution.py:692
  6.9 0.8 %fusion = (f32[3,32,128]{2,1,0:T(8,128)S(1)}, f32[3,32,128]{2,1,0:T(8,128)S(1)}) fusion(f32[3,32,2048]{2,1,0:T(8,128)} %center.1), kind=kLoop, calls=%fused_computation.2 | loop fusion | bytes 196608 | tf_op jit(solution)/shard_map/slice | solution.py:698
  7.7 2.6 %collective-permute-done.x_low = f32[3,4,2048]{2,1,0:T(4,128)S(1)} collective-permute-done((f32[3,4,2048]{2,1,0:T(4,128)S(1)}, f32[3,4,2048]{2,1,0:T(4,128)S(1)}, u32[]{:S(2)}, u32[]{:S(2)}) %collective-permute-start) | collective-permute-done | bytes 98336 | tf_op jit(solution)/shard_map/ppermute | solution.py:692
  10.3 0.8 %collective-permute-done.1.x_high = f32[3,4,2048]{2,1,0:T(4,128)S(1)} collective-permute-done((f32[3,4,2048]{2,1,0:T(4,128)S(1)}, f32[3,4,2048]{2,1,0:T(4,128)S(1)}, u32[]{:S(2)}, u32[]{:S(2)}) %collective-permute-start.1) | collective-permute-done | bytes 98336 | tf_op jit(solution)/shard_map/ppermute | solution.py:692
  11.1 0.1 collective-permute-start.2
  11.2 2.7 %collective-permute-start.3 = (f32[3,40,128]{2,1,0:T(8,128)S(1)}, f32[3,40,128]{2,1,0:T(8,128)S(1)}, u32[]{:S(2)}, u32[]{:S(2)}) collective-permute-start(f32[3,40,128]{2,1,0:T(8,128)S(1)} %pad_maximum_fusion.1), channel_id=1, source_target_pairs={{0,7},{1,0},{2,1},{3,2},{4,3},{5,4},{6,5},{7,6},{8,15},{9,8},{10,9... | collective-permute-start | bytes 184328 | tf_op jit(solution)/shard_map/ppermute | solution.py:692
  13.9 0.0 copy-start.2
  13.9 1.1 %copy-done.2 = f32[3,32,2048]{2,1,0:T(8,128)S(1)} copy-done((f32[3,32,2048]{2,1,0:T(8,128)S(1)}, f32[3,32,2048]{2,1,0:T(8,128)}, u32[]{:S(2)}) %copy-start.2) | copy-done | bytes 786456
  15.0 0.1 place.1.inside
  15.1 0.6 collective-permute-done.2.y_low
  15.7 0.0 collective-permute-done.3.y_high
  15.8 29.2 %solve.1 = (f32[4608,128]{1,0:T(8,128)S(1)}, f32[32,128]{1,0:T(8,128)}) custom-call(f32[128,2048]{1,0:T(8,128)S(1)} %place.1.inside, f32[3,4,2048]{2,1,0:T(4,128)S(1)} %collective-permute-done.x_low, f32[3,4,2048]{2,1,0:T(4,128)S(1)} %collective-permute-done.1.x_high, f32[3,40,128]{2,1,0:T(8,128)S(1)} %collective-permute-done.2.y_low, ...), custom_call_target="tpu_custom_call" | custom-call | tf_op jit(solution)/shard_map/solve/pallas_call | solution.py:728
  45.0 0.0 copy-start
  45.0 1.4 %copy-done = f32[4608,128]{1,0:T(8,128)} copy-done((f32[4608,128]{1,0:T(8,128)}, f32[4608,128]{1,0:T(8,128)S(1)}, u32[]{:S(2)}) %copy-start) | copy-done | bytes 2359320
  46.4 4.9 %all-to-all-start = ((f32[32,1,128]{2,1,0:T(1,128)}), f32[32,1,128]{2,1,0:T(1,128)S(1)}, u32[]{:S(2)}, u32[]{:S(2)}) async-start(f32[32,1,128]{2,1,0:T(1,128)} %bitcast.2), calls=%async_computation | async-start | bytes 32768 | tf_op jit(solution)/shard_map/all_to_all | solution.py:740
  51.3 0.0 copy-start.1
  51.3 1.7 %copy-done.1 = f32[4608,128]{1,0:T(8,128)S(1)} copy-done((f32[4608,128]{1,0:T(8,128)S(1)}, f32[4608,128]{1,0:T(8,128)}, u32[]{:S(2)}) %copy-start.1) | copy-done | bytes 2359320
  53.0 1.6 %turned.1 = f32[46,128,128]{2,1,0:T(8,128)S(1)} custom-call(f32[4608,128]{1,0:T(8,128)S(1)} %copy-done.1), custom_call_target="tpu_custom_call" | custom-call | flops 4000000 | bytes 8000000 | tf_op jit(solution)/shard_map/turned/pallas_call | solution.py:742
  54.6 3.8 %all-to-all-done = f32[32,1,128]{2,1,0:T(1,128)S(1)} async-done(((f32[32,1,128]{2,1,0:T(1,128)}), f32[32,1,128]{2,1,0:T(1,128)S(1)}, u32[]{:S(2)}, u32[]{:S(2)}) %all-to-all-start) | async-done | bytes 16416 | tf_op jit(solution)/shard_map/all_to_all | solution.py:740
  58.4 2.4 %pressure.1 = (f32[32,2048]{1,0:T(8,128)}, f32[16,512]{1,0:T(8,128)}) custom-call(s32[1]{0:T(128)} %bitcast.me_ref, f32[32,128]{1,0:T(8,128)S(1)} %bitcast.5, f32[46,128,128]{2,1,0:T(8,128)S(1)} %turned.1), custom_call_target="tpu_custom_call" | custom-call | tf_op jit(solution)/shard_map/pressure/pallas_call | solution.py:753
  (4 shorter events, 0.0 us)
Async XLA Ops:
  1.7 8.6 %collective-permute-start = (f32[3,4,2048]{2,1,0:T(4,128)S(1)}, f32[3,4,2048]{2,1,0:T(4,128)S(1)}, u32[]{:S(2)}, u32[]{:S(2)}) collective-permute-start(f32[3,4,2048]{2,1,0:T(4,128)S(1)} %get-tuple-element.9), channel_id=1, source_target_pairs={{0,8},{8,16},{16,24},{24,0},{1,9},{9,17},{17,25},{25,1},{2,10},{10... | collective-permute-start | bytes 294920 | tf_op jit(solution)/shard_map/ppermute | solution.py:692
  4.8 6.4 %collective-permute-start.1 = (f32[3,4,2048]{2,1,0:T(4,128)S(1)}, f32[3,4,2048]{2,1,0:T(4,128)S(1)}, u32[]{:S(2)}, u32[]{:S(2)}) collective-permute-start(f32[3,4,2048]{2,1,0:T(4,128)S(1)} %get-tuple-element.8), channel_id=1, source_target_pairs={{0,24},{8,0},{16,8},{24,16},{1,25},{9,1},{17,9},{25,17},{2,26},{10... | collective-permute-start | bytes 294920 | tf_op jit(solution)/shard_map/ppermute | solution.py:692
  11.1 4.6 %collective-permute-start.2 = (f32[3,40,128]{2,1,0:T(8,128)S(1)}, f32[3,40,128]{2,1,0:T(8,128)S(1)}, u32[]{:S(2)}, u32[]{:S(2)}) collective-permute-start(f32[3,40,128]{2,1,0:T(8,128)S(1)} %pad_maximum_fusion), channel_id=1, source_target_pairs={{0,1},{1,2},{2,3},{3,4},{4,5},{5,6},{6,7},{7,0},{8,9},{9,10},{10,1... | collective-permute-start | bytes 184328 | tf_op jit(solution)/shard_map/ppermute | solution.py:692
  11.2 4.5 %collective-permute-start.3 = (f32[3,40,128]{2,1,0:T(8,128)S(1)}, f32[3,40,128]{2,1,0:T(8,128)S(1)}, u32[]{:S(2)}, u32[]{:S(2)}) collective-permute-start(f32[3,40,128]{2,1,0:T(8,128)S(1)} %pad_maximum_fusion.1), channel_id=1, source_target_pairs={{0,7},{1,0},{2,1},{3,2},{4,3},{5,4},{6,5},{7,6},{8,15},{9,8},{10,9... | collective-permute-start | bytes 184328 | tf_op jit(solution)/shard_map/ppermute | solution.py:692
  13.9 1.1 %copy-start.2 = (f32[3,32,2048]{2,1,0:T(8,128)S(1)}, f32[3,32,2048]{2,1,0:T(8,128)}, u32[]{:S(2)}) copy-start(f32[3,32,2048]{2,1,0:T(8,128)} %center.1) | copy-start | bytes 2359300
  45.0 1.4 %copy-start = (f32[4608,128]{1,0:T(8,128)}, f32[4608,128]{1,0:T(8,128)S(1)}, u32[]{:S(2)}) copy-start(f32[4608,128]{1,0:T(8,128)S(1)} %get-tuple-element.5.phi) | copy-start | bytes 7077892
  46.4 12.0 %all-to-all-start = ((f32[32,1,128]{2,1,0:T(1,128)}), f32[32,1,128]{2,1,0:T(1,128)S(1)}, u32[]{:S(2)}, u32[]{:S(2)}) async-start(f32[32,1,128]{2,1,0:T(1,128)} %bitcast.2), calls=%async_computation | async-start | bytes 32768 | tf_op jit(solution)/shard_map/all_to_all | solution.py:740
  51.3 1.7 %copy-start.1 = (f32[4608,128]{1,0:T(8,128)S(1)}, f32[4608,128]{1,0:T(8,128)}, u32[]{:S(2)}) copy-start(f32[4608,128]{1,0:T(8,128)} %copy-done) | copy-start | bytes 7077892

commit v6 on v5

--- a/solution.py
+++ b/solution.py
@@ -17,7 +17,6 @@
 SUBS = 8
 COLUMNS = 2
 F32 = jnp.float32
-BF16 = jnp.bfloat16
 
 
 class Level(typing.NamedTuple):
@@ -50,7 +49,7 @@
 
     @property
     def planes(self):
-        return -(-(self.inner + 1) // 2) * 2
+        return self.inner + 1
 
 
 FINE = Level(EL, ELZ, MX, MZ, 1.0, 1)
@@ -141,62 +140,50 @@
     return value
 
 
-def spread_weights(lv, k_ref, high_refs, low_refs, w_refs):
+def spread_weights(lv, k_ref, w_refs):
     s = lv.seg
-    wide = (SUBS, LANES)
-    pos = lane_iota(wide)
-    yo = sub_iota(wide)
-    first = pos < 40
-    third = pos >= 80
-    second = (pos >= 40) & (pos < 80)
-    edge_x = first & (pos >= (lv.width - 1) * lv.step)
-
-    def one(z, i, c):
+    lane = lane_iota()
+    group = lane // 8
+    yo = sub_iota()
+    first = group < s
+    second = (group >= s) & (group < 2 * s)
+    turned_x = group % s == s - 1
+    edge_x = first & (lane % 8 * s + group >= lv.width - 1)
+    quarter = [group % 4 == n for n in range(4)]
+    block = [group // 4 == n for n in range(4)]
+
+    def choose(masks, values):
+        return jnp.where(masks[0], values[0], jnp.where(masks[1], values[1], jnp.where(masks[2], values[2], values[3])))
+
+    def one(z, j, c):
         part = slice(c * LANES, (c + 1) * LANES)
-        k = k_ref[z, i, :, part]
-        nbx = turn(k, -lv.step)
-        nby = k_ref[z, i + 1, :, part] if i < s - 1 else turn(k_ref[z, 0, :, part], -1, 0)
-        nbz = k_ref[z + 1, i, :, part]
+        k = k_ref[z, j, :, part]
+        nbx = jnp.where(turned_x, turn(k, 8 * (s - 1) - 1), turn(k, -8))
+        nby = k_ref[z, j + 1, :, part] if j < s - 1 else turn(k_ref[z, 0, :, part], -1, 0)
+        nbz = k_ref[z + 1, j, :, part]
         nb = jnp.where(first, nbx, jnp.where(second, nby, nbz))
         w = (2.0 * lv.spacing) * k * nb / (k + nb)
-        bad = edge_x | (second & (yo * s + i >= lv.width - 1))
-        return jnp.where(bad, 0.0, w)
-
-    def planes(t, _):
-        units = [(2 * t + n, i) for n in range(2) for i in range(s)]
-        for e in range(EZ):
-            made = []
-            for plane, i in units:
-                z = jnp.clip(e * lv.edz + plane + 1 - lv.mz, 0, lv.levels - 1)
-                w0, w1 = one(z, i, 0), one(z, i, 1)
-                near, wrap = turn(w1, 40), turn(w1, 48)
-                made.append((jnp.where(first, w0, near), jnp.where(third, near, w0), jnp.where(third, w0, wrap)))
-            for p in range(s):
-                for m in range(3):
-                    both = jnp.concatenate([made[2 * p][m], made[2 * p + 1][m]], axis=0)
-                    high = both.astype(BF16)
-                    part = slice(e * LANES, (e + 1) * LANES)
-                    high_refs[m][t * s + p, :, part] = high
-                    low_refs[m][t * s + p, :, part] = (both - high.astype(F32)).astype(BF16)
+        return jnp.where(edge_x | (second & (yo * s + j >= lv.width - 1)), 0.0, w)
+
+    def plane(number, _):
+        for j in range(s):
+            parts = []
+            for e in range(EZ):
+                z = jnp.clip(e * lv.edz + number + 1 - lv.mz, 0, lv.levels - 1)
+                for c in range(COLUMNS):
+                    parts.append(turn(one(z, j, c), 8 * len(parts)))
+            for low in range(4):
+                mixed = choose([quarter[(low + t) % 4] for t in range(4)], parts)
+                mixed = turn(mixed, -8 * low) if low else mixed
+                shifted = [mixed] + [turn(mixed, 32 * t) for t in range(1, 4)]
+                for w in range(4):
+                    target = low + 4 * w
+                    if target < 3 * s:
+                        value = choose([block[(w + t) % 4] for t in range(4)], shifted)
+                        w_refs[target // s][target % s, number * s + j] = value
         return 0
 
-    lax.fori_loop(0, lv.planes // 2, planes, 0)
-    rows = lv.planes * s * SUBS
-    row = lax.broadcasted_iota(jnp.int32, (2 * LANES, 2 * LANES), 0)
-    lane = lax.broadcasted_iota(jnp.int32, (1, 2 * LANES), 1)
-    upper = lane // LANES
-    for q in range(-(-s // 2)):
-        x = lane % 8 * s + 2 * q + upper
-        valid = (x < lv.width) & (2 * q + upper < s)
-        for m in range(3):
-            segment = jnp.where(lane // 8 % 2 == 0, m, (m + 1) % 3)
-            source = jnp.where(valid, lane // 16 % 2 * LANES + segment * 40 + lv.step * x, -1)
-            pick = (row == source).astype(F32).astype(BF16)
-            out = jnp.dot(high_refs[m][...].reshape(rows, 2 * LANES), pick, preferred_element_type=F32)
-            out = out + jnp.dot(low_refs[m][...].reshape(rows, 2 * LANES), pick, preferred_element_type=F32)
-            for half in range(min(2, s - 2 * q)):
-                part = out[:, half * LANES : (half + 1) * LANES]
-                w_refs[m][2 * q + half] = part.reshape(lv.planes * s, SUBS, LANES)
+    lax.fori_loop(0, lv.inner + 1, plane, 0)
 
 
 class Case:
@@ -213,8 +200,12 @@
 HALVES = (0, 1)
 
 
+def plane_rows(lv):
+    return (lv.tiles + lv.seg) * SUBS
+
+
 def phi_rows(lv):
-    return lv.edz * (lv.tiles + lv.seg) * SUBS
+    return lv.edz * plane_rows(lv)
 
 
 def turned_tiles(lv):
@@ -360,7 +351,7 @@
     return looped(lv.inner, group, 2, step)
 
 
-def finish(case, group, alphas, phi_ref):
+def finish(case, group, alphas, phi_ref, send):
     lv, cs, s = case.lv, case.cs, case.lv.seg
     n = lv.tiles
     corner, element, _, _ = lane_parts()
@@ -379,7 +370,7 @@
             values.append(value)
         total = values[0] + turn(values[0], 32)
         chosen = jnp.where(lower, values[1], values[0])
-        at = pl.multiple_of((z * n + k) * SUBS, SUBS)
+        at = pl.multiple_of(z * plane_rows(lv) + k * SUBS, SUBS)
         phi_ref[pl.ds(at, SUBS), :] = chosen
         return chosen, total + turn(total, 64)
 
@@ -389,7 +380,7 @@
             packed = jnp.where(corner == i, totals[i], packed)
         if s > 4:
             packed = jnp.where(lower, packed, turn(totals[4], 16))
-        at = pl.multiple_of((lv.edz * n + z * s + j) * SUBS, SUBS)
+        at = pl.multiple_of(z * plane_rows(lv) + (n + j) * SUBS, SUBS)
         phi_ref[pl.ds(at, SUBS), :] = packed
 
     gz = cs.fz(lv.mz)
@@ -442,6 +433,8 @@
             u, low = after, after_low
         for k in range(n):
             case.fz[k], case.chosen[k], case.total[k] = flux_z[k], u[k], low[k]
+        for z in [z0 + t for t in range(group)]:
+            send(z).start()
         return [tree(total) for total in sums]
 
     return looped(lv.edz, group, 4, step)
@@ -461,35 +454,51 @@
 def solve_kernel(
     inside, x_low, x_high, y_low, y_high,
     phi, message,
-    flat, sides, rows, pairs, twin_rows, *refs,
+    flat, rows, twin_pairs, pairs, twin_rows, *refs,
 ):
     lanes = inside.shape[1]
     rim = y_low.shape[2]
     wide = y_low.shape[1]
-    for m in range(3):
-        off = m * wide
-        flat[off : off + MX, :] = x_low[m]
-        flat[off + wide - MX : off + wide, :] = x_high[m]
-        sides[off : off + wide, :rim] = y_low[m]
-        sides[off : off + wide, rim:] = y_high[m]
-    sides[3 * wide :, :] = jnp.ones((LANES - 3 * wide, sides.shape[1]), F32)
+    edge_tiles, inner_tiles = rim // LANES, lanes // LANES
+    used = 3 * wide
     row = sub_iota((LANES, LANES))
-    place = row % wide
-    outer = (row < 3 * wide) & ((place < MX) | (place >= wide - MX))
-    for t in range(rim // LANES):
-        low, high = slice(t * LANES, (t + 1) * LANES), slice(rim + t * LANES, rim + (t + 1) * LANES)
-        rows[low, :] = sides[:, low].T
-        rows[lanes + rim + t * LANES : lanes + rim + (t + 1) * LANES, :] = sides[:, high].T
-    for t in range(lanes // LANES):
+    outer = (row < used) & ((row % wide < MX) | (row % wide >= wide - MX))
+    for t in range(2 * edge_tiles + inner_tiles):
+        if edge_tiles <= t < edge_tiles + inner_tiles:
+            part = slice((t - edge_tiles) * LANES, (t - edge_tiles + 1) * LANES)
+            for m in range(3):
+                flat[t, m * wide : m * wide + MX, :] = x_low[m, :, part]
+                flat[t, (m + 1) * wide - MX : (m + 1) * wide, :] = x_high[m, :, part]
+            flat[t] = jnp.where(outer, flat[t], inside[:, part])
+        else:
+            source = y_low if t < edge_tiles else y_high
+            at = t if t < edge_tiles else t - edge_tiles - inner_tiles
+            for m in range(3):
+                flat[t, m * wide : (m + 1) * wide, :] = source[m, :, at * LANES : (at + 1) * LANES]
+            flat[t, used:, :] = jnp.ones((LANES - used, LANES), F32)
+
+    def ordered(lv, t):
+        parts = []
+        for m in range(3):
+            for i in range(lv.seg):
+                some = [
+                    flat[t, pl.ds(m * wide + lv.step * i + n, SUBS, stride=lv.step * lv.seg), :]
+                    for n in range(lv.step)
+                ]
+                parts.append(tree(some))
+        parts.append(jnp.ones((LANES - len(parts) * SUBS, LANES), F32))
+        return jnp.concatenate(parts, axis=0)
+
+    for t in range(flat.shape[0]):
         part = slice(t * LANES, (t + 1) * LANES)
-        rows[rim + t * LANES : rim + (t + 1) * LANES, :] = jnp.where(outer, flat[:, part], inside[:, part]).T
+        rows[part, :] = ordered(FINE, t).T
+        twin_pairs[part, :] = ordered(TWIN, t).T
 
     nz = EZ * ELZ
     twin_y = rows.shape[0] // nz // 2
     for y in range(twin_y):
-        both = rows[2 * y * nz : (2 * y + 1) * nz, :] + rows[(2 * y + 1) * nz : (2 * y + 2) * nz, :]
-        both = both + turn(both, -1)
         at = y * nz
+        both = twin_pairs[2 * at : 2 * at + nz, :] + twin_pairs[2 * at + nz : 2 * at + 2 * nz, :]
         pairs[at : at + nz, :] = both
         twin_rows[at : at + 8, :] = jnp.broadcast_to(0.25 * both[0:1], (8, LANES))
         twin_rows[at + 8 + nz // 2 : at + nz, :] = jnp.broadcast_to(0.25 * both[nz - 1 : nz], (8, LANES))
@@ -509,14 +518,14 @@
     cases = []
     for lv, source in zip(LEVELS, (rows, twin_rows)):
         (k_ref,) = take(1)
-        high_refs, low_refs, w_refs = take(3), take(3), take(3)
+        w_refs = take(3)
         for z in range(lv.levels + 1):
             cell = min(max(z - 1, 0), nz - 1) if lv is FINE else min(z, lv.levels - 1) + 7
             for i in range(lv.seg):
                 for c in range(COLUMNS):
                     start = (lv.edge * c + i) * nz + cell
                     k_ref[z, i, :, c * LANES : (c + 1) * LANES] = source[pl.ds(start, SUBS, stride=lv.seg * nz), :]
-        spread_weights(lv, k_ref, high_refs, low_refs, w_refs)
+        spread_weights(lv, k_ref, w_refs)
         case = Case(lv, w_refs, take(5), take(3))
         for k in range(2 * lv.tiles):
             case.d[0][lv.inner, k] = jnp.zeros((SUBS, LANES), F32)
@@ -541,9 +550,19 @@
             betas = [[a / b for a, b in zip(new[n], rr[n])] for n in range(len(LEVELS))]
             rr = new
 
-    split = phi.shape[0] - phi_rows(TWIN)
-    phis = (phi.at[pl.ds(0, split)], phi.at[pl.ds(split, phi_rows(TWIN))])
-    totals = both_levels(lambda n, case, group: finish(case, group, alphas[n], phis[n]))
+    phis, sems = take(2), take(2)
+
+    def send(n, z):
+        lv = LEVELS[n]
+        size = plane_rows(lv)
+        first = sum(phi_rows(v) for v in LEVELS[:n])
+        return pltpu.make_async_copy(
+            phis[n].at[pl.ds(pl.multiple_of(z * size, SUBS), size)],
+            phi.at[pl.ds(pl.multiple_of(first + z * size, SUBS), size)],
+            sems[n].at[z],
+        )
+
+    totals = both_levels(lambda n, case, group: finish(case, group, alphas[n], phis[n], functools.partial(send, n)))
     _, element, _, slot = lane_parts()
     packed = []
     for level in totals:
@@ -555,6 +574,9 @@
     row = jnp.where(element == 0, packed[0], packed[1])
     for r in range(0, message.shape[0], SUBS):
         message[r : r + SUBS, :] = row
+    for n, lv in enumerate(LEVELS):
+        for z in range(lv.edz):
+            send(n, z).wait()
 
 
 def coarse_nodes(gathered, gy_count, me):
@@ -635,14 +657,14 @@
         s = lv.seg
         nz = EZ * lv.edz
         per = LANES // nz
-        sums_row = start_row + lv.edz * lv.tiles * SUBS
+        sums_row = start_row + lv.tiles * SUBS
         for i in range(s):
             for t in range(turned_tiles(lv)):
                 parts = []
                 for n in range(per):
                     yo, j = divmod(lv.mx + t * per + n, s)
-                    chosen = phi[pl.ds(start_row + (i * s + j) * SUBS + yo, lv.edz, stride=lv.tiles * SUBS), :]
-                    total = phi[pl.ds(sums_row + j * SUBS + yo, lv.edz, stride=s * SUBS), :]
+                    chosen = phi[pl.ds(start_row + (i * s + j) * SUBS + yo, lv.edz, stride=plane_rows(lv)), :]
+                    total = phi[pl.ds(sums_row + j * SUBS + yo, lv.edz, stride=plane_rows(lv)), :]
                     lower = lane_iota(chosen.shape) // 16 % 2 == 0
                     parts.append(jnp.where(lower, chosen, turn(total, 16) if i < 4 else total))
                     parts.append(jnp.where(lower, turn(chosen, -16), 0.0))
@@ -702,19 +724,20 @@
     halos = [x_low, x_high, y_low, y_high]
     flat_lanes = lanes + 2 * rim
     scratch = [
-        vmem((LANES, lanes)),
-        vmem((LANES, 2 * rim)),
+        vmem((flat_lanes // LANES, LANES, LANES)),
+        vmem((flat_lanes, LANES)),
         vmem((flat_lanes, LANES)),
         vmem((flat_lanes // 2, LANES)),
         vmem((SUBS * (TWIN.seg + 2) * nz, LANES)),
     ]
     for lv in LEVELS:
         scratch.append(vmem((lv.levels + 1, lv.seg, SUBS, 2 * LANES)))
-        scratch += [vmem((lv.planes * lv.seg // 2, 2 * SUBS, 2 * LANES), BF16)] * 6
         scratch += [vmem((lv.seg, lv.planes * lv.seg, SUBS, LANES))] * 3
         scratch += [vmem((lv.inner + 1, 2 * lv.tiles, SUBS, LANES))] * 5
         scratch.append(vmem((2 * lv.tiles, SUBS, LANES)))
         scratch += [vmem((lv.tiles, SUBS, LANES))] * 2
+    scratch += [vmem((phi_rows(lv), LANES)) for lv in LEVELS]
+    scratch += [pltpu.SemaphoreType.DMA((lv.edz,)) for lv in LEVELS]
     full = pl.BlockSpec(memory_space=pltpu.VMEM)
     inside = pl.pallas_call(
         place_kernel,
@@ -728,11 +751,11 @@
     phi, message = pl.pallas_call(
         solve_kernel,
         out_shape=[
-            vmem((sum(phi_rows(lv) for lv in LEVELS), LANES)),
+            pltpu.HBM((sum(phi_rows(lv) for lv in LEVELS), LANES), F32),
             jax.ShapeDtypeStruct((gx * gy, LANES), F32),
         ],
         in_specs=[full] * 5,
-        out_specs=[full] * 2,
+        out_specs=[pl.BlockSpec(memory_space=pltpu.HBM), full],
         scratch_shapes=scratch,
         compiler_params=pltpu.CompilerParams(vmem_limit_bytes=44 * 1024 * 1024),
         name="solve",

time: 61.1 us -> 65.6 us (1.074)
  Pallas kernels: 33.2 us -> 39.3 us
  local copies, waits for them, and re-layouts: 6.1 us -> 4.69 us
    pallas_call x1, Pallas kernels: 29.2 us -> 35.2 us  [shards(): pl.pallas_call(solve_kernel, out_shape=[pltpu.HBM((sum((phi_rows(lv) for...]
    unnamed x6 -> x4, local copies, waits for them, and re-layouts: 4.21 us -> 2.79 us
where the time goes in v6:
time: 65.6 us; the launch traced here: 65.4 us
  Pallas kernels  39.3 us (60%)
  starting transfers between devices  12.8 us (20%)
  waiting for transfers between devices  7.82 us (12%)
  local copies, waits for them, and re-layouts  4.69 us (7%)
  between operations  0.69 us (1%)
    pallas_call x1, Pallas kernels, shards(): pl.pallas_call(solve_kernel, out_shape=[pltpu.HBM((sum((phi_rows(lv) for...  35.2 us
    ppermute x4, starting transfers between devices, sent(): lax.ppermute(value, axis, [(i, (i + shift) % count) for i in range(count)])  7.9 us
    all_to_all x1, starting transfers between devices, shards(): gathered = lax.all_to_all(message, ('gx', 'gy'), 0, 0, tiled=True)  4.95 us
    ppermute x4, waiting for transfers between devices, sent(): lax.ppermute(value, axis, [(i, (i + shift) % count) for i in range(count)])  4.07 us
    all_to_all x1, waiting for transfers between devices, shards(): gathered = lax.all_to_all(message, ('gx', 'gy'), 0, 0, tiled=True)  3.75 us
    unnamed x4, local copies, waits for them, and re-layouts  2.79 us
    pallas_call x1, Pallas kernels, shards(): pl.pallas_call(functools.partial(pressure_kernel, gy), out_shape=[jax.Sha...  2.36 us
    pallas_call x1, Pallas kernels, shards(): pl.pallas_call(turn_kernel, out_shape=vmem((tiles, LANES, LANES)), in_spe...  1.65 us
  transfers between devices with their start and end apart: 5, of which 4 were waited for; matrix products, arithmetic and copies ran while one was open for 1% of the time, Pallas kernels for 3%

profile of v6, /device:TPU:0, one launch (start us, length us, event | category | flops | bytes accessed | tf_op | source)
XLA Modules:
  0.0 65.4 jit_solution(17735794410997547674)
XLA Ops:
  0.6 1.1 %fusion.1 = (f32[3,4,2048]{2,1,0:T(4,128)S(1)}, f32[3,4,2048]{2,1,0:T(4,128)S(1)}) fusion(f32[3,32,2048]{2,1,0:T(8,128)} %center.1), kind=kLoop, calls=%fused_computation.3 | loop fusion | bytes 393216 | tf_op jit(solution)/shard_map/slice | solution.py:717
  1.7 3.1 %collective-permute-start = (f32[3,4,2048]{2,1,0:T(4,128)S(1)}, f32[3,4,2048]{2,1,0:T(4,128)S(1)}, u32[]{:S(2)}, u32[]{:S(2)}) collective-permute-start(f32[3,4,2048]{2,1,0:T(4,128)S(1)} %get-tuple-element.9), channel_id=1, source_target_pairs={{0,8},{8,16},{16,24},{24,0},{1,9},{9,17},{17,25},{25,1},{2,10},{10... | collective-permute-start | bytes 294920 | tf_op jit(solution)/shard_map/ppermute | solution.py:714
  4.8 2.1 %collective-permute-start.1 = (f32[3,4,2048]{2,1,0:T(4,128)S(1)}, f32[3,4,2048]{2,1,0:T(4,128)S(1)}, u32[]{:S(2)}, u32[]{:S(2)}) collective-permute-start(f32[3,4,2048]{2,1,0:T(4,128)S(1)} %get-tuple-element.8), channel_id=1, source_target_pairs={{0,24},{8,0},{16,8},{24,16},{1,25},{9,1},{17,9},{25,17},{2,26},{10... | collective-permute-start | bytes 294920 | tf_op jit(solution)/shard_map/ppermute | solution.py:714
  6.9 0.8 %fusion = (f32[3,32,128]{2,1,0:T(8,128)S(1)}, f32[3,32,128]{2,1,0:T(8,128)S(1)}) fusion(f32[3,32,2048]{2,1,0:T(8,128)} %center.1), kind=kLoop, calls=%fused_computation.2 | loop fusion | bytes 196608 | tf_op jit(solution)/shard_map/slice | solution.py:720
  7.7 2.6 %collective-permute-done.x_low = f32[3,4,2048]{2,1,0:T(4,128)S(1)} collective-permute-done((f32[3,4,2048]{2,1,0:T(4,128)S(1)}, f32[3,4,2048]{2,1,0:T(4,128)S(1)}, u32[]{:S(2)}, u32[]{:S(2)}) %collective-permute-start) | collective-permute-done | bytes 98336 | tf_op jit(solution)/shard_map/ppermute | solution.py:714
  10.3 0.8 %collective-permute-done.1.x_high = f32[3,4,2048]{2,1,0:T(4,128)S(1)} collective-permute-done((f32[3,4,2048]{2,1,0:T(4,128)S(1)}, f32[3,4,2048]{2,1,0:T(4,128)S(1)}, u32[]{:S(2)}, u32[]{:S(2)}) %collective-permute-start.1) | collective-permute-done | bytes 98336 | tf_op jit(solution)/shard_map/ppermute | solution.py:714
  11.1 0.1 collective-permute-start.2
  11.2 2.7 %collective-permute-start.3 = (f32[3,40,128]{2,1,0:T(8,128)S(1)}, f32[3,40,128]{2,1,0:T(8,128)S(1)}, u32[]{:S(2)}, u32[]{:S(2)}) collective-permute-start(f32[3,40,128]{2,1,0:T(8,128)S(1)} %pad_maximum_fusion.1), channel_id=1, source_target_pairs={{0,7},{1,0},{2,1},{3,2},{4,3},{5,4},{6,5},{7,6},{8,15},{9,8},{10,9... | collective-permute-start | bytes 184328 | tf_op jit(solution)/shard_map/ppermute | solution.py:714
  13.9 0.0 copy-start.1
  13.9 1.1 %copy-done.1 = f32[3,32,2048]{2,1,0:T(8,128)S(1)} copy-done((f32[3,32,2048]{2,1,0:T(8,128)S(1)}, f32[3,32,2048]{2,1,0:T(8,128)}, u32[]{:S(2)}) %copy-start.1) | copy-done | bytes 786456
  15.0 0.1 place.1.inside
  15.1 0.6 collective-permute-done.2.y_low
  15.7 0.0 collective-permute-done.3.y_high
  15.8 35.2 %solve.1 = (f32[4608,128]{1,0:T(8,128)}, f32[32,128]{1,0:T(8,128)}) custom-call(f32[128,2048]{1,0:T(8,128)S(1)} %place.1.inside, f32[3,4,2048]{2,1,0:T(4,128)S(1)} %collective-permute-done.x_low, f32[3,4,2048]{2,1,0:T(4,128)S(1)} %collective-permute-done.1.x_high, f32[3,40,128]{2,1,0:T(8,128)S(1)} %collective-permute-done.2.y_low, ...), custom_call_target="tpu_custom_call" | custom-call | tf_op jit(solution)/shard_map/solve/pallas_call | solution.py:751
  51.0 4.9 %all-to-all-start = ((f32[32,1,128]{2,1,0:T(1,128)}), f32[32,1,128]{2,1,0:T(1,128)S(1)}, u32[]{:S(2)}, u32[]{:S(2)}) async-start(f32[32,1,128]{2,1,0:T(1,128)} %bitcast.2), calls=%async_computation | async-start | bytes 32768 | tf_op jit(solution)/shard_map/all_to_all | solution.py:763
  55.9 0.0 copy-start
  55.9 1.7 %copy-done = f32[4608,128]{1,0:T(8,128)S(1)} copy-done((f32[4608,128]{1,0:T(8,128)S(1)}, f32[4608,128]{1,0:T(8,128)}, u32[]{:S(2)}) %copy-start) | copy-done | bytes 2359320
  57.6 1.6 %turned.1 = f32[46,128,128]{2,1,0:T(8,128)S(1)} custom-call(f32[4608,128]{1,0:T(8,128)S(1)} %copy-done), custom_call_target="tpu_custom_call" | custom-call | flops 4000000 | bytes 8000000 | tf_op jit(solution)/shard_map/turned/pallas_call | solution.py:765
  59.2 3.7 %all-to-all-done = f32[32,1,128]{2,1,0:T(1,128)S(1)} async-done(((f32[32,1,128]{2,1,0:T(1,128)}), f32[32,1,128]{2,1,0:T(1,128)S(1)}, u32[]{:S(2)}, u32[]{:S(2)}) %all-to-all-start) | async-done | bytes 16416 | tf_op jit(solution)/shard_map/all_to_all | solution.py:763
  63.0 2.4 %pressure.1 = (f32[32,2048]{1,0:T(8,128)}, f32[16,512]{1,0:T(8,128)}) custom-call(s32[1]{0:T(128)} %bitcast.me_ref, f32[32,128]{1,0:T(8,128)S(1)} %bitcast.5, f32[46,128,128]{2,1,0:T(8,128)S(1)} %turned.1), custom_call_target="tpu_custom_call" | custom-call | tf_op jit(solution)/shard_map/pressure/pallas_call | solution.py:776
  (4 shorter events, 0.0 us)
Async XLA Ops:
  1.7 8.6 %collective-permute-start = (f32[3,4,2048]{2,1,0:T(4,128)S(1)}, f32[3,4,2048]{2,1,0:T(4,128)S(1)}, u32[]{:S(2)}, u32[]{:S(2)}) collective-permute-start(f32[3,4,2048]{2,1,0:T(4,128)S(1)} %get-tuple-element.9), channel_id=1, source_target_pairs={{0,8},{8,16},{16,24},{24,0},{1,9},{9,17},{17,25},{25,1},{2,10},{10... | collective-permute-start | bytes 294920 | tf_op jit(solution)/shard_map/ppermute | solution.py:714
  4.8 6.4 %collective-permute-start.1 = (f32[3,4,2048]{2,1,0:T(4,128)S(1)}, f32[3,4,2048]{2,1,0:T(4,128)S(1)}, u32[]{:S(2)}, u32[]{:S(2)}) collective-permute-start(f32[3,4,2048]{2,1,0:T(4,128)S(1)} %get-tuple-element.8), channel_id=1, source_target_pairs={{0,24},{8,0},{16,8},{24,16},{1,25},{9,1},{17,9},{25,17},{2,26},{10... | collective-permute-start | bytes 294920 | tf_op jit(solution)/shard_map/ppermute | solution.py:714
  11.1 4.6 %collective-permute-start.2 = (f32[3,40,128]{2,1,0:T(8,128)S(1)}, f32[3,40,128]{2,1,0:T(8,128)S(1)}, u32[]{:S(2)}, u32[]{:S(2)}) collective-permute-start(f32[3,40,128]{2,1,0:T(8,128)S(1)} %pad_maximum_fusion), channel_id=1, source_target_pairs={{0,1},{1,2},{2,3},{3,4},{4,5},{5,6},{6,7},{7,0},{8,9},{9,10},{10,1... | collective-permute-start | bytes 184328 | tf_op jit(solution)/shard_map/ppermute | solution.py:714
  11.2 4.5 %collective-permute-start.3 = (f32[3,40,128]{2,1,0:T(8,128)S(1)}, f32[3,40,128]{2,1,0:T(8,128)S(1)}, u32[]{:S(2)}, u32[]{:S(2)}) collective-permute-start(f32[3,40,128]{2,1,0:T(8,128)S(1)} %pad_maximum_fusion.1), channel_id=1, source_target_pairs={{0,7},{1,0},{2,1},{3,2},{4,3},{5,4},{6,5},{7,6},{8,15},{9,8},{10,9... | collective-permute-start | bytes 184328 | tf_op jit(solution)/shard_map/ppermute | solution.py:714
  13.9 1.1 %copy-start.1 = (f32[3,32,2048]{2,1,0:T(8,128)S(1)}, f32[3,32,2048]{2,1,0:T(8,128)}, u32[]{:S(2)}) copy-start(f32[3,32,2048]{2,1,0:T(8,128)} %center.1) | copy-start | bytes 2359300
  51.0 12.0 %all-to-all-start = ((f32[32,1,128]{2,1,0:T(1,128)}), f32[32,1,128]{2,1,0:T(1,128)S(1)}, u32[]{:S(2)}, u32[]{:S(2)}) async-start(f32[32,1,128]{2,1,0:T(1,128)} %bitcast.2), calls=%async_computation | async-start | bytes 32768 | tf_op jit(solution)/shard_map/all_to_all | solution.py:763
  55.9 1.7 %copy-start = (f32[4608,128]{1,0:T(8,128)S(1)}, f32[4608,128]{1,0:T(8,128)}, u32[]{:S(2)}) copy-start(f32[4608,128]{1,0:T(8,128)} %get-tuple-element.5.phi) | copy-start | bytes 7077892

commit v7 on v5

--- a/solution.py
+++ b/solution.py
@@ -203,7 +203,7 @@
     def __init__(self, lv, w_refs, fields, planes):
         self.lv, self.cs, self.w_refs = lv, Consts(lv), w_refs
         self.d, self.q, self.r = fields[:3], fields[3], fields[4]
-        self.fz, self.chosen, self.total = planes
+        (self.fz,) = planes
 
     def weights(self, plane):
         s = self.lv.seg
@@ -211,10 +211,19 @@
 
 
 HALVES = (0, 1)
-
-
-def phi_rows(lv):
-    return lv.edz * (lv.tiles + lv.seg) * SUBS
+CHUNK = 640
+
+
+def plane_rows(lv):
+    return lv.tiles * SUBS
+
+
+def field_rows(lv):
+    return lv.edz * plane_rows(lv)
+
+
+def padded_rows(lv):
+    return -(-field_rows(lv) // CHUNK) * CHUNK
 
 
 def turned_tiles(lv):
@@ -360,11 +369,14 @@
     return looped(lv.inner, group, 2, step)
 
 
-def finish(case, group, alphas, phi_ref):
+def finish(case, group, alphas, refs, send):
     lv, cs, s = case.lv, case.cs, case.lv.seg
     n = lv.tiles
-    corner, element, _, _ = lane_parts()
-    lower = element == 0
+    f_ref, p_ref, y_ref = refs
+    lower = lane_parts()[1] == 0
+
+    def at(z, k):
+        return pl.ds(pl.multiple_of(z * plane_rows(lv) + k * SUBS, SUBS), SUBS)
 
     def fresh(z, i, j, gz):
         k = i * s + j
@@ -375,45 +387,34 @@
             value = both * gz[h]
             for alpha, d_ref in zip(alphas[h], case.d):
                 value = value + alpha * d_ref[inner, h * n + k]
-            value = cs.masked(value, i, j, 1)
-            values.append(value)
-        total = values[0] + turn(values[0], 32)
+            values.append(cs.masked(value, i, j, 1))
         chosen = jnp.where(lower, values[1], values[0])
-        at = pl.multiple_of((z * n + k) * SUBS, SUBS)
-        phi_ref[pl.ds(at, SUBS), :] = chosen
-        return chosen, total + turn(total, 64)
-
-    def pack(z, j, totals):
-        packed = totals[0]
-        for i in range(1, min(s, 4)):
-            packed = jnp.where(corner == i, totals[i], packed)
-        if s > 4:
-            packed = jnp.where(lower, packed, turn(totals[4], 16))
-        at = pl.multiple_of((lv.edz * n + z * s + j) * SUBS, SUBS)
-        phi_ref[pl.ds(at, SUBS), :] = packed
+        f_ref[at(z, k), :] = chosen
+        p_ref[at(z, k), :] = values[0]
+        return chosen
 
     gz = cs.fz(lv.mz)
     for i in range(s):
         for j in range(s):
-            k = i * s + j
-            case.chosen[k], case.total[k] = fresh(0, i, j, gz)
-            case.fz[k] = jnp.zeros((SUBS, LANES), F32)
-    for j in range(s):
-        pack(0, j, [case.total[i * s + j] for i in range(s)])
+            fresh(0, i, j, gz)
+            case.fz[i * s + j] = jnp.zeros((SUBS, LANES), F32)
+    rest = padded_rows(lv) - field_rows(lv)
+    if rest:
+        for ref in refs:
+            ref[field_rows(lv) :, :] = jnp.zeros((rest, LANES), F32)
 
     def cut(values, table):
         return [v if f is None else v * f for v, f in zip(values, table)]
 
-    def step(z0):
-        sums = [[] for _ in range(4)]
-        u = [case.chosen[k] for k in range(n)]
-        low = [case.total[k] for k in range(n)]
+    def body(t, _):
+        z0 = t * group
+        u = [f_ref[at(z0, k), :] for k in range(n)]
         flux_z = [case.fz[k] for k in range(n)]
-        for z in [z0 + t for t in range(group)]:
+        for z in [z0 + m for m in range(group)]:
             get = case.weights(z + lv.mz)
             up = jnp.minimum(z + 1, lv.edz - 1)
             gz = cs.fz(up + lv.mz)
-            after, after_low = [None] * n, [None] * n
+            after = [None] * n
             last = [get(1, i, s - 1) * (u[i * s + s - 1] - turn(u[i * s], -1, 0)) for i in range(s)]
             last = cut(last, [cs.facey[s - 1]] * s)
             before = [turn(v, 1, 0) for v in last]
@@ -423,28 +424,42 @@
                 flux_y = last
                 if j < s - 1:
                     flux_y = cut([get(1, i, j) * jump_y[i] for i in range(s)], [cs.facey[j]] * s)
-                parts = [[] for _ in sums]
                 for i in range(s):
                     k = i * s + j
-                    after[k], after_low[k] = fresh(up, i, j, gz)
+                    after[k] = fresh(up, i, j, gz)
                     flux = get(2, i, j) * (u[k] - after[k])
                     prev_x = flux_x[i - 1] if i else turn(flux_x[s - 1], 1)
-                    value = (flux_x[i] - prev_x) + (flux_y[i] - before[i]) + (flux - flux_z[k])
+                    y_ref[at(z, k), :] = (flux_x[i] - prev_x) + (flux_y[i] - before[i]) + (flux - flux_z[k])
                     flux_z[k] = flux
-                    parts[0].append(value * u[k])
-                    parts[1].append(value * turn(u[k], -32))
-                    parts[2].append(value * turn(u[k], 64))
-                    parts[3].append(value * low[k])
-                pack(up, j, [after_low[i * s + j] for i in range(s)])
-                for total, part in zip(sums, parts):
-                    total.append(tree(part))
                 before = flux_y
-            u, low = after, after_low
+            u = after
         for k in range(n):
-            case.fz[k], case.chosen[k], case.total[k] = flux_z[k], u[k], low[k]
-        return [tree(total) for total in sums]
-
-    return looped(lv.edz, group, 4, step)
+            case.fz[k] = flux_z[k]
+        for z in [z0 + m for m in range(group)]:
+            for h in HALVES:
+                send(h, z).start()
+        return 0
+
+    lax.fori_loop(0, lv.edz // group, body, 0)
+    pairs = jnp.zeros((2 * LANES, LANES), F32)
+    for start in range(0, padded_rows(lv), CHUNK):
+        part = slice(start, start + CHUNK)
+        left = jnp.concatenate([f_ref[part, :].T, p_ref[part, :].T], axis=0)
+        right = y_ref[part, :]
+        left_high, right_high = left.astype(BF16), right.astype(BF16)
+        left_low = (left - left_high.astype(F32)).astype(BF16)
+        right_low = (right - right_high.astype(F32)).astype(BF16)
+        for a, b in ((left_high, right_high), (left_low, right_high), (left_high, right_low)):
+            pairs = pairs + jnp.dot(a, b, preferred_element_type=F32)
+    shape = (LANES, LANES)
+    row, lane = sub_iota(shape), lane_iota(shape)
+    sums = [jnp.where(row == (lane + 32 * k) % LANES, pairs[:LANES], 0.0) for k in range(3)]
+    sums.append(jnp.where(row % 32 == lane % 32, pairs[LANES:], 0.0))
+    out = []
+    for value in sums:
+        value = tree([value[r : r + SUBS] for r in range(0, LANES, SUBS)])
+        out.append(value)
+    return out
 
 
 GROUPS = {FINE: 1, TWIN: 8}
@@ -517,7 +532,7 @@
                     start = (lv.edge * c + i) * nz + cell
                     k_ref[z, i, :, c * LANES : (c + 1) * LANES] = source[pl.ds(start, SUBS, stride=lv.seg * nz), :]
         spread_weights(lv, k_ref, high_refs, low_refs, w_refs)
-        case = Case(lv, w_refs, take(5), take(3))
+        case = Case(lv, w_refs, take(5), take(1))
         for k in range(2 * lv.tiles):
             case.d[0][lv.inner, k] = jnp.zeros((SUBS, LANES), F32)
             case.r[lv.inner, k] = jnp.zeros((SUBS, LANES), F32)
@@ -541,9 +556,22 @@
             betas = [[a / b for a, b in zip(new[n], rr[n])] for n in range(len(LEVELS))]
             rr = new
 
-    split = phi.shape[0] - phi_rows(TWIN)
-    phis = (phi.at[pl.ds(0, split)], phi.at[pl.ds(split, phi_rows(TWIN))])
-    totals = both_levels(lambda n, case, group: finish(case, group, alphas[n], phis[n]))
+    results = [take(3), take(3)]
+    sems = take(2)
+
+    def send(n, h, z):
+        lv = LEVELS[n]
+        size = plane_rows(lv)
+        first = sum(2 * field_rows(v) for v in LEVELS[:n]) + h * field_rows(lv)
+        return pltpu.make_async_copy(
+            results[n][h].at[pl.ds(pl.multiple_of(z * size, SUBS), size)],
+            phi.at[pl.ds(pl.multiple_of(first + z * size, SUBS), size)],
+            sems[n].at[h * lv.edz + z],
+        )
+
+    totals = both_levels(
+        lambda n, case, group: finish(case, group, alphas[n], results[n], functools.partial(send, n))
+    )
     _, element, _, slot = lane_parts()
     packed = []
     for level in totals:
@@ -555,6 +583,10 @@
     row = jnp.where(element == 0, packed[0], packed[1])
     for r in range(0, message.shape[0], SUBS):
         message[r : r + SUBS, :] = row
+    for n, lv in enumerate(LEVELS):
+        for h in HALVES:
+            for z in range(lv.edz):
+                send(n, h, z).wait()
 
 
 def coarse_nodes(gathered, gy_count, me):
@@ -635,20 +667,21 @@
         s = lv.seg
         nz = EZ * lv.edz
         per = LANES // nz
-        sums_row = start_row + lv.edz * lv.tiles * SUBS
         for i in range(s):
             for t in range(turned_tiles(lv)):
                 parts = []
                 for n in range(per):
                     yo, j = divmod(lv.mx + t * per + n, s)
-                    chosen = phi[pl.ds(start_row + (i * s + j) * SUBS + yo, lv.edz, stride=lv.tiles * SUBS), :]
-                    total = phi[pl.ds(sums_row + j * SUBS + yo, lv.edz, stride=s * SUBS), :]
+                    start = start_row + (i * s + j) * SUBS + yo
+                    chosen, bottom = [
+                        phi[pl.ds(start + h * field_rows(lv), lv.edz, stride=plane_rows(lv)), :] for h in HALVES
+                    ]
                     lower = lane_iota(chosen.shape) // 16 % 2 == 0
-                    parts.append(jnp.where(lower, chosen, turn(total, 16) if i < 4 else total))
+                    parts.append(jnp.where(lower, chosen, turn(bottom, 16)))
                     parts.append(jnp.where(lower, turn(chosen, -16), 0.0))
                 out_ref[number] = jnp.concatenate(parts, axis=0).T
                 number += 1
-        start_row += phi_rows(lv)
+        start_row += 2 * field_rows(lv)
 
 
 def pressure_kernel(gy_count, me_ref, gathered, turned, fine_out, twin_out, fine_all, twin_all):
@@ -669,7 +702,7 @@
                     def part(group):
                         return turned[first + i * tiles + t, group * 16 + c * 8 : group * 16 + c * 8 + 8, :]
 
-                    value = tree([part(2 * p) * nodes[p, c] for p in range(4)]) + part(2 * (i % 4) + 1)
+                    value = tree([part(2 * p) * nodes[p, c] + part(2 * p + 1) for p in range(4)])
                     all_ref[c * tiles + t, pl.ds(i, SUBS, stride=s), :] = value
                 out_ref[:, at : at + LANES] = all_ref[c * tiles + t, lv.mx : lv.mx + lv.edge, :]
         first += s * tiles
@@ -714,7 +747,9 @@
         scratch += [vmem((lv.seg, lv.planes * lv.seg, SUBS, LANES))] * 3
         scratch += [vmem((lv.inner + 1, 2 * lv.tiles, SUBS, LANES))] * 5
         scratch.append(vmem((2 * lv.tiles, SUBS, LANES)))
-        scratch += [vmem((lv.tiles, SUBS, LANES))] * 2
+    for lv in LEVELS:
+        scratch += [vmem((padded_rows(lv), LANES))] * 3
+    scratch += [pltpu.SemaphoreType.DMA((2 * lv.edz,)) for lv in LEVELS]
     full = pl.BlockSpec(memory_space=pltpu.VMEM)
     inside = pl.pallas_call(
         place_kernel,
@@ -728,13 +763,13 @@
     phi, message = pl.pallas_call(
         solve_kernel,
         out_shape=[
-            vmem((sum(phi_rows(lv) for lv in LEVELS), LANES)),
+            pltpu.HBM((sum(2 * field_rows(lv) for lv in LEVELS), LANES), F32),
             jax.ShapeDtypeStruct((gx * gy, LANES), F32),
         ],
         in_specs=[full] * 5,
-        out_specs=[full] * 2,
+        out_specs=[pl.BlockSpec(memory_space=pltpu.HBM), full],
         scratch_shapes=scratch,
-        compiler_params=pltpu.CompilerParams(vmem_limit_bytes=44 * 1024 * 1024),
+        compiler_params=pltpu.CompilerParams(vmem_limit_bytes=50 * 1024 * 1024),
         name="solve",
     )(inside, *halos)
     gathered = lax.all_to_all(message, ("gx", "gy"), 0, 0, tiled=True)

time: 61.1 us -> 59.1 us (0.967)
  local copies, waits for them, and re-layouts: 6.1 us -> 5.12 us
    unnamed x6 -> x4, local copies, waits for them, and re-layouts: 4.21 us -> 3.22 us
    pallas_call x1, Pallas kernels: 29.2 us -> 28.6 us  [shards(): pl.pallas_call(solve_kernel, out_shape=[pltpu.HBM((sum((2 * field_rows(lv...]
where the time goes in v7:
time: 59.1 us; the launch traced here: 58.8 us
  Pallas kernels  32.7 us (55%)
  starting transfers between devices  12.8 us (22%)
  waiting for transfers between devices  7.41 us (13%)
  local copies, waits for them, and re-layouts  5.12 us (9%)
  between operations  0.7 us (1%)
    pallas_call x1, Pallas kernels, shards(): pl.pallas_call(solve_kernel, out_shape=[pltpu.HBM((sum((2 * field_rows(lv...  28.6 us
    ppermute x4, starting transfers between devices, sent(): lax.ppermute(value, axis, [(i, (i + shift) % count) for i in range(count)])  7.9 us
    all_to_all x1, starting transfers between devices, shards(): gathered = lax.all_to_all(message, ('gx', 'gy'), 0, 0, tiled=True)  4.95 us
    ppermute x4, waiting for transfers between devices, sent(): lax.ppermute(value, axis, [(i, (i + shift) % count) for i in range(count)])  4.07 us
    all_to_all x1, waiting for transfers between devices, shards(): gathered = lax.all_to_all(message, ('gx', 'gy'), 0, 0, tiled=True)  3.33 us
    unnamed x4, local copies, waits for them, and re-layouts  3.22 us
    pallas_call x1, Pallas kernels, shards(): pl.pallas_call(functools.partial(pressure_kernel, gy), out_shape=[jax.Sha...  2.38 us
    pallas_call x1, Pallas kernels, shards(): pl.pallas_call(turn_kernel, out_shape=vmem((tiles, LANES, LANES)), in_spe...  1.63 us
  transfers between devices with their start and end apart: 5, of which 4 were waited for; matrix products, arithmetic and copies ran while one was open for 1% of the time, Pallas kernels for 3%

profile of v7, /device:TPU:0, one launch (start us, length us, event | category | flops | bytes accessed | tf_op | source)
XLA Modules:
  0.0 58.8 jit_solution(15411735691591247402)
XLA Ops:
  0.6 1.1 %fusion.1 = (f32[3,4,2048]{2,1,0:T(4,128)S(1)}, f32[3,4,2048]{2,1,0:T(4,128)S(1)}) fusion(f32[3,32,2048]{2,1,0:T(8,128)} %center.1), kind=kLoop, calls=%fused_computation.3 | loop fusion | bytes 393216 | tf_op jit(solution)/shard_map/slice | solution.py:728
  1.7 3.1 %collective-permute-start = (f32[3,4,2048]{2,1,0:T(4,128)S(1)}, f32[3,4,2048]{2,1,0:T(4,128)S(1)}, u32[]{:S(2)}, u32[]{:S(2)}) collective-permute-start(f32[3,4,2048]{2,1,0:T(4,128)S(1)} %get-tuple-element.9), channel_id=1, source_target_pairs={{0,8},{8,16},{16,24},{24,0},{1,9},{9,17},{17,25},{25,1},{2,10},{10... | collective-permute-start | bytes 294920 | tf_op jit(solution)/shard_map/ppermute | solution.py:725
  4.8 2.1 %collective-permute-start.1 = (f32[3,4,2048]{2,1,0:T(4,128)S(1)}, f32[3,4,2048]{2,1,0:T(4,128)S(1)}, u32[]{:S(2)}, u32[]{:S(2)}) collective-permute-start(f32[3,4,2048]{2,1,0:T(4,128)S(1)} %get-tuple-element.8), channel_id=1, source_target_pairs={{0,24},{8,0},{16,8},{24,16},{1,25},{9,1},{17,9},{25,17},{2,26},{10... | collective-permute-start | bytes 294920 | tf_op jit(solution)/shard_map/ppermute | solution.py:725
  6.9 0.8 %fusion = (f32[3,32,128]{2,1,0:T(8,128)S(1)}, f32[3,32,128]{2,1,0:T(8,128)S(1)}) fusion(f32[3,32,2048]{2,1,0:T(8,128)} %center.1), kind=kLoop, calls=%fused_computation.2 | loop fusion | bytes 196608 | tf_op jit(solution)/shard_map/slice | solution.py:731
  7.7 2.6 %collective-permute-done.x_low = f32[3,4,2048]{2,1,0:T(4,128)S(1)} collective-permute-done((f32[3,4,2048]{2,1,0:T(4,128)S(1)}, f32[3,4,2048]{2,1,0:T(4,128)S(1)}, u32[]{:S(2)}, u32[]{:S(2)}) %collective-permute-start) | collective-permute-done | bytes 98336 | tf_op jit(solution)/shard_map/ppermute | solution.py:725
  10.3 0.8 %collective-permute-done.1.x_high = f32[3,4,2048]{2,1,0:T(4,128)S(1)} collective-permute-done((f32[3,4,2048]{2,1,0:T(4,128)S(1)}, f32[3,4,2048]{2,1,0:T(4,128)S(1)}, u32[]{:S(2)}, u32[]{:S(2)}) %collective-permute-start.1) | collective-permute-done | bytes 98336 | tf_op jit(solution)/shard_map/ppermute | solution.py:725
  11.1 0.1 collective-permute-start.2
  11.2 2.7 %collective-permute-start.3 = (f32[3,40,128]{2,1,0:T(8,128)S(1)}, f32[3,40,128]{2,1,0:T(8,128)S(1)}, u32[]{:S(2)}, u32[]{:S(2)}) collective-permute-start(f32[3,40,128]{2,1,0:T(8,128)S(1)} %pad_maximum_fusion.1), channel_id=1, source_target_pairs={{0,7},{1,0},{2,1},{3,2},{4,3},{5,4},{6,5},{7,6},{8,15},{9,8},{10,9... | collective-permute-start | bytes 184328 | tf_op jit(solution)/shard_map/ppermute | solution.py:725
  13.9 0.0 copy-start.1
  13.9 1.1 %copy-done.1 = f32[3,32,2048]{2,1,0:T(8,128)S(1)} copy-done((f32[3,32,2048]{2,1,0:T(8,128)S(1)}, f32[3,32,2048]{2,1,0:T(8,128)}, u32[]{:S(2)}) %copy-start.1) | copy-done | bytes 786456
  15.0 0.1 place.1.inside
  15.1 0.6 %collective-permute-done.2.y_low = f32[3,40,128]{2,1,0:T(8,128)S(1)} collective-permute-done((f32[3,40,128]{2,1,0:T(8,128)S(1)}, f32[3,40,128]{2,1,0:T(8,128)S(1)}, u32[]{:S(2)}, u32[]{:S(2)}) %collective-permute-start.2) | collective-permute-done | bytes 61472 | tf_op jit(solution)/shard_map/ppermute | solution.py:725
  15.7 0.0 collective-permute-done.3.y_high
  15.8 28.6 %solve.1 = (f32[7552,128]{1,0:T(8,128)}, f32[32,128]{1,0:T(8,128)}) custom-call(f32[128,2048]{1,0:T(8,128)S(1)} %place.1.inside, f32[3,4,2048]{2,1,0:T(4,128)S(1)} %collective-permute-done.x_low, f32[3,4,2048]{2,1,0:T(4,128)S(1)} %collective-permute-done.1.x_high, f32[3,40,128]{2,1,0:T(8,128)S(1)} %collective-permute-done.2.y_low, ...), custom_call_target="tpu_custom_call" | custom-call | tf_op jit(solution)/shard_map/solve/pallas_call | solution.py:763
  44.3 4.9 %all-to-all-start = ((f32[32,1,128]{2,1,0:T(1,128)}), f32[32,1,128]{2,1,0:T(1,128)S(1)}, u32[]{:S(2)}, u32[]{:S(2)}) async-start(f32[32,1,128]{2,1,0:T(1,128)} %bitcast.2), calls=%async_computation | async-start | bytes 32768 | tf_op jit(solution)/shard_map/all_to_all | solution.py:775
  49.3 0.0 copy-start
  49.3 2.1 %copy-done = f32[7552,128]{1,0:T(8,128)S(1)} copy-done((f32[7552,128]{1,0:T(8,128)S(1)}, f32[7552,128]{1,0:T(8,128)}, u32[]{:S(2)}) %copy-start) | copy-done | bytes 3866648
  51.4 1.6 %turned.1 = f32[46,128,128]{2,1,0:T(8,128)S(1)} custom-call(f32[7552,128]{1,0:T(8,128)S(1)} %copy-done), custom_call_target="tpu_custom_call" | custom-call | flops 4000000 | bytes 8000000 | tf_op jit(solution)/shard_map/turned/pallas_call | solution.py:777
  53.0 3.3 %all-to-all-done = f32[32,1,128]{2,1,0:T(1,128)S(1)} async-done(((f32[32,1,128]{2,1,0:T(1,128)}), f32[32,1,128]{2,1,0:T(1,128)S(1)}, u32[]{:S(2)}, u32[]{:S(2)}) %all-to-all-start) | async-done | bytes 16416 | tf_op jit(solution)/shard_map/all_to_all | solution.py:775
  56.4 2.4 %pressure.1 = (f32[32,2048]{1,0:T(8,128)}, f32[16,512]{1,0:T(8,128)}) custom-call(s32[1]{0:T(128)} %bitcast.me_ref, f32[32,128]{1,0:T(8,128)S(1)} %bitcast.5, f32[46,128,128]{2,1,0:T(8,128)S(1)} %turned.1), custom_call_target="tpu_custom_call" | custom-call | tf_op jit(solution)/shard_map/pressure/pallas_call | solution.py:788
  (4 shorter events, 0.0 us)
Async XLA Ops:
  1.7 8.6 %collective-permute-start = (f32[3,4,2048]{2,1,0:T(4,128)S(1)}, f32[3,4,2048]{2,1,0:T(4,128)S(1)}, u32[]{:S(2)}, u32[]{:S(2)}) collective-permute-start(f32[3,4,2048]{2,1,0:T(4,128)S(1)} %get-tuple-element.9), channel_id=1, source_target_pairs={{0,8},{8,16},{16,24},{24,0},{1,9},{9,17},{17,25},{25,1},{2,10},{10... | collective-permute-start | bytes 294920 | tf_op jit(solution)/shard_map/ppermute | solution.py:725
  4.8 6.4 %collective-permute-start.1 = (f32[3,4,2048]{2,1,0:T(4,128)S(1)}, f32[3,4,2048]{2,1,0:T(4,128)S(1)}, u32[]{:S(2)}, u32[]{:S(2)}) collective-permute-start(f32[3,4,2048]{2,1,0:T(4,128)S(1)} %get-tuple-element.8), channel_id=1, source_target_pairs={{0,24},{8,0},{16,8},{24,16},{1,25},{9,1},{17,9},{25,17},{2,26},{10... | collective-permute-start | bytes 294920 | tf_op jit(solution)/shard_map/ppermute | solution.py:725
  11.1 4.6 %collective-permute-start.2 = (f32[3,40,128]{2,1,0:T(8,128)S(1)}, f32[3,40,128]{2,1,0:T(8,128)S(1)}, u32[]{:S(2)}, u32[]{:S(2)}) collective-permute-start(f32[3,40,128]{2,1,0:T(8,128)S(1)} %pad_maximum_fusion), channel_id=1, source_target_pairs={{0,1},{1,2},{2,3},{3,4},{4,5},{5,6},{6,7},{7,0},{8,9},{9,10},{10,1... | collective-permute-start | bytes 184328 | tf_op jit(solution)/shard_map/ppermute | solution.py:725
  11.2 4.5 %collective-permute-start.3 = (f32[3,40,128]{2,1,0:T(8,128)S(1)}, f32[3,40,128]{2,1,0:T(8,128)S(1)}, u32[]{:S(2)}, u32[]{:S(2)}) collective-permute-start(f32[3,40,128]{2,1,0:T(8,128)S(1)} %pad_maximum_fusion.1), channel_id=1, source_target_pairs={{0,7},{1,0},{2,1},{3,2},{4,3},{5,4},{6,5},{7,6},{8,15},{9,8},{10,9... | collective-permute-start | bytes 184328 | tf_op jit(solution)/shard_map/ppermute | solution.py:725
  13.9 1.1 %copy-start.1 = (f32[3,32,2048]{2,1,0:T(8,128)S(1)}, f32[3,32,2048]{2,1,0:T(8,128)}, u32[]{:S(2)}) copy-start(f32[3,32,2048]{2,1,0:T(8,128)} %center.1) | copy-start | bytes 2359300
  44.3 12.0 %all-to-all-start = ((f32[32,1,128]{2,1,0:T(1,128)}), f32[32,1,128]{2,1,0:T(1,128)S(1)}, u32[]{:S(2)}, u32[]{:S(2)}) async-start(f32[32,1,128]{2,1,0:T(1,128)} %bitcast.2), calls=%async_computation | async-start | bytes 32768 | tf_op jit(solution)/shard_map/all_to_all | solution.py:775
  49.3 2.1 %copy-start = (f32[7552,128]{1,0:T(8,128)S(1)}, f32[7552,128]{1,0:T(8,128)}, u32[]{:S(2)}) copy-start(f32[7552,128]{1,0:T(8,128)} %get-tuple-element.5.phi) | copy-start | bytes 11599876

commit v8 on v7

--- a/solution.py
+++ b/solution.py
@@ -270,13 +270,15 @@
     return looped(lv.inner, group, 2, step)
 
 
-def row_jumps(u, s, j):
-    jump_x = [u[i * s + j] - (u[(i + 1) * s + j] if i < s - 1 else turn(u[j], -1)) for i in range(s)]
-    jump_y = [u[i * s + j] - (u[i * s + j + 1] if j < s - 1 else turn(u[i * s], -1, 0)) for i in range(s)]
-    return jump_x, jump_y
-
-
-def apply(case, group, number, betas):
+def plane_rows_of(get, s):
+    return lambda j: [get(i, j) for i in range(s)]
+
+
+def x_jumps(row, s):
+    return [row[i] - (row[i + 1] if i < s - 1 else turn(row[0], -1)) for i in range(s)]
+
+
+def apply(case, number, betas):
     lv, cs, s = case.lv, case.cs, case.lv.seg
     keep = number < 2
     n = lv.tiles
@@ -302,51 +304,55 @@
                 terms.append(-flux * value)
         firsts.append(tree(terms) if terms else 0.0)
 
-    def step(z0):
+    def step(z):
         total = [[], []]
-        u = [[case.d[number][z0, h * n + k] for k in range(n)] for h in HALVES]
-        flux_z = [[case.fz[h * n + k] for k in range(n)] for h in HALVES] if keep else None
-        for z in [z0 + t for t in range(group)]:
-            get = case.weights(z + 1)
-            after = [[None] * n for _ in HALVES]
-            if keep:
-                wy = [get(1, i, s - 1) for i in range(s)]
-                last = [[wy[i] * (u[h][i * s + s - 1] - turn(u[h][i * s], -1, 0)) for i in range(s)] for h in HALVES]
-                before = [[turn(v, 1, 0) for v in last[h]] for h in HALVES]
-            for j in range(s):
-                wx = [get(0, i, j) for i in range(s)]
-                wy = [get(1, i, j) for i in range(s)]
-                wz = [get(2, i, j) for i in range(s)]
-                for h in HALVES:
-                    jump_x, jump_y = row_jumps(u[h], s, j)
-                    flux_x = [w * v for w, v in zip(wx, jump_x)]
-                    flux_y = last[h] if keep and j == s - 1 else [w * v for w, v in zip(wy, jump_y)]
-                    terms = []
-                    for i in range(s):
-                        k = i * s + j
-                        after[h][k] = fresh(z + 1, h, k)
-                        jump = u[h][k] - after[h][k]
-                        flux = wz[i] * jump
-                        if keep:
-                            prev_x = flux_x[i - 1] if i else turn(flux_x[s - 1], 1)
-                            value = (flux_x[i] - prev_x) + (flux_y[i] - before[h][i]) + (flux - flux_z[h][k])
-                            flux_z[h][k] = flux
-                            value = cs.masked(value, i, j, 0)
-                            case.q[z, h * n + k] = value
-                            terms.append(u[h][k] * value)
-                        else:
-                            terms.append((flux * jump + flux_x[i] * jump_x[i]) + flux_y[i] * jump_y[i])
-                    total[h].append(tree(terms))
+        get = case.weights(z + 1)
+        rows = [
+            plane_rows_of(lambda i, j, h=h: case.d[number][z, h * n + i * s + j], s) for h in HALVES
+        ]
+        now = [rows[h](0) for h in HALVES]
+        if keep:
+            ends = [rows[h](s - 1) for h in HALVES]
+            wy = [get(1, i, s - 1) for i in range(s)]
+            last = [[wy[i] * (ends[h][i] - turn(now[h][i], -1, 0)) for i in range(s)] for h in HALVES]
+            before = [[turn(v, 1, 0) for v in last[h]] for h in HALVES]
+        for j in range(s):
+            wx = [get(0, i, j) for i in range(s)]
+            wy = [get(1, i, j) for i in range(s)]
+            wz = [get(2, i, j) for i in range(s)]
+            for h in HALVES:
+                u = now[h]
+                jump_x = x_jumps(u, s)
+                flux_x = [w * v for w, v in zip(wx, jump_x)]
+                if j < s - 1:
+                    now[h] = rows[h](j + 1)
+                    jump_y = [a - b for a, b in zip(u, now[h])]
+                    flux_y = [w * v for w, v in zip(wy, jump_y)]
+                elif keep:
+                    flux_y = last[h]
+                else:
+                    jump_y = [a - turn(b, -1, 0) for a, b in zip(u, rows[h](0))]
+                    flux_y = [w * v for w, v in zip(wy, jump_y)]
+                terms = []
+                for i in range(s):
+                    k = i * s + j
+                    jump = u[i] - fresh(z + 1, h, k)
+                    flux = wz[i] * jump
                     if keep:
-                        before[h] = flux_y
-            u = after
-        if keep:
-            for h in HALVES:
-                for k in range(n):
-                    case.fz[h * n + k] = flux_z[h][k]
+                        prev_x = flux_x[i - 1] if i else turn(flux_x[s - 1], 1)
+                        value = (flux_x[i] - prev_x) + (flux_y[i] - before[h][i]) + (flux - case.fz[h * n + k])
+                        case.fz[h * n + k] = flux
+                        value = cs.masked(value, i, j, 0)
+                        case.q[z, h * n + k] = value
+                        terms.append(u[i] * value)
+                    else:
+                        terms.append((flux * jump + flux_x[i] * jump_x[i]) + flux_y[i] * jump_y[i])
+                total[h].append(tree(terms))
+                if keep:
+                    before[h] = flux_y
         return [tree(t) for t in total]
 
-    return [a + b for a, b in zip(looped(lv.inner, group, 2, step), firsts)]
+    return [a + b for a, b in zip(looped(lv.inner, 1, 2, step), firsts)]
 
 
 def reduce_residual(case, group, number, alphas):
@@ -369,7 +375,7 @@
     return looped(lv.inner, group, 2, step)
 
 
-def finish(case, group, alphas, refs, send):
+def finish(case, alphas, refs, send):
     lv, cs, s = case.lv, case.cs, case.lv.seg
     n = lv.tiles
     f_ref, p_ref, y_ref = refs
@@ -406,41 +412,34 @@
     def cut(values, table):
         return [v if f is None else v * f for v, f in zip(values, table)]
 
-    def body(t, _):
-        z0 = t * group
-        u = [f_ref[at(z0, k), :] for k in range(n)]
-        flux_z = [case.fz[k] for k in range(n)]
-        for z in [z0 + m for m in range(group)]:
-            get = case.weights(z + lv.mz)
-            up = jnp.minimum(z + 1, lv.edz - 1)
-            gz = cs.fz(up + lv.mz)
-            after = [None] * n
-            last = [get(1, i, s - 1) * (u[i * s + s - 1] - turn(u[i * s], -1, 0)) for i in range(s)]
-            last = cut(last, [cs.facey[s - 1]] * s)
-            before = [turn(v, 1, 0) for v in last]
-            for j in range(s):
-                jump_x, jump_y = row_jumps(u, s, j)
-                flux_x = cut([get(0, i, j) * jump_x[i] for i in range(s)], cs.facex)
-                flux_y = last
-                if j < s - 1:
-                    flux_y = cut([get(1, i, j) * jump_y[i] for i in range(s)], [cs.facey[j]] * s)
-                for i in range(s):
-                    k = i * s + j
-                    after[k] = fresh(up, i, j, gz)
-                    flux = get(2, i, j) * (u[k] - after[k])
-                    prev_x = flux_x[i - 1] if i else turn(flux_x[s - 1], 1)
-                    y_ref[at(z, k), :] = (flux_x[i] - prev_x) + (flux_y[i] - before[i]) + (flux - flux_z[k])
-                    flux_z[k] = flux
-                before = flux_y
-            u = after
-        for k in range(n):
-            case.fz[k] = flux_z[k]
-        for z in [z0 + m for m in range(group)]:
-            for h in HALVES:
-                send(h, z).start()
+    def body(z, _):
+        get = case.weights(z + lv.mz)
+        up = jnp.minimum(z + 1, lv.edz - 1)
+        gz = cs.fz(up + lv.mz)
+        rows = plane_rows_of(lambda i, j: f_ref[at(z, i * s + j), :], s)
+        now = rows(0)
+        last = [get(1, i, s - 1) * (v - turn(now[i], -1, 0)) for i, v in enumerate(rows(s - 1))]
+        last = cut(last, [cs.facey[s - 1]] * s)
+        before = [turn(v, 1, 0) for v in last]
+        for j in range(s):
+            u = now
+            flux_x = cut([get(0, i, j) * v for i, v in enumerate(x_jumps(u, s))], cs.facex)
+            flux_y = last
+            if j < s - 1:
+                now = rows(j + 1)
+                flux_y = cut([get(1, i, j) * (u[i] - now[i]) for i in range(s)], [cs.facey[j]] * s)
+            for i in range(s):
+                k = i * s + j
+                flux = get(2, i, j) * (u[i] - fresh(up, i, j, gz))
+                prev_x = flux_x[i - 1] if i else turn(flux_x[s - 1], 1)
+                y_ref[at(z, k), :] = (flux_x[i] - prev_x) + (flux_y[i] - before[i]) + (flux - case.fz[k])
+                case.fz[k] = flux
+            before = flux_y
+        for h in HALVES:
+            send(h, z).start()
         return 0
 
-    lax.fori_loop(0, lv.edz // group, body, 0)
+    lax.fori_loop(0, lv.edz, body, 0)
     pairs = jnp.zeros((2 * LANES, LANES), F32)
     for start in range(0, padded_rows(lv), CHUNK):
         part = slice(start, start + CHUNK)
@@ -462,7 +461,7 @@
     return out
 
 
-GROUPS = {FINE: 1, TWIN: 8}
+GROUPS = {FINE: 1, TWIN: 4}
 
 
 def place_kernel(center, out_ref):
@@ -546,7 +545,7 @@
     alphas = [[[], []] for _ in LEVELS]
     betas = [None] * len(LEVELS)
     for step in range(3):
-        dots = both_levels(lambda n, case, group: apply(case, group, step, betas[n]))
+        dots = both_levels(lambda n, case, group: apply(case, step, betas[n]))
         now = [[a / b for a, b in zip(rr[n], dots[n])] for n in range(len(LEVELS))]
         for n in range(len(LEVELS)):
             for h in HALVES:
@@ -570,7 +569,7 @@
         )
 
     totals = both_levels(
-        lambda n, case, group: finish(case, group, alphas[n], results[n], functools.partial(send, n))
+        lambda n, case, group: finish(case, alphas[n], results[n], functools.partial(send, n))
     )
     _, element, _, slot = lane_parts()
     packed = []

time: 59.1 us -> 63 us (1.066)
  Pallas kernels: 32.7 us -> 36.6 us
    pallas_call x1, Pallas kernels: 28.6 us -> 32.5 us  [shards(): pl.pallas_call(solve_kernel, out_shape=[pltpu.HBM((sum((2 * field_rows(lv...]
where the time goes in v8:
time: 63 us; the launch traced here: 62.7 us
  Pallas kernels  36.6 us (58%)
  starting transfers between devices  12.8 us (20%)
  waiting for transfers between devices  7.41 us (12%)
  local copies, waits for them, and re-layouts  5.12 us (8%)
  between operations  0.7 us (1%)
    pallas_call x1, Pallas kernels, shards(): pl.pallas_call(solve_kernel, out_shape=[pltpu.HBM((sum((2 * field_rows(lv...  32.5 us
    ppermute x4, starting transfers between devices, sent(): lax.ppermute(value, axis, [(i, (i + shift) % count) for i in range(count)])  7.9 us
    all_to_all x1, starting transfers between devices, shards(): gathered = lax.all_to_all(message, ('gx', 'gy'), 0, 0, tiled=True)  4.95 us
    ppermute x4, waiting for transfers between devices, sent(): lax.ppermute(value, axis, [(i, (i + shift) % count) for i in range(count)])  4.07 us
    all_to_all x1, waiting for transfers between devices, shards(): gathered = lax.all_to_all(message, ('gx', 'gy'), 0, 0, tiled=True)  3.33 us
    unnamed x4, local copies, waits for them, and re-layouts  3.22 us
    pallas_call x1, Pallas kernels, shards(): pl.pallas_call(functools.partial(pressure_kernel, gy), out_shape=[jax.Sha...  2.38 us
    pallas_call x1, Pallas kernels, shards(): pl.pallas_call(turn_kernel, out_shape=vmem((tiles, LANES, LANES)), in_spe...  1.63 us
  transfers between devices with their start and end apart: 5, of which 4 were waited for; matrix products, arithmetic and copies ran while one was open for 1% of the time, Pallas kernels for 3%

profile of v8, /device:TPU:0, one launch (start us, length us, event | category | flops | bytes accessed | tf_op | source)
XLA Modules:
  0.0 62.7 jit_solution(11689991542020334067)
XLA Ops:
  0.6 1.1 %fusion.1 = (f32[3,4,2048]{2,1,0:T(4,128)S(1)}, f32[3,4,2048]{2,1,0:T(4,128)S(1)}) fusion(f32[3,32,2048]{2,1,0:T(8,128)} %center.1), kind=kLoop, calls=%fused_computation.3 | loop fusion | bytes 393216 | tf_op jit(solution)/shard_map/slice | solution.py:727
  1.7 3.1 %collective-permute-start = (f32[3,4,2048]{2,1,0:T(4,128)S(1)}, f32[3,4,2048]{2,1,0:T(4,128)S(1)}, u32[]{:S(2)}, u32[]{:S(2)}) collective-permute-start(f32[3,4,2048]{2,1,0:T(4,128)S(1)} %get-tuple-element.9), channel_id=1, source_target_pairs={{0,8},{8,16},{16,24},{24,0},{1,9},{9,17},{17,25},{25,1},{2,10},{10... | collective-permute-start | bytes 294920 | tf_op jit(solution)/shard_map/ppermute | solution.py:724
  4.8 2.1 %collective-permute-start.1 = (f32[3,4,2048]{2,1,0:T(4,128)S(1)}, f32[3,4,2048]{2,1,0:T(4,128)S(1)}, u32[]{:S(2)}, u32[]{:S(2)}) collective-permute-start(f32[3,4,2048]{2,1,0:T(4,128)S(1)} %get-tuple-element.8), channel_id=1, source_target_pairs={{0,24},{8,0},{16,8},{24,16},{1,25},{9,1},{17,9},{25,17},{2,26},{10... | collective-permute-start | bytes 294920 | tf_op jit(solution)/shard_map/ppermute | solution.py:724
  6.9 0.8 %fusion = (f32[3,32,128]{2,1,0:T(8,128)S(1)}, f32[3,32,128]{2,1,0:T(8,128)S(1)}) fusion(f32[3,32,2048]{2,1,0:T(8,128)} %center.1), kind=kLoop, calls=%fused_computation.2 | loop fusion | bytes 196608 | tf_op jit(solution)/shard_map/slice | solution.py:730
  7.7 2.6 %collective-permute-done.x_low = f32[3,4,2048]{2,1,0:T(4,128)S(1)} collective-permute-done((f32[3,4,2048]{2,1,0:T(4,128)S(1)}, f32[3,4,2048]{2,1,0:T(4,128)S(1)}, u32[]{:S(2)}, u32[]{:S(2)}) %collective-permute-start) | collective-permute-done | bytes 98336 | tf_op jit(solution)/shard_map/ppermute | solution.py:724
  10.3 0.8 %collective-permute-done.1.x_high = f32[3,4,2048]{2,1,0:T(4,128)S(1)} collective-permute-done((f32[3,4,2048]{2,1,0:T(4,128)S(1)}, f32[3,4,2048]{2,1,0:T(4,128)S(1)}, u32[]{:S(2)}, u32[]{:S(2)}) %collective-permute-start.1) | collective-permute-done | bytes 98336 | tf_op jit(solution)/shard_map/ppermute | solution.py:724
  11.1 0.1 collective-permute-start.2
  11.2 2.7 %collective-permute-start.3 = (f32[3,40,128]{2,1,0:T(8,128)S(1)}, f32[3,40,128]{2,1,0:T(8,128)S(1)}, u32[]{:S(2)}, u32[]{:S(2)}) collective-permute-start(f32[3,40,128]{2,1,0:T(8,128)S(1)} %pad_maximum_fusion.1), channel_id=1, source_target_pairs={{0,7},{1,0},{2,1},{3,2},{4,3},{5,4},{6,5},{7,6},{8,15},{9,8},{10,9... | collective-permute-start | bytes 184328 | tf_op jit(solution)/shard_map/ppermute | solution.py:724
  13.9 0.0 copy-start.1
  13.9 1.1 %copy-done.1 = f32[3,32,2048]{2,1,0:T(8,128)S(1)} copy-done((f32[3,32,2048]{2,1,0:T(8,128)S(1)}, f32[3,32,2048]{2,1,0:T(8,128)}, u32[]{:S(2)}) %copy-start.1) | copy-done | bytes 786456
  15.0 0.1 place.1.inside
  15.1 0.6 collective-permute-done.2.y_low
  15.7 0.0 collective-permute-done.3.y_high
  15.8 32.5 %solve.1 = (f32[7552,128]{1,0:T(8,128)}, f32[32,128]{1,0:T(8,128)}) custom-call(f32[128,2048]{1,0:T(8,128)S(1)} %place.1.inside, f32[3,4,2048]{2,1,0:T(4,128)S(1)} %collective-permute-done.x_low, f32[3,4,2048]{2,1,0:T(4,128)S(1)} %collective-permute-done.1.x_high, f32[3,40,128]{2,1,0:T(8,128)S(1)} %collective-permute-done.2.y_low, ...), custom_call_target="tpu_custom_call" | custom-call | tf_op jit(solution)/shard_map/solve/pallas_call | solution.py:762
  48.3 4.9 %all-to-all-start = ((f32[32,1,128]{2,1,0:T(1,128)}), f32[32,1,128]{2,1,0:T(1,128)S(1)}, u32[]{:S(2)}, u32[]{:S(2)}) async-start(f32[32,1,128]{2,1,0:T(1,128)} %bitcast.2), calls=%async_computation | async-start | bytes 32768 | tf_op jit(solution)/shard_map/all_to_all | solution.py:774
  53.2 0.0 copy-start
  53.2 2.1 %copy-done = f32[7552,128]{1,0:T(8,128)S(1)} copy-done((f32[7552,128]{1,0:T(8,128)S(1)}, f32[7552,128]{1,0:T(8,128)}, u32[]{:S(2)}) %copy-start) | copy-done | bytes 3866648
  55.3 1.6 %turned.1 = f32[46,128,128]{2,1,0:T(8,128)S(1)} custom-call(f32[7552,128]{1,0:T(8,128)S(1)} %copy-done), custom_call_target="tpu_custom_call" | custom-call | flops 4000000 | bytes 8000000 | tf_op jit(solution)/shard_map/turned/pallas_call | solution.py:776
  56.9 3.3 %all-to-all-done = f32[32,1,128]{2,1,0:T(1,128)S(1)} async-done(((f32[32,1,128]{2,1,0:T(1,128)}), f32[32,1,128]{2,1,0:T(1,128)S(1)}, u32[]{:S(2)}, u32[]{:S(2)}) %all-to-all-start) | async-done | bytes 16416 | tf_op jit(solution)/shard_map/all_to_all | solution.py:774
  60.3 2.4 %pressure.1 = (f32[32,2048]{1,0:T(8,128)}, f32[16,512]{1,0:T(8,128)}) custom-call(s32[1]{0:T(128)} %bitcast.me_ref, f32[32,128]{1,0:T(8,128)S(1)} %bitcast.5, f32[46,128,128]{2,1,0:T(8,128)S(1)} %turned.1), custom_call_target="tpu_custom_call" | custom-call | tf_op jit(solution)/shard_map/pressure/pallas_call | solution.py:787
  (4 shorter events, 0.0 us)
Async XLA Ops:
  1.7 8.6 %collective-permute-start = (f32[3,4,2048]{2,1,0:T(4,128)S(1)}, f32[3,4,2048]{2,1,0:T(4,128)S(1)}, u32[]{:S(2)}, u32[]{:S(2)}) collective-permute-start(f32[3,4,2048]{2,1,0:T(4,128)S(1)} %get-tuple-element.9), channel_id=1, source_target_pairs={{0,8},{8,16},{16,24},{24,0},{1,9},{9,17},{17,25},{25,1},{2,10},{10... | collective-permute-start | bytes 294920 | tf_op jit(solution)/shard_map/ppermute | solution.py:724
  4.8 6.4 %collective-permute-start.1 = (f32[3,4,2048]{2,1,0:T(4,128)S(1)}, f32[3,4,2048]{2,1,0:T(4,128)S(1)}, u32[]{:S(2)}, u32[]{:S(2)}) collective-permute-start(f32[3,4,2048]{2,1,0:T(4,128)S(1)} %get-tuple-element.8), channel_id=1, source_target_pairs={{0,24},{8,0},{16,8},{24,16},{1,25},{9,1},{17,9},{25,17},{2,26},{10... | collective-permute-start | bytes 294920 | tf_op jit(solution)/shard_map/ppermute | solution.py:724
  11.1 4.6 %collective-permute-start.2 = (f32[3,40,128]{2,1,0:T(8,128)S(1)}, f32[3,40,128]{2,1,0:T(8,128)S(1)}, u32[]{:S(2)}, u32[]{:S(2)}) collective-permute-start(f32[3,40,128]{2,1,0:T(8,128)S(1)} %pad_maximum_fusion), channel_id=1, source_target_pairs={{0,1},{1,2},{2,3},{3,4},{4,5},{5,6},{6,7},{7,0},{8,9},{9,10},{10,1... | collective-permute-start | bytes 184328 | tf_op jit(solution)/shard_map/ppermute | solution.py:724
  11.2 4.5 %collective-permute-start.3 = (f32[3,40,128]{2,1,0:T(8,128)S(1)}, f32[3,40,128]{2,1,0:T(8,128)S(1)}, u32[]{:S(2)}, u32[]{:S(2)}) collective-permute-start(f32[3,40,128]{2,1,0:T(8,128)S(1)} %pad_maximum_fusion.1), channel_id=1, source_target_pairs={{0,7},{1,0},{2,1},{3,2},{4,3},{5,4},{6,5},{7,6},{8,15},{9,8},{10,9... | collective-permute-start | bytes 184328 | tf_op jit(solution)/shard_map/ppermute | solution.py:724
  13.9 1.1 %copy-start.1 = (f32[3,32,2048]{2,1,0:T(8,128)S(1)}, f32[3,32,2048]{2,1,0:T(8,128)}, u32[]{:S(2)}) copy-start(f32[3,32,2048]{2,1,0:T(8,128)} %center.1) | copy-start | bytes 2359300
  48.3 12.0 %all-to-all-start = ((f32[32,1,128]{2,1,0:T(1,128)}), f32[32,1,128]{2,1,0:T(1,128)S(1)}, u32[]{:S(2)}, u32[]{:S(2)}) async-start(f32[32,1,128]{2,1,0:T(1,128)} %bitcast.2), calls=%async_computation | async-start | bytes 32768 | tf_op jit(solution)/shard_map/all_to_all | solution.py:774
  53.2 2.1 %copy-start = (f32[7552,128]{1,0:T(8,128)S(1)}, f32[7552,128]{1,0:T(8,128)}, u32[]{:S(2)}) copy-start(f32[7552,128]{1,0:T(8,128)} %get-tuple-element.5.phi) | copy-start | bytes 11599876

commit v9 on v8

--- a/solution.py
+++ b/solution.py
@@ -243,6 +243,7 @@
 
     def step(z0):
         total = [[], []]
+        stores = []
         for z in [z0 + n for n in range(group)]:
             get, below = case.weights(z + 1), case.weights(z)
             gz = cs.fz(z + 1)
@@ -251,27 +252,29 @@
             for j in range(s):
                 flux_y = last if j == s - 1 else [get(1, i, j) * cs.along_y[i] for i in range(s)]
                 flux_x = [get(0, i, j) * cs.along_x[j] for i in range(s)]
+                tops = [below(2, i, j) - get(2, i, j) for i in range(s)]
+                for index, value in stores:
+                    case.d[0][index] = value
+                del stores[:]
                 squares = [[], []]
                 for i in range(s):
                     k = i * s + j
                     prev_x = flux_x[i - 1] if i else turn(flux_x[s - 1], 1)
                     flat = (prev_x - flux_x[i]) + (before[i] - flux_y[i])
                     flat = cs.masked(flat, i, j, 0)
-                    tall = (cs.fx[i] * cs.fy[j]) * (1.0 / lv.edz) * (below(2, i, j) - get(2, i, j))
+                    tall = (cs.fx[i] * cs.fy[j]) * (1.0 / lv.edz) * tops[i]
                     tall = cs.masked(tall, i, j, 0)
                     for h, value in enumerate((flat * gz[0] + tall, flat * gz[1] - tall)):
-                        case.d[0][z, h * lv.tiles + k] = value
+                        stores.append(((z, h * lv.tiles + k), value))
                         squares[h].append(value * value)
                 for h in HALVES:
                     total[h].append(tree(squares[h]))
                 before = flux_y
+        for index, value in stores:
+            case.d[0][index] = value
         return [tree(t) for t in total]
 
     return looped(lv.inner, group, 2, step)
-
-
-def plane_rows_of(get, s):
-    return lambda j: [get(i, j) for i in range(s)]
 
 
 def x_jumps(row, s):
@@ -307,49 +310,72 @@
     def step(z):
         total = [[], []]
         get = case.weights(z + 1)
-        rows = [
-            plane_rows_of(lambda i, j, h=h: case.d[number][z, h * n + i * s + j], s) for h in HALVES
-        ]
-        now = [rows[h](0) for h in HALVES]
+
+        def load(j):
+            cells = [i * s + j for i in range(s)]
+            out = {"u": [[case.d[number][z, h * n + k] for k in cells] for h in HALVES]}
+            out["w"] = [[get(m, i, j) for i in range(s)] for m in range(3)]
+            if keep:
+                out["fz"] = [[case.fz[h * n + k] for k in cells] for h in HALVES]
+            if number == 0:
+                out["up"] = [[case.d[0][z + 1, h * n + k] for k in cells] for h in HALVES]
+            else:
+                old = case.d[number - 1]
+                out["up"] = [
+                    [(case.r[z + 1, h * n + k], old[z + 1, h * n + k]) for k in cells] for h in HALVES
+                ]
+            return out
+
+        row = load(0)
         if keep:
-            ends = [rows[h](s - 1) for h in HALVES]
             wy = [get(1, i, s - 1) for i in range(s)]
-            last = [[wy[i] * (ends[h][i] - turn(now[h][i], -1, 0)) for i in range(s)] for h in HALVES]
+            ends = [[case.d[number][z, h * n + i * s + s - 1] for i in range(s)] for h in HALVES]
+        heads = [[turn(v, -1, 0) for v in row["u"][h]] for h in HALVES]
+        if keep:
+            last = [[wy[i] * (ends[h][i] - heads[h][i]) for i in range(s)] for h in HALVES]
             before = [[turn(v, 1, 0) for v in last[h]] for h in HALVES]
+        stores = []
+
+        def flush():
+            for ref, index, value in stores:
+                ref[index] = value
+            del stores[:]
+
         for j in range(s):
-            wx = [get(0, i, j) for i in range(s)]
-            wy = [get(1, i, j) for i in range(s)]
-            wz = [get(2, i, j) for i in range(s)]
+            now, row = row, (load(j + 1) if j < s - 1 else None)
+            flush()
+            wx, wy, wz = now["w"]
             for h in HALVES:
-                u = now[h]
+                u = now["u"][h]
                 jump_x = x_jumps(u, s)
                 flux_x = [w * v for w, v in zip(wx, jump_x)]
-                if j < s - 1:
-                    now[h] = rows[h](j + 1)
-                    jump_y = [a - b for a, b in zip(u, now[h])]
-                    flux_y = [w * v for w, v in zip(wy, jump_y)]
-                elif keep:
+                if keep and j == s - 1:
                     flux_y = last[h]
                 else:
-                    jump_y = [a - turn(b, -1, 0) for a, b in zip(u, rows[h](0))]
+                    jump_y = [a - b for a, b in zip(u, row["u"][h] if j < s - 1 else heads[h])]
                     flux_y = [w * v for w, v in zip(wy, jump_y)]
                 terms = []
                 for i in range(s):
                     k = i * s + j
-                    jump = u[i] - fresh(z + 1, h, k)
+                    after = now["up"][h][i]
+                    if number:
+                        after = after[0] + betas[h] * after[1]
+                        stores.append((case.d[number], (z + 1, h * n + k), after))
+                    jump = u[i] - after
                     flux = wz[i] * jump
                     if keep:
                         prev_x = flux_x[i - 1] if i else turn(flux_x[s - 1], 1)
-                        value = (flux_x[i] - prev_x) + (flux_y[i] - before[h][i]) + (flux - case.fz[h * n + k])
-                        case.fz[h * n + k] = flux
+                        value = (flux_x[i] - prev_x) + (flux_y[i] - before[h][i]) + (flux - now["fz"][h][i])
+                        stores.append((case.fz, h * n + k, flux))
                         value = cs.masked(value, i, j, 0)
-                        case.q[z, h * n + k] = value
+                        stores.append((case.q, (z, h * n + k), value))
                         terms.append(u[i] * value)
                     else:
                         terms.append((flux * jump + flux_x[i] * jump_x[i]) + flux_y[i] * jump_y[i])
                 total[h].append(tree(terms))
                 if keep:
                     before[h] = flux_y
+        flush()
         return [tree(t) for t in total]
 
     return [a + b for a, b in zip(looped(lv.inner, 1, 2, step), firsts)]
@@ -363,13 +389,11 @@
         source = case.d[0] if number == 0 else case.r
         for z in [z0 + n for n in range(group)]:
             for h in HALVES:
-                squares = []
-                for k in range(lv.tiles):
-                    at = h * lv.tiles + k
-                    value = source[z, at] - alphas[h] * case.q[z, at]
+                cells = range(h * lv.tiles, (h + 1) * lv.tiles)
+                values = [source[z, at] - alphas[h] * case.q[z, at] for at in cells]
+                for at, value in zip(cells, values):
                     case.r[z, at] = value
-                    squares.append(value * value)
-                total[h].append(tree(squares))
+                total[h].append(tree([v * v for v in values]))
         return [tree(t) for t in total]
 
     return looped(lv.inner, group, 2, step)
@@ -384,26 +408,25 @@
     def at(z, k):
         return pl.ds(pl.multiple_of(z * plane_rows(lv) + k * SUBS, SUBS), SUBS)
 
-    def fresh(z, i, j, gz):
-        k = i * s + j
-        inner = z + lv.mz - 1
+    def parts(z, k):
+        return [[d_ref[z + lv.mz - 1, h * n + k] for d_ref in case.d] for h in HALVES]
+
+    def fresh(i, j, gz, fields):
         both = cs.fx[i] * cs.fy[j]
         values = []
         for h in HALVES:
             value = both * gz[h]
-            for alpha, d_ref in zip(alphas[h], case.d):
-                value = value + alpha * d_ref[inner, h * n + k]
+            for alpha, d in zip(alphas[h], fields[h]):
+                value = value + alpha * d
             values.append(cs.masked(value, i, j, 1))
-        chosen = jnp.where(lower, values[1], values[0])
-        f_ref[at(z, k), :] = chosen
-        p_ref[at(z, k), :] = values[0]
-        return chosen
+        return jnp.where(lower, values[1], values[0]), values[0]
 
     gz = cs.fz(lv.mz)
     for i in range(s):
         for j in range(s):
-            fresh(0, i, j, gz)
-            case.fz[i * s + j] = jnp.zeros((SUBS, LANES), F32)
+            k = i * s + j
+            f_ref[at(0, k), :], p_ref[at(0, k), :] = fresh(i, j, gz, parts(0, k))
+            case.fz[k] = jnp.zeros((SUBS, LANES), F32)
     rest = padded_rows(lv) - field_rows(lv)
     if rest:
         for ref in refs:
@@ -416,25 +439,50 @@
         get = case.weights(z + lv.mz)
         up = jnp.minimum(z + 1, lv.edz - 1)
         gz = cs.fz(up + lv.mz)
-        rows = plane_rows_of(lambda i, j: f_ref[at(z, i * s + j), :], s)
-        now = rows(0)
-        last = [get(1, i, s - 1) * (v - turn(now[i], -1, 0)) for i, v in enumerate(rows(s - 1))]
+
+        def load(j):
+            cells = [i * s + j for i in range(s)]
+            return {
+                "u": [f_ref[at(z, k), :] for k in cells],
+                "w": [[get(m, i, j) for i in range(s)] for m in range(3)],
+                "fz": [case.fz[k] for k in cells],
+                "up": [parts(up, k) for k in cells],
+            }
+
+        row = load(0)
+        wy = [get(1, i, s - 1) for i in range(s)]
+        ends = [f_ref[at(z, i * s + s - 1), :] for i in range(s)]
+        last = [wy[i] * (ends[i] - turn(row["u"][i], -1, 0)) for i in range(s)]
         last = cut(last, [cs.facey[s - 1]] * s)
         before = [turn(v, 1, 0) for v in last]
+        stores = []
+
+        def flush():
+            for ref, index, value in stores:
+                ref[index] = value
+            del stores[:]
+
         for j in range(s):
-            u = now
-            flux_x = cut([get(0, i, j) * v for i, v in enumerate(x_jumps(u, s))], cs.facex)
+            now, row = row, (load(j + 1) if j < s - 1 else None)
+            flush()
+            u = now["u"]
+            wx, wy, wz = now["w"]
+            flux_x = cut([w * v for w, v in zip(wx, x_jumps(u, s))], cs.facex)
             flux_y = last
             if j < s - 1:
-                now = rows(j + 1)
-                flux_y = cut([get(1, i, j) * (u[i] - now[i]) for i in range(s)], [cs.facey[j]] * s)
+                flux_y = cut([w * (a - b) for w, a, b in zip(wy, u, row["u"])], [cs.facey[j]] * s)
             for i in range(s):
                 k = i * s + j
-                flux = get(2, i, j) * (u[i] - fresh(up, i, j, gz))
+                chosen, bottom = fresh(i, j, gz, now["up"][i])
+                flux = wz[i] * (u[i] - chosen)
                 prev_x = flux_x[i - 1] if i else turn(flux_x[s - 1], 1)
-                y_ref[at(z, k), :] = (flux_x[i] - prev_x) + (flux_y[i] - before[i]) + (flux - case.fz[k])
-                case.fz[k] = flux
+                value = (flux_x[i] - prev_x) + (flux_y[i] - before[i]) + (flux - now["fz"][i])
+                stores.append((f_ref, (at(up, k), slice(None)), chosen))
+                stores.append((p_ref, (at(up, k), slice(None)), bottom))
+                stores.append((y_ref, (at(z, k), slice(None)), value))
+                stores.append((case.fz, k, flux))
             before = flux_y
+        flush()
         for h in HALVES:
             send(h, z).start()
         return 0

time: 63 us -> 62.7 us (level)
  no operation moved by 1% of the time
where the time goes in v9:
time: 62.7 us; the launch traced here: 62.4 us
  Pallas kernels  36.3 us (58%)
  starting transfers between devices  12.8 us (20%)
  waiting for transfers between devices  7.41 us (12%)
  local copies, waits for them, and re-layouts  5.12 us (8%)
  between operations  0.7 us (1%)
    pallas_call x1, Pallas kernels, shards(): pl.pallas_call(solve_kernel, out_shape=[pltpu.HBM((sum((2 * field_rows(lv...  32.2 us
    ppermute x4, starting transfers between devices, sent(): lax.ppermute(value, axis, [(i, (i + shift) % count) for i in range(count)])  7.9 us
    all_to_all x1, starting transfers between devices, shards(): gathered = lax.all_to_all(message, ('gx', 'gy'), 0, 0, tiled=True)  4.94 us
    ppermute x4, waiting for transfers between devices, sent(): lax.ppermute(value, axis, [(i, (i + shift) % count) for i in range(count)])  4.07 us
    all_to_all x1, waiting for transfers between devices, shards(): gathered = lax.all_to_all(message, ('gx', 'gy'), 0, 0, tiled=True)  3.33 us
    unnamed x4, local copies, waits for them, and re-layouts  3.22 us
    pallas_call x1, Pallas kernels, shards(): pl.pallas_call(functools.partial(pressure_kernel, gy), out_shape=[jax.Sha...  2.38 us
    pallas_call x1, Pallas kernels, shards(): pl.pallas_call(turn_kernel, out_shape=vmem((tiles, LANES, LANES)), in_spe...  1.63 us
  transfers between devices with their start and end apart: 5, of which 4 were waited for; matrix products, arithmetic and copies ran while one was open for 1% of the time, Pallas kernels for 3%

profile of v9, /device:TPU:0, one launch (start us, length us, event | category | flops | bytes accessed | tf_op | source)
XLA Modules:
  0.0 62.4 jit_solution(6175532113759223771)
XLA Ops:
  0.6 1.1 %fusion.1 = (f32[3,4,2048]{2,1,0:T(4,128)S(1)}, f32[3,4,2048]{2,1,0:T(4,128)S(1)}) fusion(f32[3,32,2048]{2,1,0:T(8,128)} %center.1), kind=kLoop, calls=%fused_computation.3 | loop fusion | bytes 393216 | tf_op jit(solution)/shard_map/slice | solution.py:775
  1.7 3.1 %collective-permute-start = (f32[3,4,2048]{2,1,0:T(4,128)S(1)}, f32[3,4,2048]{2,1,0:T(4,128)S(1)}, u32[]{:S(2)}, u32[]{:S(2)}) collective-permute-start(f32[3,4,2048]{2,1,0:T(4,128)S(1)} %get-tuple-element.9), channel_id=1, source_target_pairs={{0,8},{8,16},{16,24},{24,0},{1,9},{9,17},{17,25},{25,1},{2,10},{10... | collective-permute-start | bytes 294920 | tf_op jit(solution)/shard_map/ppermute | solution.py:772
  4.8 2.1 %collective-permute-start.1 = (f32[3,4,2048]{2,1,0:T(4,128)S(1)}, f32[3,4,2048]{2,1,0:T(4,128)S(1)}, u32[]{:S(2)}, u32[]{:S(2)}) collective-permute-start(f32[3,4,2048]{2,1,0:T(4,128)S(1)} %get-tuple-element.8), channel_id=1, source_target_pairs={{0,24},{8,0},{16,8},{24,16},{1,25},{9,1},{17,9},{25,17},{2,26},{10... | collective-permute-start | bytes 294920 | tf_op jit(solution)/shard_map/ppermute | solution.py:772
  6.9 0.8 %fusion = (f32[3,32,128]{2,1,0:T(8,128)S(1)}, f32[3,32,128]{2,1,0:T(8,128)S(1)}) fusion(f32[3,32,2048]{2,1,0:T(8,128)} %center.1), kind=kLoop, calls=%fused_computation.2 | loop fusion | bytes 196608 | tf_op jit(solution)/shard_map/slice | solution.py:778
  7.7 2.6 %collective-permute-done.x_low = f32[3,4,2048]{2,1,0:T(4,128)S(1)} collective-permute-done((f32[3,4,2048]{2,1,0:T(4,128)S(1)}, f32[3,4,2048]{2,1,0:T(4,128)S(1)}, u32[]{:S(2)}, u32[]{:S(2)}) %collective-permute-start) | collective-permute-done | bytes 98336 | tf_op jit(solution)/shard_map/ppermute | solution.py:772
  10.3 0.8 %collective-permute-done.1.x_high = f32[3,4,2048]{2,1,0:T(4,128)S(1)} collective-permute-done((f32[3,4,2048]{2,1,0:T(4,128)S(1)}, f32[3,4,2048]{2,1,0:T(4,128)S(1)}, u32[]{:S(2)}, u32[]{:S(2)}) %collective-permute-start.1) | collective-permute-done | bytes 98336 | tf_op jit(solution)/shard_map/ppermute | solution.py:772
  11.1 0.1 collective-permute-start.2
  11.2 2.7 %collective-permute-start.3 = (f32[3,40,128]{2,1,0:T(8,128)S(1)}, f32[3,40,128]{2,1,0:T(8,128)S(1)}, u32[]{:S(2)}, u32[]{:S(2)}) collective-permute-start(f32[3,40,128]{2,1,0:T(8,128)S(1)} %pad_maximum_fusion.1), channel_id=1, source_target_pairs={{0,7},{1,0},{2,1},{3,2},{4,3},{5,4},{6,5},{7,6},{8,15},{9,8},{10,9... | collective-permute-start | bytes 184328 | tf_op jit(solution)/shard_map/ppermute | solution.py:772
  13.9 0.0 copy-start.1
  13.9 1.1 %copy-done.1 = f32[3,32,2048]{2,1,0:T(8,128)S(1)} copy-done((f32[3,32,2048]{2,1,0:T(8,128)S(1)}, f32[3,32,2048]{2,1,0:T(8,128)}, u32[]{:S(2)}) %copy-start.1) | copy-done | bytes 786456
  15.0 0.1 place.1.inside
  15.1 0.6 collective-permute-done.2.y_low
  15.7 0.0 collective-permute-done.3.y_high
  15.8 32.2 %solve.1 = (f32[7552,128]{1,0:T(8,128)}, f32[32,128]{1,0:T(8,128)}) custom-call(f32[128,2048]{1,0:T(8,128)S(1)} %place.1.inside, f32[3,4,2048]{2,1,0:T(4,128)S(1)} %collective-permute-done.x_low, f32[3,4,2048]{2,1,0:T(4,128)S(1)} %collective-permute-done.1.x_high, f32[3,40,128]{2,1,0:T(8,128)S(1)} %collective-permute-done.2.y_low, ...), custom_call_target="tpu_custom_call" | custom-call | tf_op jit(solution)/shard_map/solve/pallas_call | solution.py:810
  48.0 4.9 %all-to-all-start = ((f32[32,1,128]{2,1,0:T(1,128)}), f32[32,1,128]{2,1,0:T(1,128)S(1)}, u32[]{:S(2)}, u32[]{:S(2)}) async-start(f32[32,1,128]{2,1,0:T(1,128)} %bitcast.2), calls=%async_computation | async-start | bytes 32768 | tf_op jit(solution)/shard_map/all_to_all | solution.py:822
  52.9 0.0 copy-start
  52.9 2.1 %copy-done = f32[7552,128]{1,0:T(8,128)S(1)} copy-done((f32[7552,128]{1,0:T(8,128)S(1)}, f32[7552,128]{1,0:T(8,128)}, u32[]{:S(2)}) %copy-start) | copy-done | bytes 3866648
  55.0 1.6 %turned.1 = f32[46,128,128]{2,1,0:T(8,128)S(1)} custom-call(f32[7552,128]{1,0:T(8,128)S(1)} %copy-done), custom_call_target="tpu_custom_call" | custom-call | flops 4000000 | bytes 8000000 | tf_op jit(solution)/shard_map/turned/pallas_call | solution.py:824
  56.7 3.3 %all-to-all-done = f32[32,1,128]{2,1,0:T(1,128)S(1)} async-done(((f32[32,1,128]{2,1,0:T(1,128)}), f32[32,1,128]{2,1,0:T(1,128)S(1)}, u32[]{:S(2)}, u32[]{:S(2)}) %all-to-all-start) | async-done | bytes 16416 | tf_op jit(solution)/shard_map/all_to_all | solution.py:822
  60.0 2.4 %pressure.1 = (f32[32,2048]{1,0:T(8,128)}, f32[16,512]{1,0:T(8,128)}) custom-call(s32[1]{0:T(128)} %bitcast.me_ref, f32[32,128]{1,0:T(8,128)S(1)} %bitcast.5, f32[46,128,128]{2,1,0:T(8,128)S(1)} %turned.1), custom_call_target="tpu_custom_call" | custom-call | tf_op jit(solution)/shard_map/pressure/pallas_call | solution.py:835
  (4 shorter events, 0.0 us)
Async XLA Ops:
  1.7 8.6 %collective-permute-start = (f32[3,4,2048]{2,1,0:T(4,128)S(1)}, f32[3,4,2048]{2,1,0:T(4,128)S(1)}, u32[]{:S(2)}, u32[]{:S(2)}) collective-permute-start(f32[3,4,2048]{2,1,0:T(4,128)S(1)} %get-tuple-element.9), channel_id=1, source_target_pairs={{0,8},{8,16},{16,24},{24,0},{1,9},{9,17},{17,25},{25,1},{2,10},{10... | collective-permute-start | bytes 294920 | tf_op jit(solution)/shard_map/ppermute | solution.py:772
  4.8 6.4 %collective-permute-start.1 = (f32[3,4,2048]{2,1,0:T(4,128)S(1)}, f32[3,4,2048]{2,1,0:T(4,128)S(1)}, u32[]{:S(2)}, u32[]{:S(2)}) collective-permute-start(f32[3,4,2048]{2,1,0:T(4,128)S(1)} %get-tuple-element.8), channel_id=1, source_target_pairs={{0,24},{8,0},{16,8},{24,16},{1,25},{9,1},{17,9},{25,17},{2,26},{10... | collective-permute-start | bytes 294920 | tf_op jit(solution)/shard_map/ppermute | solution.py:772
  11.1 4.6 %collective-permute-start.2 = (f32[3,40,128]{2,1,0:T(8,128)S(1)}, f32[3,40,128]{2,1,0:T(8,128)S(1)}, u32[]{:S(2)}, u32[]{:S(2)}) collective-permute-start(f32[3,40,128]{2,1,0:T(8,128)S(1)} %pad_maximum_fusion), channel_id=1, source_target_pairs={{0,1},{1,2},{2,3},{3,4},{4,5},{5,6},{6,7},{7,0},{8,9},{9,10},{10,1... | collective-permute-start | bytes 184328 | tf_op jit(solution)/shard_map/ppermute | solution.py:772
  11.2 4.5 %collective-permute-start.3 = (f32[3,40,128]{2,1,0:T(8,128)S(1)}, f32[3,40,128]{2,1,0:T(8,128)S(1)}, u32[]{:S(2)}, u32[]{:S(2)}) collective-permute-start(f32[3,40,128]{2,1,0:T(8,128)S(1)} %pad_maximum_fusion.1), channel_id=1, source_target_pairs={{0,7},{1,0},{2,1},{3,2},{4,3},{5,4},{6,5},{7,6},{8,15},{9,8},{10,9... | collective-permute-start | bytes 184328 | tf_op jit(solution)/shard_map/ppermute | solution.py:772
  13.9 1.1 %copy-start.1 = (f32[3,32,2048]{2,1,0:T(8,128)S(1)}, f32[3,32,2048]{2,1,0:T(8,128)}, u32[]{:S(2)}) copy-start(f32[3,32,2048]{2,1,0:T(8,128)} %center.1) | copy-start | bytes 2359300
  48.0 12.0 %all-to-all-start = ((f32[32,1,128]{2,1,0:T(1,128)}), f32[32,1,128]{2,1,0:T(1,128)S(1)}, u32[]{:S(2)}, u32[]{:S(2)}) async-start(f32[32,1,128]{2,1,0:T(1,128)} %bitcast.2), calls=%async_computation | async-start | bytes 32768 | tf_op jit(solution)/shard_map/all_to_all | solution.py:822
  52.9 2.1 %copy-start = (f32[7552,128]{1,0:T(8,128)S(1)}, f32[7552,128]{1,0:T(8,128)}, u32[]{:S(2)}) copy-start(f32[7552,128]{1,0:T(8,128)} %get-tuple-element.5.phi) | copy-start | bytes 11599876

commit v10 on v7

--- a/solution.py
+++ b/solution.py
@@ -230,20 +230,31 @@
     return lv.edge * EZ * lv.edz // LANES
 
 
-def looped(count, group, sums, step):
-    def body(t, sums):
-        return tuple(a + b for a, b in zip(sums, step(t * group)))
-
-    start = tuple(jnp.zeros((SUBS, LANES), F32) for _ in range(sums))
-    return list(lax.fori_loop(0, count // group, body, start))
-
-
-def start_residual(case, group):
+def together(works):
+    zero = jnp.zeros((SUBS, LANES), F32)
+    sums = [tuple(zero for _ in range(number)) for _, number, _, _ in works]
+    done = 0
+    for stop in sorted({count for count, _, _, _ in works}):
+        active = [n for n, work in enumerate(works) if work[0] > done]
+
+        def body(z, carry, active=active):
+            return tuple(
+                tuple(a + b for a, b in zip(old, works[n][2](z))) for n, old in zip(active, carry)
+            )
+
+        got = lax.fori_loop(done, stop, body, tuple(sums[n] for n in active))
+        for n, part in zip(active, got):
+            sums[n] = part
+        done = stop
+    return [work[3](list(part)) for work, part in zip(works, sums)]
+
+
+def start_residual(case):
     lv, cs, s = case.lv, case.cs, case.lv.seg
 
     def step(z0):
         total = [[], []]
-        for z in [z0 + n for n in range(group)]:
+        for z in [z0]:
             get, below = case.weights(z + 1), case.weights(z)
             gz = cs.fz(z + 1)
             last = [get(1, i, s - 1) * cs.along_y[i] for i in range(s)]
@@ -267,7 +278,7 @@
                 before = flux_y
         return [tree(t) for t in total]
 
-    return looped(lv.inner, group, 2, step)
+    return lv.inner, 2, step, lambda sums: sums
 
 
 def row_jumps(u, s, j):
@@ -276,7 +287,7 @@
     return jump_x, jump_y
 
 
-def apply(case, group, number, betas):
+def apply(case, number, betas):
     lv, cs, s = case.lv, case.cs, case.lv.seg
     keep = number < 2
     n = lv.tiles
@@ -306,7 +317,7 @@
         total = [[], []]
         u = [[case.d[number][z0, h * n + k] for k in range(n)] for h in HALVES]
         flux_z = [[case.fz[h * n + k] for k in range(n)] for h in HALVES] if keep else None
-        for z in [z0 + t for t in range(group)]:
+        for z in [z0]:
             get = case.weights(z + 1)
             after = [[None] * n for _ in HALVES]
             if keep:
@@ -346,16 +357,16 @@
                     case.fz[h * n + k] = flux_z[h][k]
         return [tree(t) for t in total]
 
-    return [a + b for a, b in zip(looped(lv.inner, group, 2, step), firsts)]
-
-
-def reduce_residual(case, group, number, alphas):
+    return lv.inner, 2, step, lambda sums: [a + b for a, b in zip(sums, firsts)]
+
+
+def reduce_residual(case, number, alphas):
     lv = case.lv
 
     def step(z0):
         total = [[], []]
         source = case.d[0] if number == 0 else case.r
-        for z in [z0 + n for n in range(group)]:
+        for z in [z0]:
             for h in HALVES:
                 squares = []
                 for k in range(lv.tiles):
@@ -366,10 +377,10 @@
                 total[h].append(tree(squares))
         return [tree(t) for t in total]
 
-    return looped(lv.inner, group, 2, step)
-
-
-def finish(case, group, alphas, refs, send):
+    return lv.inner, 2, step, lambda sums: sums
+
+
+def finish(case, alphas, refs, send):
     lv, cs, s = case.lv, case.cs, case.lv.seg
     n = lv.tiles
     f_ref, p_ref, y_ref = refs
@@ -406,11 +417,10 @@
     def cut(values, table):
         return [v if f is None else v * f for v, f in zip(values, table)]
 
-    def body(t, _):
-        z0 = t * group
+    def step(z0):
         u = [f_ref[at(z0, k), :] for k in range(n)]
         flux_z = [case.fz[k] for k in range(n)]
-        for z in [z0 + m for m in range(group)]:
+        for z in [z0]:
             get = case.weights(z + lv.mz)
             up = jnp.minimum(z + 1, lv.edz - 1)
             gz = cs.fz(up + lv.mz)
@@ -435,12 +445,16 @@
             u = after
         for k in range(n):
             case.fz[k] = flux_z[k]
-        for z in [z0 + m for m in range(group)]:
+        for z in [z0]:
             for h in HALVES:
                 send(h, z).start()
-        return 0
-
-    lax.fori_loop(0, lv.edz // group, body, 0)
+        return ()
+
+    return lv.edz, 0, step, lambda _: corner_pairs(lv, refs)
+
+
+def corner_pairs(lv, refs):
+    f_ref, p_ref, y_ref = refs
     pairs = jnp.zeros((2 * LANES, LANES), F32)
     for start in range(0, padded_rows(lv), CHUNK):
         part = slice(start, start + CHUNK)
@@ -460,9 +474,6 @@
         value = tree([value[r : r + SUBS] for r in range(0, LANES, SUBS)])
         out.append(value)
     return out
-
-
-GROUPS = {FINE: 1, TWIN: 8}
 
 
 def place_kernel(center, out_ref):
@@ -539,20 +550,19 @@
         cases.append(case)
 
     def both_levels(work):
-        sums = [work(n, case, GROUPS[case.lv]) for n, case in enumerate(cases)]
-        return [[problem_sum(v) for v in part] for part in sums]
-
-    rr = both_levels(lambda n, case, group: start_residual(case, group))
+        return [[problem_sum(v) for v in part] for part in together([work(n, case) for n, case in enumerate(cases)])]
+
+    rr = both_levels(lambda n, case: start_residual(case))
     alphas = [[[], []] for _ in LEVELS]
     betas = [None] * len(LEVELS)
     for step in range(3):
-        dots = both_levels(lambda n, case, group: apply(case, group, step, betas[n]))
+        dots = both_levels(lambda n, case: apply(case, step, betas[n]))
         now = [[a / b for a, b in zip(rr[n], dots[n])] for n in range(len(LEVELS))]
         for n in range(len(LEVELS)):
             for h in HALVES:
                 alphas[n][h].append(now[n][h])
         if step < 2:
-            new = both_levels(lambda n, case, group: reduce_residual(case, group, step, now[n]))
+            new = both_levels(lambda n, case: reduce_residual(case, step, now[n]))
             betas = [[a / b for a, b in zip(new[n], rr[n])] for n in range(len(LEVELS))]
             rr = new
 
@@ -570,7 +580,7 @@
         )
 
     totals = both_levels(
-        lambda n, case, group: finish(case, group, alphas[n], results[n], functools.partial(send, n))
+        lambda n, case: finish(case, alphas[n], results[n], functools.partial(send, n))
     )
     _, element, _, slot = lane_parts()
     packed = []

time: 59.1 us -> 58.6 us (level)
  no operation moved by 1% of the time
where the time goes in v10:
time: 58.6 us; the launch traced here: 58.3 us
  Pallas kernels  32.2 us (55%)
  starting transfers between devices  12.8 us (22%)
  waiting for transfers between devices  7.41 us (13%)
  local copies, waits for them, and re-layouts  5.12 us (9%)
  between operations  0.7 us (1%)
    pallas_call x1, Pallas kernels, shards(): pl.pallas_call(solve_kernel, out_shape=[pltpu.HBM((sum((2 * field_rows(lv...  28.1 us
    ppermute x4, starting transfers between devices, sent(): lax.ppermute(value, axis, [(i, (i + shift) % count) for i in range(count)])  7.9 us
    all_to_all x1, starting transfers between devices, shards(): gathered = lax.all_to_all(message, ('gx', 'gy'), 0, 0, tiled=True)  4.94 us
    ppermute x4, waiting for transfers between devices, sent(): lax.ppermute(value, axis, [(i, (i + shift) % count) for i in range(count)])  4.07 us
    all_to_all x1, waiting for transfers between devices, shards(): gathered = lax.all_to_all(message, ('gx', 'gy'), 0, 0, tiled=True)  3.33 us
    unnamed x4, local copies, waits for them, and re-layouts  3.22 us
    pallas_call x1, Pallas kernels, shards(): pl.pallas_call(functools.partial(pressure_kernel, gy), out_shape=[jax.Sha...  2.38 us
    pallas_call x1, Pallas kernels, shards(): pl.pallas_call(turn_kernel, out_shape=vmem((tiles, LANES, LANES)), in_spe...  1.63 us
  transfers between devices with their start and end apart: 5, of which 4 were waited for; matrix products, arithmetic and copies ran while one was open for 1% of the time, Pallas kernels for 3%

profile of v10, /device:TPU:0, one launch (start us, length us, event | category | flops | bytes accessed | tf_op | source)
XLA Modules:
  0.0 58.3 jit_solution(792332743926789443)
XLA Ops:
  0.6 1.1 %fusion.1 = (f32[3,4,2048]{2,1,0:T(4,128)S(1)}, f32[3,4,2048]{2,1,0:T(4,128)S(1)}) fusion(f32[3,32,2048]{2,1,0:T(8,128)} %center.1), kind=kLoop, calls=%fused_computation.3 | loop fusion | bytes 393216 | tf_op jit(solution)/shard_map/slice | solution.py:738
  1.7 3.1 %collective-permute-start = (f32[3,4,2048]{2,1,0:T(4,128)S(1)}, f32[3,4,2048]{2,1,0:T(4,128)S(1)}, u32[]{:S(2)}, u32[]{:S(2)}) collective-permute-start(f32[3,4,2048]{2,1,0:T(4,128)S(1)} %get-tuple-element.9), channel_id=1, source_target_pairs={{0,8},{8,16},{16,24},{24,0},{1,9},{9,17},{17,25},{25,1},{2,10},{10... | collective-permute-start | bytes 294920 | tf_op jit(solution)/shard_map/ppermute | solution.py:735
  4.8 2.1 %collective-permute-start.1 = (f32[3,4,2048]{2,1,0:T(4,128)S(1)}, f32[3,4,2048]{2,1,0:T(4,128)S(1)}, u32[]{:S(2)}, u32[]{:S(2)}) collective-permute-start(f32[3,4,2048]{2,1,0:T(4,128)S(1)} %get-tuple-element.8), channel_id=1, source_target_pairs={{0,24},{8,0},{16,8},{24,16},{1,25},{9,1},{17,9},{25,17},{2,26},{10... | collective-permute-start | bytes 294920 | tf_op jit(solution)/shard_map/ppermute | solution.py:735
  6.9 0.8 %fusion = (f32[3,32,128]{2,1,0:T(8,128)S(1)}, f32[3,32,128]{2,1,0:T(8,128)S(1)}) fusion(f32[3,32,2048]{2,1,0:T(8,128)} %center.1), kind=kLoop, calls=%fused_computation.2 | loop fusion | bytes 196608 | tf_op jit(solution)/shard_map/slice | solution.py:741
  7.7 2.6 %collective-permute-done.x_low = f32[3,4,2048]{2,1,0:T(4,128)S(1)} collective-permute-done((f32[3,4,2048]{2,1,0:T(4,128)S(1)}, f32[3,4,2048]{2,1,0:T(4,128)S(1)}, u32[]{:S(2)}, u32[]{:S(2)}) %collective-permute-start) | collective-permute-done | bytes 98336 | tf_op jit(solution)/shard_map/ppermute | solution.py:735
  10.3 0.8 %collective-permute-done.1.x_high = f32[3,4,2048]{2,1,0:T(4,128)S(1)} collective-permute-done((f32[3,4,2048]{2,1,0:T(4,128)S(1)}, f32[3,4,2048]{2,1,0:T(4,128)S(1)}, u32[]{:S(2)}, u32[]{:S(2)}) %collective-permute-start.1) | collective-permute-done | bytes 98336 | tf_op jit(solution)/shard_map/ppermute | solution.py:735
  11.1 0.1 collective-permute-start.2
  11.2 2.7 %collective-permute-start.3 = (f32[3,40,128]{2,1,0:T(8,128)S(1)}, f32[3,40,128]{2,1,0:T(8,128)S(1)}, u32[]{:S(2)}, u32[]{:S(2)}) collective-permute-start(f32[3,40,128]{2,1,0:T(8,128)S(1)} %pad_maximum_fusion.1), channel_id=1, source_target_pairs={{0,7},{1,0},{2,1},{3,2},{4,3},{5,4},{6,5},{7,6},{8,15},{9,8},{10,9... | collective-permute-start | bytes 184328 | tf_op jit(solution)/shard_map/ppermute | solution.py:735
  13.9 0.0 copy-start.1
  13.9 1.1 %copy-done.1 = f32[3,32,2048]{2,1,0:T(8,128)S(1)} copy-done((f32[3,32,2048]{2,1,0:T(8,128)S(1)}, f32[3,32,2048]{2,1,0:T(8,128)}, u32[]{:S(2)}) %copy-start.1) | copy-done | bytes 786456
  15.0 0.1 place.1.inside
  15.1 0.6 %collective-permute-done.2.y_low = f32[3,40,128]{2,1,0:T(8,128)S(1)} collective-permute-done((f32[3,40,128]{2,1,0:T(8,128)S(1)}, f32[3,40,128]{2,1,0:T(8,128)S(1)}, u32[]{:S(2)}, u32[]{:S(2)}) %collective-permute-start.2) | collective-permute-done | bytes 61472 | tf_op jit(solution)/shard_map/ppermute | solution.py:735
  15.7 0.0 collective-permute-done.3.y_high
  15.8 28.1 %solve.1 = (f32[7552,128]{1,0:T(8,128)}, f32[32,128]{1,0:T(8,128)}) custom-call(f32[128,2048]{1,0:T(8,128)S(1)} %place.1.inside, f32[3,4,2048]{2,1,0:T(4,128)S(1)} %collective-permute-done.x_low, f32[3,4,2048]{2,1,0:T(4,128)S(1)} %collective-permute-done.1.x_high, f32[3,40,128]{2,1,0:T(8,128)S(1)} %collective-permute-done.2.y_low, ...), custom_call_target="tpu_custom_call" | custom-call | tf_op jit(solution)/shard_map/solve/pallas_call | solution.py:773
  43.9 4.9 %all-to-all-start = ((f32[32,1,128]{2,1,0:T(1,128)}), f32[32,1,128]{2,1,0:T(1,128)S(1)}, u32[]{:S(2)}, u32[]{:S(2)}) async-start(f32[32,1,128]{2,1,0:T(1,128)} %bitcast.2), calls=%async_computation | async-start | bytes 32768 | tf_op jit(solution)/shard_map/all_to_all | solution.py:785
  48.9 0.0 copy-start
  48.9 2.1 %copy-done = f32[7552,128]{1,0:T(8,128)S(1)} copy-done((f32[7552,128]{1,0:T(8,128)S(1)}, f32[7552,128]{1,0:T(8,128)}, u32[]{:S(2)}) %copy-start) | copy-done | bytes 3866648
  51.0 1.6 %turned.1 = f32[46,128,128]{2,1,0:T(8,128)S(1)} custom-call(f32[7552,128]{1,0:T(8,128)S(1)} %copy-done), custom_call_target="tpu_custom_call" | custom-call | flops 4000000 | bytes 8000000 | tf_op jit(solution)/shard_map/turned/pallas_call | solution.py:787
  52.6 3.3 %all-to-all-done = f32[32,1,128]{2,1,0:T(1,128)S(1)} async-done(((f32[32,1,128]{2,1,0:T(1,128)}), f32[32,1,128]{2,1,0:T(1,128)S(1)}, u32[]{:S(2)}, u32[]{:S(2)}) %all-to-all-start) | async-done | bytes 16416 | tf_op jit(solution)/shard_map/all_to_all | solution.py:785
  55.9 2.4 %pressure.1 = (f32[32,2048]{1,0:T(8,128)}, f32[16,512]{1,0:T(8,128)}) custom-call(s32[1]{0:T(128)} %bitcast.me_ref, f32[32,128]{1,0:T(8,128)S(1)} %bitcast.5, f32[46,128,128]{2,1,0:T(8,128)S(1)} %turned.1), custom_call_target="tpu_custom_call" | custom-call | tf_op jit(solution)/shard_map/pressure/pallas_call | solution.py:798
  (4 shorter events, 0.0 us)
Async XLA Ops:
  1.7 8.6 %collective-permute-start = (f32[3,4,2048]{2,1,0:T(4,128)S(1)}, f32[3,4,2048]{2,1,0:T(4,128)S(1)}, u32[]{:S(2)}, u32[]{:S(2)}) collective-permute-start(f32[3,4,2048]{2,1,0:T(4,128)S(1)} %get-tuple-element.9), channel_id=1, source_target_pairs={{0,8},{8,16},{16,24},{24,0},{1,9},{9,17},{17,25},{25,1},{2,10},{10... | collective-permute-start | bytes 294920 | tf_op jit(solution)/shard_map/ppermute | solution.py:735
  4.8 6.4 %collective-permute-start.1 = (f32[3,4,2048]{2,1,0:T(4,128)S(1)}, f32[3,4,2048]{2,1,0:T(4,128)S(1)}, u32[]{:S(2)}, u32[]{:S(2)}) collective-permute-start(f32[3,4,2048]{2,1,0:T(4,128)S(1)} %get-tuple-element.8), channel_id=1, source_target_pairs={{0,24},{8,0},{16,8},{24,16},{1,25},{9,1},{17,9},{25,17},{2,26},{10... | collective-permute-start | bytes 294920 | tf_op jit(solution)/shard_map/ppermute | solution.py:735
  11.1 4.6 %collective-permute-start.2 = (f32[3,40,128]{2,1,0:T(8,128)S(1)}, f32[3,40,128]{2,1,0:T(8,128)S(1)}, u32[]{:S(2)}, u32[]{:S(2)}) collective-permute-start(f32[3,40,128]{2,1,0:T(8,128)S(1)} %pad_maximum_fusion), channel_id=1, source_target_pairs={{0,1},{1,2},{2,3},{3,4},{4,5},{5,6},{6,7},{7,0},{8,9},{9,10},{10,1... | collective-permute-start | bytes 184328 | tf_op jit(solution)/shard_map/ppermute | solution.py:735
  11.2 4.5 %collective-permute-start.3 = (f32[3,40,128]{2,1,0:T(8,128)S(1)}, f32[3,40,128]{2,1,0:T(8,128)S(1)}, u32[]{:S(2)}, u32[]{:S(2)}) collective-permute-start(f32[3,40,128]{2,1,0:T(8,128)S(1)} %pad_maximum_fusion.1), channel_id=1, source_target_pairs={{0,7},{1,0},{2,1},{3,2},{4,3},{5,4},{6,5},{7,6},{8,15},{9,8},{10,9... | collective-permute-start | bytes 184328 | tf_op jit(solution)/shard_map/ppermute | solution.py:735
  13.9 1.1 %copy-start.1 = (f32[3,32,2048]{2,1,0:T(8,128)S(1)}, f32[3,32,2048]{2,1,0:T(8,128)}, u32[]{:S(2)}) copy-start(f32[3,32,2048]{2,1,0:T(8,128)} %center.1) | copy-start | bytes 2359300
  43.9 12.0 %all-to-all-start = ((f32[32,1,128]{2,1,0:T(1,128)}), f32[32,1,128]{2,1,0:T(1,128)S(1)}, u32[]{:S(2)}, u32[]{:S(2)}) async-start(f32[32,1,128]{2,1,0:T(1,128)} %bitcast.2), calls=%async_computation | async-start | bytes 32768 | tf_op jit(solution)/shard_map/all_to_all | solution.py:785
  48.9 2.1 %copy-start = (f32[7552,128]{1,0:T(8,128)S(1)}, f32[7552,128]{1,0:T(8,128)}, u32[]{:S(2)}) copy-start(f32[7552,128]{1,0:T(8,128)} %get-tuple-element.5.phi) | copy-start | bytes 11599876

commit v11 on v9

--- a/solution.py
+++ b/solution.py
@@ -230,21 +230,32 @@
     return lv.edge * EZ * lv.edz // LANES
 
 
-def looped(count, group, sums, step):
-    def body(t, sums):
-        return tuple(a + b for a, b in zip(sums, step(t * group)))
-
-    start = tuple(jnp.zeros((SUBS, LANES), F32) for _ in range(sums))
-    return list(lax.fori_loop(0, count // group, body, start))
-
-
-def start_residual(case, group):
+def together(works):
+    zero = jnp.zeros((SUBS, LANES), F32)
+    sums = [tuple(zero for _ in range(number)) for _, number, _, _ in works]
+    done = 0
+    for stop in sorted({count for count, _, _, _ in works}):
+        active = [n for n, work in enumerate(works) if work[0] > done]
+
+        def body(z, carry, active=active):
+            return tuple(
+                tuple(a + b for a, b in zip(old, works[n][2](z))) for n, old in zip(active, carry)
+            )
+
+        got = lax.fori_loop(done, stop, body, tuple(sums[n] for n in active))
+        for n, part in zip(active, got):
+            sums[n] = part
+        done = stop
+    return [work[3](list(part)) for work, part in zip(works, sums)]
+
+
+def start_residual(case):
     lv, cs, s = case.lv, case.cs, case.lv.seg
 
     def step(z0):
         total = [[], []]
         stores = []
-        for z in [z0 + n for n in range(group)]:
+        for z in [z0]:
             get, below = case.weights(z + 1), case.weights(z)
             gz = cs.fz(z + 1)
             last = [get(1, i, s - 1) * cs.along_y[i] for i in range(s)]
@@ -274,7 +285,7 @@
             case.d[0][index] = value
         return [tree(t) for t in total]
 
-    return looped(lv.inner, group, 2, step)
+    return lv.inner, 2, step, lambda sums: sums
 
 
 def x_jumps(row, s):
@@ -378,16 +389,16 @@
         flush()
         return [tree(t) for t in total]
 
-    return [a + b for a, b in zip(looped(lv.inner, 1, 2, step), firsts)]
-
-
-def reduce_residual(case, group, number, alphas):
+    return lv.inner, 2, step, lambda sums: [a + b for a, b in zip(sums, firsts)]
+
+
+def reduce_residual(case, number, alphas):
     lv = case.lv
 
     def step(z0):
         total = [[], []]
         source = case.d[0] if number == 0 else case.r
-        for z in [z0 + n for n in range(group)]:
+        for z in [z0]:
             for h in HALVES:
                 cells = range(h * lv.tiles, (h + 1) * lv.tiles)
                 values = [source[z, at] - alphas[h] * case.q[z, at] for at in cells]
@@ -396,7 +407,7 @@
                 total[h].append(tree([v * v for v in values]))
         return [tree(t) for t in total]
 
-    return looped(lv.inner, group, 2, step)
+    return lv.inner, 2, step, lambda sums: sums
 
 
 def finish(case, alphas, refs, send):
@@ -435,7 +446,7 @@
     def cut(values, table):
         return [v if f is None else v * f for v, f in zip(values, table)]
 
-    def body(z, _):
+    def step(z):
         get = case.weights(z + lv.mz)
         up = jnp.minimum(z + 1, lv.edz - 1)
         gz = cs.fz(up + lv.mz)
@@ -485,9 +496,13 @@
         flush()
         for h in HALVES:
             send(h, z).start()
-        return 0
-
-    lax.fori_loop(0, lv.edz, body, 0)
+        return ()
+
+    return lv.edz, 0, step, lambda _: corner_pairs(lv, refs)
+
+
+def corner_pairs(lv, refs):
+    f_ref, p_ref, y_ref = refs
     pairs = jnp.zeros((2 * LANES, LANES), F32)
     for start in range(0, padded_rows(lv), CHUNK):
         part = slice(start, start + CHUNK)
@@ -507,9 +522,6 @@
         value = tree([value[r : r + SUBS] for r in range(0, LANES, SUBS)])
         out.append(value)
     return out
-
-
-GROUPS = {FINE: 1, TWIN: 4}
 
 
 def place_kernel(center, out_ref):
@@ -586,20 +598,19 @@
         cases.append(case)
 
     def both_levels(work):
-        sums = [work(n, case, GROUPS[case.lv]) for n, case in enumerate(cases)]
-        return [[problem_sum(v) for v in part] for part in sums]
-
-    rr = both_levels(lambda n, case, group: start_residual(case, group))
+        return [[problem_sum(v) for v in part] for part in together([work(n, case) for n, case in enumerate(cases)])]
+
+    rr = both_levels(lambda n, case: start_residual(case))
     alphas = [[[], []] for _ in LEVELS]
     betas = [None] * len(LEVELS)
     for step in range(3):
-        dots = both_levels(lambda n, case, group: apply(case, step, betas[n]))
+        dots = both_levels(lambda n, case: apply(case, step, betas[n]))
         now = [[a / b for a, b in zip(rr[n], dots[n])] for n in range(len(LEVELS))]
         for n in range(len(LEVELS)):
             for h in HALVES:
                 alphas[n][h].append(now[n][h])
         if step < 2:
-            new = both_levels(lambda n, case, group: reduce_residual(case, group, step, now[n]))
+            new = both_levels(lambda n, case: reduce_residual(case, step, now[n]))
             betas = [[a / b for a, b in zip(new[n], rr[n])] for n in range(len(LEVELS))]
             rr = new
 
@@ -617,7 +628,7 @@
         )
 
     totals = both_levels(
-        lambda n, case, group: finish(case, alphas[n], results[n], functools.partial(send, n))
+        lambda n, case: finish(case, alphas[n], results[n], functools.partial(send, n))
     )
     _, element, _, slot = lane_parts()
     packed = []

time: 62.7 us -> 59.1 us (0.943)
  Pallas kernels: 36.3 us -> 32.7 us
    pallas_call x1, Pallas kernels: 32.2 us -> 28.6 us  [shards(): pl.pallas_call(solve_kernel, out_shape=[pltpu.HBM((sum((2 * field_rows(lv...]
where the time goes in v11:
time: 59.1 us; the launch traced here: 58.8 us
  Pallas kernels  32.7 us (55%)
  starting transfers between devices  12.8 us (22%)
  waiting for transfers between devices  7.41 us (13%)
  local copies, waits for them, and re-layouts  5.12 us (9%)
  between operations  0.7 us (1%)
    pallas_call x1, Pallas kernels, shards(): pl.pallas_call(solve_kernel, out_shape=[pltpu.HBM((sum((2 * field_rows(lv...  28.6 us
    ppermute x4, starting transfers between devices, sent(): lax.ppermute(value, axis, [(i, (i + shift) % count) for i in range(count)])  7.9 us
    all_to_all x1, starting transfers between devices, shards(): gathered = lax.all_to_all(message, ('gx', 'gy'), 0, 0, tiled=True)  4.94 us
    ppermute x4, waiting for transfers between devices, sent(): lax.ppermute(value, axis, [(i, (i + shift) % count) for i in range(count)])  4.07 us
    all_to_all x1, waiting for transfers between devices, shards(): gathered = lax.all_to_all(message, ('gx', 'gy'), 0, 0, tiled=True)  3.33 us
    unnamed x4, local copies, waits for them, and re-layouts  3.22 us
    pallas_call x1, Pallas kernels, shards(): pl.pallas_call(functools.partial(pressure_kernel, gy), out_shape=[jax.Sha...  2.38 us
    pallas_call x1, Pallas kernels, shards(): pl.pallas_call(turn_kernel, out_shape=vmem((tiles, LANES, LANES)), in_spe...  1.63 us
  transfers between devices with their start and end apart: 5, of which 4 were waited for; matrix products, arithmetic and copies ran while one was open for 1% of the time, Pallas kernels for 3%

profile of v11, /device:TPU:0, one launch (start us, length us, event | category | flops | bytes accessed | tf_op | source)
XLA Modules:
  0.0 58.8 jit_solution(13851224625570494098)
XLA Ops:
  0.6 1.1 %fusion.1 = (f32[3,4,2048]{2,1,0:T(4,128)S(1)}, f32[3,4,2048]{2,1,0:T(4,128)S(1)}) fusion(f32[3,32,2048]{2,1,0:T(8,128)} %center.1), kind=kLoop, calls=%fused_computation.3 | loop fusion | bytes 393216 | tf_op jit(solution)/shard_map/slice | solution.py:786
  1.7 3.1 %collective-permute-start = (f32[3,4,2048]{2,1,0:T(4,128)S(1)}, f32[3,4,2048]{2,1,0:T(4,128)S(1)}, u32[]{:S(2)}, u32[]{:S(2)}) collective-permute-start(f32[3,4,2048]{2,1,0:T(4,128)S(1)} %get-tuple-element.9), channel_id=1, source_target_pairs={{0,8},{8,16},{16,24},{24,0},{1,9},{9,17},{17,25},{25,1},{2,10},{10... | collective-permute-start | bytes 294920 | tf_op jit(solution)/shard_map/ppermute | solution.py:783
  4.8 2.1 %collective-permute-start.1 = (f32[3,4,2048]{2,1,0:T(4,128)S(1)}, f32[3,4,2048]{2,1,0:T(4,128)S(1)}, u32[]{:S(2)}, u32[]{:S(2)}) collective-permute-start(f32[3,4,2048]{2,1,0:T(4,128)S(1)} %get-tuple-element.8), channel_id=1, source_target_pairs={{0,24},{8,0},{16,8},{24,16},{1,25},{9,1},{17,9},{25,17},{2,26},{10... | collective-permute-start | bytes 294920 | tf_op jit(solution)/shard_map/ppermute | solution.py:783
  6.9 0.8 %fusion = (f32[3,32,128]{2,1,0:T(8,128)S(1)}, f32[3,32,128]{2,1,0:T(8,128)S(1)}) fusion(f32[3,32,2048]{2,1,0:T(8,128)} %center.1), kind=kLoop, calls=%fused_computation.2 | loop fusion | bytes 196608 | tf_op jit(solution)/shard_map/slice | solution.py:789
  7.7 2.6 %collective-permute-done.x_low = f32[3,4,2048]{2,1,0:T(4,128)S(1)} collective-permute-done((f32[3,4,2048]{2,1,0:T(4,128)S(1)}, f32[3,4,2048]{2,1,0:T(4,128)S(1)}, u32[]{:S(2)}, u32[]{:S(2)}) %collective-permute-start) | collective-permute-done | bytes 98336 | tf_op jit(solution)/shard_map/ppermute | solution.py:783
  10.3 0.8 %collective-permute-done.1.x_high = f32[3,4,2048]{2,1,0:T(4,128)S(1)} collective-permute-done((f32[3,4,2048]{2,1,0:T(4,128)S(1)}, f32[3,4,2048]{2,1,0:T(4,128)S(1)}, u32[]{:S(2)}, u32[]{:S(2)}) %collective-permute-start.1) | collective-permute-done | bytes 98336 | tf_op jit(solution)/shard_map/ppermute | solution.py:783
  11.1 0.1 collective-permute-start.2
  11.2 2.7 %collective-permute-start.3 = (f32[3,40,128]{2,1,0:T(8,128)S(1)}, f32[3,40,128]{2,1,0:T(8,128)S(1)}, u32[]{:S(2)}, u32[]{:S(2)}) collective-permute-start(f32[3,40,128]{2,1,0:T(8,128)S(1)} %pad_maximum_fusion.1), channel_id=1, source_target_pairs={{0,7},{1,0},{2,1},{3,2},{4,3},{5,4},{6,5},{7,6},{8,15},{9,8},{10,9... | collective-permute-start | bytes 184328 | tf_op jit(solution)/shard_map/ppermute | solution.py:783
  13.9 0.0 copy-start.1
  13.9 1.1 %copy-done.1 = f32[3,32,2048]{2,1,0:T(8,128)S(1)} copy-done((f32[3,32,2048]{2,1,0:T(8,128)S(1)}, f32[3,32,2048]{2,1,0:T(8,128)}, u32[]{:S(2)}) %copy-start.1) | copy-done | bytes 786456
  15.0 0.1 place.1.inside
  15.1 0.6 %collective-permute-done.2.y_low = f32[3,40,128]{2,1,0:T(8,128)S(1)} collective-permute-done((f32[3,40,128]{2,1,0:T(8,128)S(1)}, f32[3,40,128]{2,1,0:T(8,128)S(1)}, u32[]{:S(2)}, u32[]{:S(2)}) %collective-permute-start.2) | collective-permute-done | bytes 61472 | tf_op jit(solution)/shard_map/ppermute | solution.py:783
  15.7 0.0 collective-permute-done.3.y_high
  15.8 28.6 %solve.1 = (f32[7552,128]{1,0:T(8,128)}, f32[32,128]{1,0:T(8,128)}) custom-call(f32[128,2048]{1,0:T(8,128)S(1)} %place.1.inside, f32[3,4,2048]{2,1,0:T(4,128)S(1)} %collective-permute-done.x_low, f32[3,4,2048]{2,1,0:T(4,128)S(1)} %collective-permute-done.1.x_high, f32[3,40,128]{2,1,0:T(8,128)S(1)} %collective-permute-done.2.y_low, ...), custom_call_target="tpu_custom_call" | custom-call | tf_op jit(solution)/shard_map/solve/pallas_call | solution.py:821
  44.4 4.9 %all-to-all-start = ((f32[32,1,128]{2,1,0:T(1,128)}), f32[32,1,128]{2,1,0:T(1,128)S(1)}, u32[]{:S(2)}, u32[]{:S(2)}) async-start(f32[32,1,128]{2,1,0:T(1,128)} %bitcast.2), calls=%async_computation | async-start | bytes 32768 | tf_op jit(solution)/shard_map/all_to_all | solution.py:833
  49.4 0.0 copy-start
  49.4 2.1 %copy-done = f32[7552,128]{1,0:T(8,128)S(1)} copy-done((f32[7552,128]{1,0:T(8,128)S(1)}, f32[7552,128]{1,0:T(8,128)}, u32[]{:S(2)}) %copy-start) | copy-done | bytes 3866648
  51.5 1.6 %turned.1 = f32[46,128,128]{2,1,0:T(8,128)S(1)} custom-call(f32[7552,128]{1,0:T(8,128)S(1)} %copy-done), custom_call_target="tpu_custom_call" | custom-call | flops 4000000 | bytes 8000000 | tf_op jit(solution)/shard_map/turned/pallas_call | solution.py:835
  53.1 3.3 %all-to-all-done = f32[32,1,128]{2,1,0:T(1,128)S(1)} async-done(((f32[32,1,128]{2,1,0:T(1,128)}), f32[32,1,128]{2,1,0:T(1,128)S(1)}, u32[]{:S(2)}, u32[]{:S(2)}) %all-to-all-start) | async-done | bytes 16416 | tf_op jit(solution)/shard_map/all_to_all | solution.py:833
  56.4 2.4 %pressure.1 = (f32[32,2048]{1,0:T(8,128)}, f32[16,512]{1,0:T(8,128)}) custom-call(s32[1]{0:T(128)} %bitcast.me_ref, f32[32,128]{1,0:T(8,128)S(1)} %bitcast.5, f32[46,128,128]{2,1,0:T(8,128)S(1)} %turned.1), custom_call_target="tpu_custom_call" | custom-call | tf_op jit(solution)/shard_map/pressure/pallas_call | solution.py:846
  (4 shorter events, 0.0 us)
Async XLA Ops:
  1.7 8.6 %collective-permute-start = (f32[3,4,2048]{2,1,0:T(4,128)S(1)}, f32[3,4,2048]{2,1,0:T(4,128)S(1)}, u32[]{:S(2)}, u32[]{:S(2)}) collective-permute-start(f32[3,4,2048]{2,1,0:T(4,128)S(1)} %get-tuple-element.9), channel_id=1, source_target_pairs={{0,8},{8,16},{16,24},{24,0},{1,9},{9,17},{17,25},{25,1},{2,10},{10... | collective-permute-start | bytes 294920 | tf_op jit(solution)/shard_map/ppermute | solution.py:783
  4.8 6.4 %collective-permute-start.1 = (f32[3,4,2048]{2,1,0:T(4,128)S(1)}, f32[3,4,2048]{2,1,0:T(4,128)S(1)}, u32[]{:S(2)}, u32[]{:S(2)}) collective-permute-start(f32[3,4,2048]{2,1,0:T(4,128)S(1)} %get-tuple-element.8), channel_id=1, source_target_pairs={{0,24},{8,0},{16,8},{24,16},{1,25},{9,1},{17,9},{25,17},{2,26},{10... | collective-permute-start | bytes 294920 | tf_op jit(solution)/shard_map/ppermute | solution.py:783
  11.1 4.6 %collective-permute-start.2 = (f32[3,40,128]{2,1,0:T(8,128)S(1)}, f32[3,40,128]{2,1,0:T(8,128)S(1)}, u32[]{:S(2)}, u32[]{:S(2)}) collective-permute-start(f32[3,40,128]{2,1,0:T(8,128)S(1)} %pad_maximum_fusion), channel_id=1, source_target_pairs={{0,1},{1,2},{2,3},{3,4},{4,5},{5,6},{6,7},{7,0},{8,9},{9,10},{10,1... | collective-permute-start | bytes 184328 | tf_op jit(solution)/shard_map/ppermute | solution.py:783
  11.2 4.5 %collective-permute-start.3 = (f32[3,40,128]{2,1,0:T(8,128)S(1)}, f32[3,40,128]{2,1,0:T(8,128)S(1)}, u32[]{:S(2)}, u32[]{:S(2)}) collective-permute-start(f32[3,40,128]{2,1,0:T(8,128)S(1)} %pad_maximum_fusion.1), channel_id=1, source_target_pairs={{0,7},{1,0},{2,1},{3,2},{4,3},{5,4},{6,5},{7,6},{8,15},{9,8},{10,9... | collective-permute-start | bytes 184328 | tf_op jit(solution)/shard_map/ppermute | solution.py:783
  13.9 1.1 %copy-start.1 = (f32[3,32,2048]{2,1,0:T(8,128)S(1)}, f32[3,32,2048]{2,1,0:T(8,128)}, u32[]{:S(2)}) copy-start(f32[3,32,2048]{2,1,0:T(8,128)} %center.1) | copy-start | bytes 2359300
  44.4 12.0 %all-to-all-start = ((f32[32,1,128]{2,1,0:T(1,128)}), f32[32,1,128]{2,1,0:T(1,128)S(1)}, u32[]{:S(2)}, u32[]{:S(2)}) async-start(f32[32,1,128]{2,1,0:T(1,128)} %bitcast.2), calls=%async_computation | async-start | bytes 32768 | tf_op jit(solution)/shard_map/all_to_all | solution.py:833
  49.4 2.1 %copy-start = (f32[7552,128]{1,0:T(8,128)S(1)}, f32[7552,128]{1,0:T(8,128)}, u32[]{:S(2)}) copy-start(f32[7552,128]{1,0:T(8,128)} %get-tuple-element.5.phi) | copy-start | bytes 11599876

commit v12 on v10

--- a/solution.py
+++ b/solution.py
@@ -141,7 +141,7 @@
     return value
 
 
-def spread_weights(lv, k_ref, high_refs, low_refs, w_refs):
+def split_weights(lv, k_ref, high_refs, low_refs):
     s = lv.seg
     wide = (SUBS, LANES)
     pos = lane_iota(wide)
@@ -180,7 +180,11 @@
                     low_refs[m][t * s + p, :, part] = (both - high.astype(F32)).astype(BF16)
         return 0
 
-    lax.fori_loop(0, lv.planes // 2, planes, 0)
+    return planes
+
+
+def place_weights(lv, high_refs, low_refs, w_refs):
+    s = lv.seg
     rows = lv.planes * s * SUBS
     row = lax.broadcasted_iota(jnp.int32, (2 * LANES, 2 * LANES), 0)
     lane = lax.broadcasted_iota(jnp.int32, (1, 2 * LANES), 1)
@@ -532,7 +536,7 @@
         del refs[:count]
         return got
 
-    cases = []
+    cases, splits, places = [], [], []
     for lv, source in zip(LEVELS, (rows, twin_rows)):
         (k_ref,) = take(1)
         high_refs, low_refs, w_refs = take(3), take(3), take(3)
@@ -542,12 +546,24 @@
                 for c in range(COLUMNS):
                     start = (lv.edge * c + i) * nz + cell
                     k_ref[z, i, :, c * LANES : (c + 1) * LANES] = source[pl.ds(start, SUBS, stride=lv.seg * nz), :]
-        spread_weights(lv, k_ref, high_refs, low_refs, w_refs)
+        splits.append(split_weights(lv, k_ref, high_refs, low_refs))
+        places.append(functools.partial(place_weights, lv, high_refs, low_refs, w_refs))
         case = Case(lv, w_refs, take(5), take(1))
         for k in range(2 * lv.tiles):
             case.d[0][lv.inner, k] = jnp.zeros((SUBS, LANES), F32)
             case.r[lv.inner, k] = jnp.zeros((SUBS, LANES), F32)
         cases.append(case)
+
+    def split(t, _):
+        for step in splits:
+            step(t, 0)
+        return 0
+
+    both = TWIN.planes // 2
+    lax.fori_loop(0, both, split, 0)
+    lax.fori_loop(both, FINE.planes // 2, splits[0], 0)
+    for work in places:
+        work()
 
     def both_levels(work):
         return [[problem_sum(v) for v in part] for part in together([work(n, case) for n, case in enumerate(cases)])]

time: 58.6 us -> 57.5 us (0.981)
  Pallas kernels: 32.2 us -> 31.1 us
    pallas_call x1, Pallas kernels: 28.1 us -> 27 us  [shards(): pl.pallas_call(solve_kernel, out_shape=[pltpu.HBM((sum((2 * field_rows(lv...]
where the time goes in v12:
time: 57.5 us; the launch traced here: 57.2 us
  Pallas kernels  31.1 us (54%)
  starting transfers between devices  12.9 us (22%)
  waiting for transfers between devices  7.41 us (13%)
  local copies, waits for them, and re-layouts  5.12 us (9%)
  between operations  0.7 us (1%)
    pallas_call x1, Pallas kernels, shards(): pl.pallas_call(solve_kernel, out_shape=[pltpu.HBM((sum((2 * field_rows(lv...  27 us
    ppermute x4, starting transfers between devices, sent(): lax.ppermute(value, axis, [(i, (i + shift) % count) for i in range(count)])  7.9 us
    all_to_all x1, starting transfers between devices, shards(): gathered = lax.all_to_all(message, ('gx', 'gy'), 0, 0, tiled=True)  4.95 us
    ppermute x4, waiting for transfers between devices, sent(): lax.ppermute(value, axis, [(i, (i + shift) % count) for i in range(count)])  4.07 us
    all_to_all x1, waiting for transfers between devices, shards(): gathered = lax.all_to_all(message, ('gx', 'gy'), 0, 0, tiled=True)  3.33 us
    unnamed x4, local copies, waits for them, and re-layouts  3.22 us
    pallas_call x1, Pallas kernels, shards(): pl.pallas_call(functools.partial(pressure_kernel, gy), out_shape=[jax.Sha...  2.38 us
    pallas_call x1, Pallas kernels, shards(): pl.pallas_call(turn_kernel, out_shape=vmem((tiles, LANES, LANES)), in_spe...  1.63 us
  transfers between devices with their start and end apart: 5, of which 4 were waited for; matrix products, arithmetic and copies ran while one was open for 1% of the time, Pallas kernels for 3%

profile of v12, /device:TPU:0, one launch (start us, length us, event | category | flops | bytes accessed | tf_op | source)
XLA Modules:
  0.0 57.2 jit_solution(14700942289996101946)
XLA Ops:
  0.6 1.1 %fusion.1 = (f32[3,4,2048]{2,1,0:T(4,128)S(1)}, f32[3,4,2048]{2,1,0:T(4,128)S(1)}) fusion(f32[3,32,2048]{2,1,0:T(8,128)} %center.1), kind=kLoop, calls=%fused_computation.3 | loop fusion | bytes 393216 | tf_op jit(solution)/shard_map/slice | solution.py:754
  1.7 3.1 %collective-permute-start = (f32[3,4,2048]{2,1,0:T(4,128)S(1)}, f32[3,4,2048]{2,1,0:T(4,128)S(1)}, u32[]{:S(2)}, u32[]{:S(2)}) collective-permute-start(f32[3,4,2048]{2,1,0:T(4,128)S(1)} %get-tuple-element.9), channel_id=1, source_target_pairs={{0,8},{8,16},{16,24},{24,0},{1,9},{9,17},{17,25},{25,1},{2,10},{10... | collective-permute-start | bytes 294920 | tf_op jit(solution)/shard_map/ppermute | solution.py:751
  4.8 2.1 %collective-permute-start.1 = (f32[3,4,2048]{2,1,0:T(4,128)S(1)}, f32[3,4,2048]{2,1,0:T(4,128)S(1)}, u32[]{:S(2)}, u32[]{:S(2)}) collective-permute-start(f32[3,4,2048]{2,1,0:T(4,128)S(1)} %get-tuple-element.8), channel_id=1, source_target_pairs={{0,24},{8,0},{16,8},{24,16},{1,25},{9,1},{17,9},{25,17},{2,26},{10... | collective-permute-start | bytes 294920 | tf_op jit(solution)/shard_map/ppermute | solution.py:751
  6.9 0.8 %fusion = (f32[3,32,128]{2,1,0:T(8,128)S(1)}, f32[3,32,128]{2,1,0:T(8,128)S(1)}) fusion(f32[3,32,2048]{2,1,0:T(8,128)} %center.1), kind=kLoop, calls=%fused_computation.2 | loop fusion | bytes 196608 | tf_op jit(solution)/shard_map/slice | solution.py:757
  7.7 2.6 %collective-permute-done.x_low = f32[3,4,2048]{2,1,0:T(4,128)S(1)} collective-permute-done((f32[3,4,2048]{2,1,0:T(4,128)S(1)}, f32[3,4,2048]{2,1,0:T(4,128)S(1)}, u32[]{:S(2)}, u32[]{:S(2)}) %collective-permute-start) | collective-permute-done | bytes 98336 | tf_op jit(solution)/shard_map/ppermute | solution.py:751
  10.3 0.8 %collective-permute-done.1.x_high = f32[3,4,2048]{2,1,0:T(4,128)S(1)} collective-permute-done((f32[3,4,2048]{2,1,0:T(4,128)S(1)}, f32[3,4,2048]{2,1,0:T(4,128)S(1)}, u32[]{:S(2)}, u32[]{:S(2)}) %collective-permute-start.1) | collective-permute-done | bytes 98336 | tf_op jit(solution)/shard_map/ppermute | solution.py:751
  11.1 0.1 collective-permute-start.2
  11.2 2.7 %collective-permute-start.3 = (f32[3,40,128]{2,1,0:T(8,128)S(1)}, f32[3,40,128]{2,1,0:T(8,128)S(1)}, u32[]{:S(2)}, u32[]{:S(2)}) collective-permute-start(f32[3,40,128]{2,1,0:T(8,128)S(1)} %pad_maximum_fusion.1), channel_id=1, source_target_pairs={{0,7},{1,0},{2,1},{3,2},{4,3},{5,4},{6,5},{7,6},{8,15},{9,8},{10,9... | collective-permute-start | bytes 184328 | tf_op jit(solution)/shard_map/ppermute | solution.py:751
  13.9 0.0 copy-start.1
  13.9 1.1 %copy-done.1 = f32[3,32,2048]{2,1,0:T(8,128)S(1)} copy-done((f32[3,32,2048]{2,1,0:T(8,128)S(1)}, f32[3,32,2048]{2,1,0:T(8,128)}, u32[]{:S(2)}) %copy-start.1) | copy-done | bytes 786456
  15.0 0.1 place.1.inside
  15.1 0.6 %collective-permute-done.2.y_low = f32[3,40,128]{2,1,0:T(8,128)S(1)} collective-permute-done((f32[3,40,128]{2,1,0:T(8,128)S(1)}, f32[3,40,128]{2,1,0:T(8,128)S(1)}, u32[]{:S(2)}, u32[]{:S(2)}) %collective-permute-start.2) | collective-permute-done | bytes 61472 | tf_op jit(solution)/shard_map/ppermute | solution.py:751
  15.7 0.0 collective-permute-done.3.y_high
  15.8 27.0 %solve.1 = (f32[7552,128]{1,0:T(8,128)}, f32[32,128]{1,0:T(8,128)}) custom-call(f32[128,2048]{1,0:T(8,128)S(1)} %place.1.inside, f32[3,4,2048]{2,1,0:T(4,128)S(1)} %collective-permute-done.x_low, f32[3,4,2048]{2,1,0:T(4,128)S(1)} %collective-permute-done.1.x_high, f32[3,40,128]{2,1,0:T(8,128)S(1)} %collective-permute-done.2.y_low, ...), custom_call_target="tpu_custom_call" | custom-call | tf_op jit(solution)/shard_map/solve/pallas_call | solution.py:789
  42.8 5.0 %all-to-all-start = ((f32[32,1,128]{2,1,0:T(1,128)}), f32[32,1,128]{2,1,0:T(1,128)S(1)}, u32[]{:S(2)}, u32[]{:S(2)}) async-start(f32[32,1,128]{2,1,0:T(1,128)} %bitcast.2), calls=%async_computation | async-start | bytes 32768 | tf_op jit(solution)/shard_map/all_to_all | solution.py:801
  47.7 0.0 copy-start
  47.8 2.1 %copy-done = f32[7552,128]{1,0:T(8,128)S(1)} copy-done((f32[7552,128]{1,0:T(8,128)S(1)}, f32[7552,128]{1,0:T(8,128)}, u32[]{:S(2)}) %copy-start) | copy-done | bytes 3866648
  49.8 1.6 %turned.1 = f32[46,128,128]{2,1,0:T(8,128)S(1)} custom-call(f32[7552,128]{1,0:T(8,128)S(1)} %copy-done), custom_call_target="tpu_custom_call" | custom-call | flops 4000000 | bytes 8000000 | tf_op jit(solution)/shard_map/turned/pallas_call | solution.py:803
  51.5 3.3 %all-to-all-done = f32[32,1,128]{2,1,0:T(1,128)S(1)} async-done(((f32[32,1,128]{2,1,0:T(1,128)}), f32[32,1,128]{2,1,0:T(1,128)S(1)}, u32[]{:S(2)}, u32[]{:S(2)}) %all-to-all-start) | async-done | bytes 16416 | tf_op jit(solution)/shard_map/all_to_all | solution.py:801
  54.8 2.4 %pressure.1 = (f32[32,2048]{1,0:T(8,128)}, f32[16,512]{1,0:T(8,128)}) custom-call(s32[1]{0:T(128)} %bitcast.me_ref, f32[32,128]{1,0:T(8,128)S(1)} %bitcast.5, f32[46,128,128]{2,1,0:T(8,128)S(1)} %turned.1), custom_call_target="tpu_custom_call" | custom-call | tf_op jit(solution)/shard_map/pressure/pallas_call | solution.py:814
  (4 shorter events, 0.0 us)
Async XLA Ops:
  1.7 8.6 %collective-permute-start = (f32[3,4,2048]{2,1,0:T(4,128)S(1)}, f32[3,4,2048]{2,1,0:T(4,128)S(1)}, u32[]{:S(2)}, u32[]{:S(2)}) collective-permute-start(f32[3,4,2048]{2,1,0:T(4,128)S(1)} %get-tuple-element.9), channel_id=1, source_target_pairs={{0,8},{8,16},{16,24},{24,0},{1,9},{9,17},{17,25},{25,1},{2,10},{10... | collective-permute-start | bytes 294920 | tf_op jit(solution)/shard_map/ppermute | solution.py:751
  4.8 6.4 %collective-permute-start.1 = (f32[3,4,2048]{2,1,0:T(4,128)S(1)}, f32[3,4,2048]{2,1,0:T(4,128)S(1)}, u32[]{:S(2)}, u32[]{:S(2)}) collective-permute-start(f32[3,4,2048]{2,1,0:T(4,128)S(1)} %get-tuple-element.8), channel_id=1, source_target_pairs={{0,24},{8,0},{16,8},{24,16},{1,25},{9,1},{17,9},{25,17},{2,26},{10... | collective-permute-start | bytes 294920 | tf_op jit(solution)/shard_map/ppermute | solution.py:751
  11.1 4.6 %collective-permute-start.2 = (f32[3,40,128]{2,1,0:T(8,128)S(1)}, f32[3,40,128]{2,1,0:T(8,128)S(1)}, u32[]{:S(2)}, u32[]{:S(2)}) collective-permute-start(f32[3,40,128]{2,1,0:T(8,128)S(1)} %pad_maximum_fusion), channel_id=1, source_target_pairs={{0,1},{1,2},{2,3},{3,4},{4,5},{5,6},{6,7},{7,0},{8,9},{9,10},{10,1... | collective-permute-start | bytes 184328 | tf_op jit(solution)/shard_map/ppermute | solution.py:751
  11.2 4.5 %collective-permute-start.3 = (f32[3,40,128]{2,1,0:T(8,128)S(1)}, f32[3,40,128]{2,1,0:T(8,128)S(1)}, u32[]{:S(2)}, u32[]{:S(2)}) collective-permute-start(f32[3,40,128]{2,1,0:T(8,128)S(1)} %pad_maximum_fusion.1), channel_id=1, source_target_pairs={{0,7},{1,0},{2,1},{3,2},{4,3},{5,4},{6,5},{7,6},{8,15},{9,8},{10,9... | collective-permute-start | bytes 184328 | tf_op jit(solution)/shard_map/ppermute | solution.py:751
  13.9 1.1 %copy-start.1 = (f32[3,32,2048]{2,1,0:T(8,128)S(1)}, f32[3,32,2048]{2,1,0:T(8,128)}, u32[]{:S(2)}) copy-start(f32[3,32,2048]{2,1,0:T(8,128)} %center.1) | copy-start | bytes 2359300
  42.8 12.0 %all-to-all-start = ((f32[32,1,128]{2,1,0:T(1,128)}), f32[32,1,128]{2,1,0:T(1,128)S(1)}, u32[]{:S(2)}, u32[]{:S(2)}) async-start(f32[32,1,128]{2,1,0:T(1,128)} %bitcast.2), calls=%async_computation | async-start | bytes 32768 | tf_op jit(solution)/shard_map/all_to_all | solution.py:801
  47.7 2.1 %copy-start = (f32[7552,128]{1,0:T(8,128)S(1)}, f32[7552,128]{1,0:T(8,128)}, u32[]{:S(2)}) copy-start(f32[7552,128]{1,0:T(8,128)} %get-tuple-element.5.phi) | copy-start | bytes 11599876
